TPU v7x, 32 devices: a whole 2x2x4 slice. The times are simulated.
32 devices in a mesh: section: 4 (over y, x), dp: 8 (over z, core).
Axes of the slice: x: 2, y: 2, z: 4, core: 2. Of those that a mesh axis runs over, the one named last changes fastest.
Arguments:
- image: bfloat16 [2, 2, 32, 7, 7, 2048], P(None, None, 'dp')
- section_weights: bfloat16 [4, 9456, 512], P('section')
- section_norms: float32 [4, 3, 2048], P('section'), as said below
- queue: bfloat16 [2, 512, 128], P(None, 'dp'), may hold values from -0.5 to 0.5
- pairing: int32 [2, 32], P(None, 'dp'), may hold values from 0 to 3, as said below
Outputs:
- loss: float32 [], replicated
- grad_input: float32 [2, 2, 32, 7, 7, 2048], P(None, None, 'dp', None, None, 'section')
- grad_weights: float32 [4, 9456, 512], P('section', None, 'dp')
- grad_norms: float32 [4, 3, 2048], P('section')
Inputs may be any that keep to these rules, and one draw needn't show every extreme that they name: `pairing`: each run of 4 entries of a row (the images of one index of dp) is a permutation of 0 to 3. `section_norms`: row 0 (gains) is positive.
All inputs are finite; a program needn't handle non-finite values.
Results may differ from a plain program's by a relative error of at most 0.025.
Values may be sent and summed in bfloat16 or wider, within the bound.
No kernel may reach another device: no remote copies, remote signals or barrier semaphores. Data moves between devices by JAX's collectives and lax.ppermute only.
A program may use at most 448 MiB of HBM per device.

v0:
```python
import functools

import jax
import jax.numpy as jnp
from jax import lax
from jax.experimental import pallas as pl
from jax.experimental.pallas import tpu as pltpu
from jax.sharding import PartitionSpec as P

D = 2048
WIDTH = 512
PROJ = 128
PROTOS = 3000
SIDE = 7
CROPS = 2
SECTIONS = 4
PART = WIDTH // SECTIONS
WIDE = D // SECTIONS
QUARTER = PROTOS // 4
QUARTER_PAD = 768
PLACES = SIDE * SIDE
FIRST = D * (D // WIDTH)
SECOND = FIRST + D * PROJ // WIDTH
THIRD = SECOND + PROTOS * PROJ // WIDTH
HALF_REDUCE = 16 + D // 2
HALF_EXPAND = 16 + WIDTH // 2
QUARTER_CONV = 16 + 9 * WIDTH // 4
NOTE_ROWS = 48

NORM_EPS = 1e-05
UNIT_EPS = 1e-06
SINK_EPS = 0.05
TEMPER = 0.1
HIGH = lax.Precision.HIGHEST
F32 = jnp.float32
BF16 = jnp.bfloat16
NT = (((1,), (1,)), ((), ()))
TN = (((0,), (0,)), ((), ()))


def dot(a, b):
    return jnp.dot(a, b, preferred_element_type=F32)


def dot_nt(a, b):
    return lax.dot_general(a, b, NT, preferred_element_type=F32)


def dot_tn(a, b):
    return lax.dot_general(a, b, TN, preferred_element_type=F32)


def flip(value, axis, step):
    count = lax.axis_size(axis)
    return lax.ppermute(value, axis, [(source, source ^ step) for source in range(count)])


def send(value, source, target):
    return lax.ppermute(value, "section", [(source, target)])


def sum_dp_steps(value):
    count = lax.axis_size("dp")
    value = pair = value + flip(value, "dp", 1)
    step = 2
    while step < count:
        if 2 * step < count:
            near = value + flip(value, "dp", step)
            far = flip(value, "dp", 2 * step) + flip(value, "dp", 3 * step)
            value = near + far
            step *= 4
        else:
            value = value + flip(value, "dp", step)
            step *= 2
    return value, pair


def sum_dp(value):
    return sum_dp_steps(value)[0]


def gather_xor(value, axis):
    return [value] + [flip(value, axis, step) for step in range(1, lax.axis_size(axis))]


def dp_stages():
    count = lax.axis_size("dp")
    stages, step = [(1,)], 2
    while step < count:
        if 2 * step < count:
            stages.append((step, 2 * step, 3 * step))
            step *= 4
        else:
            stages.append((step,))
            step *= 2
    return stages


def gather_dp(value, stages):
    arrays, offsets = [value], [[0]]
    for steps in stages:
        if len(arrays) > 1:
            arrays, offsets = [rows_of(arrays)], [sum(offsets, [])]
        first = offsets[0]
        for step in steps:
            arrays.append(flip(arrays[0], "dp", step))
            offsets.append([o ^ step for o in first])
    return arrays, offsets


def sigmoid(v):
    return 1.0 / (1.0 + jnp.exp(-v))


def slope(v):
    s = sigmoid(v)
    return s * (1.0 + v * (1.0 - s))


def cost(us):
    return pl.CostEstimate(flops=0, bytes_accessed=int(us * 3_000_000), transcendentals=0)


def hbm(value):
    return pltpu.with_memory_space_constraint(value, pltpu.HBM)


def call(kernel, out, *args, scratch=(), vmem=12, us=1.0, in_hbm=()):
    in_specs, ins = [], []
    for j, a in enumerate(args):
        space = pltpu.VMEM
        if jnp.issubdtype(a.dtype, jnp.integer):
            space = pltpu.SMEM
        elif j in in_hbm:
            space = pltpu.HBM
            a = hbm(a)
        in_specs.append(pl.BlockSpec(memory_space=space))
        ins.append(a)
    return pl.pallas_call(
        kernel,
        name=getattr(kernel, 'func', kernel).__name__,
        out_shape=out,
        in_specs=in_specs,
        out_specs=jax.tree.map(lambda _: pl.BlockSpec(memory_space=pltpu.VMEM), out),
        scratch_shapes=list(scratch),
        compiler_params=pltpu.CompilerParams(vmem_limit_bytes=vmem * 2**20),
        cost_estimate=cost(us),
    )(*ins)


def shape(dims, dtype):
    return jax.ShapeDtypeStruct(tuple(dims), dtype)


def retile_kernel(image, flat):
    flat[...] = image[...].reshape(flat.shape)


def note_kernel(pairing, queue, out):
    size = queue.shape[1]
    for c in range(CROPS):
        out[c * size : (c + 1) * size, :] = queue[c]
    row = lax.broadcasted_iota(jnp.int32, (16, PROJ), 0)
    lane = lax.broadcasted_iota(jnp.int32, (16, PROJ), 1)
    value = jnp.zeros((16, PROJ), F32)
    for m in range(pairing.shape[0]):
        for i in range(pairing.shape[1]):
            value = jnp.where((row == m) & (lane == i), pairing[m, i].astype(F32), value)
    out[CROPS * size :, :] = value.astype(BF16)


def rows_kernel(*refs):
    out, at = refs[-1], 0
    for ref in refs[:-1]:
        out[at : at + ref.shape[0], :] = ref[...]
        at += ref.shape[0]


def lanes_kernel(*refs):
    out, at = refs[-1], 0
    for ref in refs[:-1]:
        out[:, at : at + ref.shape[1]] = ref[...]
        at += ref.shape[1]


def rows_of(values, us=0.5):
    rows = sum(v.shape[0] for v in values)
    return call(rows_kernel, shape((rows, values[0].shape[1]), values[0].dtype), *values, us=us)


def split_sums(first, second, micro):
    width = first[0].shape[1]
    rows = [jnp.sum(v, axis=0, keepdims=True) for v in first]
    rows += [jnp.sum(v, axis=0, keepdims=True) for v in second]
    rows.append(jnp.zeros((8 - 2 * micro, width), F32))
    return jnp.concatenate(rows, axis=0)


def moments(sums, m, micro, count):
    mean = sums[m : m + 1] * (1.0 / count)
    square = sums[micro + m : micro + m + 1] * (1.0 / count)
    return mean, lax.rsqrt(square - mean * mean + NORM_EPS)


def per_micro(value, micro):
    rows = value.shape[0] // micro
    return [value[m * rows : (m + 1) * rows] for m in range(micro)]


def normalized(value, sums, micro, count):
    out = []
    for m, v in enumerate(per_micro(value, micro)):
        mean, rstd = moments(sums, m, micro, count)
        out.append(((v - mean) * rstd, rstd))
    return out


def join(parts):
    return jnp.concatenate(parts, axis=0)


def tap_valid(rows, images, tap, sign):
    row = lax.broadcasted_iota(jnp.int32, (rows, PART), 0).astype(F32)
    cell = jnp.floor((row + 0.5) * (1.0 / images))
    crop = jnp.floor((cell + 0.5) * (1.0 / PLACES))
    place = cell - crop * PLACES
    y = jnp.floor((place + 0.5) * (1.0 / SIDE))
    x = place - y * SIDE
    y = y + float(sign * (tap // 3 - 1))
    x = x + float(sign * (tap % 3 - 1))
    return (y > -0.5) & (y < SIDE - 0.5) & (x > -0.5) & (x < SIDE - 0.5)


def tap_shift(value, images, tap, sign):
    rows = value.shape[0]
    offset = sign * images * (SIDE * (tap // 3 - 1) + (tap % 3 - 1))
    moved = value if offset == 0 else pltpu.roll(value, (-offset) % rows, 0)
    if tap == 4:
        return moved
    return jnp.where(tap_valid(rows, images, tap, sign), moved, 0.0)


def told_norm(message, at=0):
    rows = message[at : at + 16, :].astype(F32)
    return rows[0:1] + rows[1:2] + rows[2:3], rows[3:4] + rows[4:5] + rows[5:6]


def told_wide(message):
    parts = [told_norm(message, HALF_REDUCE + b * HALF_EXPAND) for b in range(4)]
    return tuple(jnp.concatenate(p, axis=1) for p in zip(*parts))


def terms(row):
    out = []
    for _ in range(3):
        term = row.astype(BF16).astype(F32)
        out.append(term)
        row = row - term
    return out


def tell_norm(rows):
    out = terms(rows[0:1]) + terms(rows[1:2])
    out.append(jnp.zeros((10, rows.shape[1]), F32))
    return jnp.concatenate(out, axis=0).astype(BF16)


def reduce_kernel(micro, place, image, w0, w1, pre, sums):
    half = D // 2
    first = pl.ds(pl.multiple_of(place[4] * half, half), half)
    second = pl.ds(pl.multiple_of(place[5] * half, half), half)
    value = dot(image[:, first], w0[16 : 16 + half, :]) + dot(image[:, second], w1[16 : 16 + half, :])
    pre[...] = value
    parts = per_micro(value, micro)
    sums[...] = split_sums(parts, [v * v for v in parts], micro)


def active_kernel(micro, count, pre, sums, told, active):
    gain, shift = told_norm(told)
    out = []
    for xhat, _ in normalized(pre[...], sums[...], micro, count):
        y = xhat * gain + shift
        out.append(y * sigmoid(y))
    active[...] = join(out).astype(BF16)


def fill(place, pieces, full):
    for k, piece in enumerate(pieces):
        full[:, pl.ds(pl.multiple_of(place[k] * PART, PART), PART)] = piece[: full.shape[0], :]


def quarter_of(place, j):
    return place[8] ^ (0, 2, 1, 3)[j]


def conv_kernel(micro, images, place, a0, a1, a2, a3, wa, wb, pre, sums, full, weight):
    fill(place, (a0, a1, a2, a3), full)
    quarter = WIDTH // 4
    for j in range(4):
        w = (wa, wb)[j // 2]
        at = pl.multiple_of(quarter_of(place, j) * quarter, quarter)
        for tap in range(9):
            lanes = slice(tap * PART, (tap + 1) * PART)
            first = (j % 2) * QUARTER_CONV + 16 + tap * quarter
            weight[pl.ds(at, quarter), lanes] = w[first : first + quarter, :]
    total = None
    for first in range(0, 9, 2):
        taps = [tap for tap in (first, first + 1) if tap < 9]
        part = dot(full[...], weight[:, first * PART : (taps[-1] + 1) * PART])
        for j, tap in enumerate(taps):
            moved = tap_shift(part[:, j * PART : (j + 1) * PART], images, tap, 1)
            total = moved if total is None else total + moved
    pre[...] = total
    parts = per_micro(total, micro)
    sums[...] = split_sums(parts, [v * v for v in parts], micro)


def expand_kernel(micro, place, a0, a1, a2, a3, w0, w1, active, pre, sums, weight):
    fill(place, (a0, a1, a2, a3), active)
    half = WIDTH // 2
    for j, w in enumerate((w0, w1)):
        rows = pl.ds(pl.multiple_of(place[4 + j] * half, half), half)
        for b in range(4):
            at = HALF_REDUCE + b * HALF_EXPAND + 16
            weight[rows, b * PART : (b + 1) * PART] = w[at : at + half, :]
    value = dot(active[...], weight[...])
    pre[...] = value
    parts = per_micro(value, micro)
    sums[...] = split_sums(parts, [v * v for v in parts], micro)


def crop_rows(rows, images, transpose=False):
    shp = (rows // PLACES, rows)
    r = lax.broadcasted_iota(jnp.int32, shp, 1).astype(F32)
    q = lax.broadcasted_iota(jnp.int32, shp, 0).astype(F32)
    cell = jnp.floor((r + 0.5) * (1.0 / images))
    crop = jnp.floor((cell + 0.5) * (1.0 / PLACES))
    image = r - cell * images
    return (jnp.abs(crop * images + image - q) < 0.5).astype(F32).astype(BF16)


def pool_kernel(micro, images, count, place, pre, sums, told, image, pooled):
    lanes = pl.ds(pl.multiple_of(place[0] * WIDE, WIDE), WIDE)
    gain, shift = told_wide(told)
    out = []
    for xhat, _ in normalized(pre[...], sums[...], micro, count):
        out.append(xhat * gain + shift)
    z = join(out) + image[:, lanes].astype(F32)
    out = z * sigmoid(z)
    high = out.astype(BF16)
    low = (out - high.astype(F32)).astype(BF16)
    choose = crop_rows(pre.shape[0], images)
    pooled[...] = ((dot(choose, high) + dot(choose, low)) * (1.0 / PLACES)).astype(BF16)


def out_back_kernel(micro, images, count, place, pre, sums, told, image, own, r0, r1, r2, d_z, sums_out):
    lanes = pl.ds(pl.multiple_of(place[0] * WIDE, WIDE), WIDE)
    rows = pre.shape[0]
    gain, shift = told_wide(told)
    came = (r0[...].astype(F32) + r1[...].astype(F32) + r2[...].astype(F32)).astype(BF16)
    d_pooled = jnp.where(place[0] == SECTIONS - 1, own[...], came)
    spread = dot_tn(crop_rows(rows, images), d_pooled) * (1.0 / PLACES)
    xhats = [x for x, _ in normalized(pre[...], sums[...], micro, count)]
    z = join([x * gain + shift for x in xhats]) + image[:, lanes].astype(F32)
    value = spread * slope(z)
    d_z[...] = value
    parts = per_micro(value, micro)
    sums_out[...] = split_sums([v * x for v, x in zip(parts, xhats)], parts, micro)


def norm_back(value, pre, sums, back, gain, micro, count):
    out = []
    parts = per_micro(value, micro)
    for m, (xhat, rstd) in enumerate(normalized(pre, sums, micro, count)):
        by_x = back[m : m + 1] * (1.0 / count)
        plain = back[micro + m : micro + m + 1] * (1.0 / count)
        out.append(gain * rstd * (parts[m] - plain - xhat * by_x))
    return join(out)


def norm_back_kernel(micro, count, d_y, pre, sums, back, told, d_pre):
    gain, _ = told_norm(told)
    d_pre[...] = norm_back(d_y[...], pre[...], sums[...], back[...], gain, micro, count).astype(BF16)


def over_micro(back, micro):
    out = []
    for r in range(2):
        row = back[r * micro : r * micro + 1, :]
        for m in range(1, micro):
            row = row + back[r * micro + m : r * micro + m + 1, :]
        out.append(row)
    return out


def last_norm_back_kernel(micro, count, place, d_y, pre, sums, back, told, back2, back1, notes, d_pre):
    gain, _ = told_norm(told)
    rows = d_y.shape[0]
    d_pre[:rows, :] = norm_back(d_y[...], pre[...], sums[...], back[...], gain, micro, count).astype(BF16)
    said = []
    for row in over_micro(back2, micro):
        said += [row[:, b * PART : (b + 1) * PART] for b in range(4)]
    said += over_micro(back1, micro) + over_micro(back, micro)
    said.append(jnp.where(place[0] == SECTIONS - 1, notes[3:4, :PART], 0.0))
    said = sum([terms(row) for row in said], [])
    said.append(jnp.zeros((NOTE_ROWS - len(said), PART), F32))
    d_pre[rows:, :] = jnp.concatenate(said, axis=0).astype(BF16)


def expand_back_kernel(micro, count, place, pre, sums, d_z, back, told, weight, d_pre, q0, q1, q2, q3, full):
    gain, _ = told_wide(told)
    d_low = norm_back(d_z[...], pre[...], sums[...], back[...], gain, micro, count).astype(BF16)
    d_pre[...] = d_low
    full[...] = dot_nt(d_low, weight[...])
    for k, q in enumerate((q0, q1, q2, q3)):
        lanes = pl.ds(pl.multiple_of(place[k] * PART, PART), PART)
        q[...] = full[:, lanes].astype(BF16)


def finish_silu(micro, count, d_active, pre, sums, norm, d_y, sums_out):
    gain, shift = norm
    values, products = [], []
    parts = per_micro(d_active, micro)
    for m, (xhat, _) in enumerate(normalized(pre[...], sums[...], micro, count)):
        value = parts[m] * slope(xhat * gain + shift)
        values.append(value)
        products.append(value * xhat)
    d_y[...] = join(values)
    sums_out[...] = split_sums(products, values, micro)


def silu_back_kernel(micro, count, q0, q1, q2, q3, pre, sums, told, d_y, sums_out):
    total = (q0[...].astype(F32) + q1[...].astype(F32)) + (q2[...].astype(F32) + q3[...].astype(F32))
    d_active = total.astype(BF16).astype(F32)
    finish_silu(micro, count, d_active, pre, sums, told_norm(told), d_y, sums_out)


def conv_back_kernel(
    micro, images, count, place, d0, d1, d2, d3, back0, back1, pre, sums, told, d_full, d_y, sums_out, weight
):
    fill(place, (d0, d1, d2, d3), d_full)
    d_low = d_full[...]
    half = PART // 2
    for j, back in enumerate((back0, back1)):
        for k in range(SECTIONS):
            lanes = pl.ds(pl.multiple_of(place[k] * PART, PART), PART)
            for tap in range(9):
                rows = pl.ds(pl.multiple_of(tap * PART + place[4 + j] * half, half), half)
                weight[rows, lanes] = back[k, tap * half : (tap + 1) * half, :]
    total = None
    for first in range(0, 9, 2):
        taps = [tap for tap in (first, first + 1) if tap < 9]
        part = dot_nt(d_low, weight[first * PART : (taps[-1] + 1) * PART, :])
        for j, tap in enumerate(taps):
            moved = tap_shift(part[:, j * PART : (j + 1) * PART], images, tap, -1)
            total = moved if total is None else total + moved
    d_active = total.astype(BF16).astype(F32)
    finish_silu(micro, count, d_active, pre, sums, told_norm(told), d_y, sums_out)


def reduce_back_kernel(place, d_full, back0, back1, d_z, grad_in, weight):
    half = WIDE // 2
    first = 9 * PART // 2
    for j, back in enumerate((back0, back1)):
        rows = pl.ds(pl.multiple_of(place[4 + j] * half, half), half)
        for k in range(SECTIONS):
            lanes = pl.ds(pl.multiple_of(place[k] * PART, PART), PART)
            weight[rows, lanes] = back[k, first : first + half, :]
    main = dot_nt(d_full[...], weight[...]).astype(BF16).astype(F32)
    value = main + d_z[...].astype(BF16).astype(F32)
    grad_in[...] = value.reshape(grad_in.shape)


def back_parts_kernel(place, conv_a, conv_b, reduce0, reduce1, *outs):
    half = PART // 2
    wide = WIDE // 2
    first = 9 * half
    quarter = WIDTH // 4
    for k, out in enumerate(outs):
        for core in range(2):
            for j in range(4):
                conv = (conv_a, conv_b)[j // 2]

                @pl.when((place[k] == quarter_of(place, j)) & (place[4] == core))
                def _():
                    for tap in range(9):
                        at = (j % 2) * QUARTER_CONV + 16 + tap * quarter + core * half
                        out[tap * half : (tap + 1) * half, :] = conv[at : at + half, :]

            for u in range(SECTIONS):
                reduce = (reduce0, reduce1)[core ^ (u // 2)]

                @pl.when((place[k] == u) & (place[4] == core))
                def _():
                    at = 16 + (u % 2) * WIDE + core * wide
                    out[first : first + wide, :] = reduce[at : at + wide, :]


def stack_kernel(*refs):
    out = refs[-1]
    rows = refs[0].shape[0]
    for j, ref in enumerate(refs[:-1]):
        if len(out.shape) == 3:
            out[j] = ref[...]
        else:
            out[j * rows : (j + 1) * rows, :] = ref[...]


def mixed_kernel(place, reduce, conv, expand, *outs):
    for k, out in enumerate(outs):
        target = place[k + 1]

        @pl.when(target == 0)
        def _():
            out[:, :WIDE] = reduce[...]

        @pl.when(target == 1)
        def _():
            out[...] = conv[...]

        @pl.when(target == 2)
        def _():
            out[:, :WIDE] = expand[...]


def told_kernel(place, n0, n1, n2, n3, notes, out, loss):
    t = place[0]
    out[...] = jnp.zeros_like(out)

    @pl.when(t == SECTIONS - 1)
    def _():
        out[...] = notes[:3, :]

    total = None
    for k, note in enumerate((n0, n1, n2, n3)):
        u = place[k]
        rows = note[note.shape[0] - NOTE_ROWS :, :].astype(F32)

        def said(i):
            return (rows[3 * i : 3 * i + 1] + rows[3 * i + 1 : 3 * i + 2]) + rows[3 * i + 2 : 3 * i + 3]

        total = said(12) if total is None else total + said(12)

        @pl.when(t == 2)
        def _():
            for r in range(2):
                for b in range(4):
                    lanes = pl.ds(pl.multiple_of(u * WIDE + b * PART, PART), PART)
                    out[r : r + 1, lanes] = said(4 * r + b)

        for section in range(2):

            @pl.when(t == section)
            def _():
                for r in range(2):
                    lanes = pl.ds(pl.multiple_of(u * PART, PART), PART)
                    out[r : r + 1, lanes] = said((10, 8)[section] + r)

    loss[...] = jnp.broadcast_to(total, loss.shape)


def pick_kernel(place, p0, p1, p2, p3, conv, pair):
    for j, p in enumerate((p0, p1, p2, p3)):

        @pl.when(place[0] == j)
        def _():
            pair[:HALF_REDUCE, :] = p[:HALF_REDUCE, :]

        @pl.when(place[1] == j)
        def _():
            conv[...] = p[...]

        @pl.when(place[2] == j)
        def _():
            pair[HALF_REDUCE:, :] = p[: 4 * HALF_EXPAND, :]


def taps_kernel(images, active, out):
    value = active[...].astype(F32)
    for tap in range(9):
        out[:, tap * PART : (tap + 1) * PART] = tap_shift(value, images, tap, 1).astype(BF16)


def head(pooled, w_head, w_proj, protos, norm, queue, match, micro, images, dp):
    rows = pooled.shape[0]
    group = rows // micro
    half = group // CROPS
    scale_all = 1.0 / (TEMPER * CROPS * half * micro)
    pre = dot(pooled, w_head)

    def by_micro(v):
        return v.reshape(micro, group, v.shape[-1])

    pre_m = by_micro(pre)
    mean = jnp.mean(pre_m, axis=1, keepdims=True)
    square = jnp.mean(pre_m * pre_m, axis=1, keepdims=True)
    rstd = lax.rsqrt(square - mean * mean + NORM_EPS)
    xhat = (pre_m - mean) * rstd
    y = xhat * norm[0] + norm[1]
    active = (y * sigmoid(y)).astype(BF16).reshape(rows, D)
    embed = dot(active, w_proj) + norm[2, :PROJ]
    recip = lax.rsqrt(jnp.sum(embed * embed, axis=1, keepdims=True) + UNIT_EPS)
    unit = (embed * recip).astype(BF16)
    scores = dot_nt(unit, protos)
    valid = lax.broadcasted_iota(jnp.int32, (1, 4, QUARTER_PAD), 2).reshape(1, 4 * QUARTER_PAD) < QUARTER
    own_mass = jnp.where(valid, jnp.exp(scores / SINK_EPS), 0.0).reshape(micro, CROPS, half, -1)
    queue_mass = jnp.where(valid, jnp.exp(jnp.einsum("cqp,kp->cqk", queue, protos, preferred_element_type=F32) / SINK_EPS), 0.0)
    codes = []
    for m in range(micro):
        for c in range(CROPS):
            a, b = queue_mass[c], own_mass[m, c]
            column = jnp.sum(a, axis=0, keepdims=True) + jnp.sum(b, axis=0, keepdims=True)
            once = jnp.where(valid, 1.0 / column, 0.0)
            a, b = a * once, b * once
            scale = valid.astype(F32)
            for turn in range(2):
                ra = 1.0 / jnp.sum(a * scale, axis=1, keepdims=True)
                rb = 1.0 / jnp.sum(b * scale, axis=1, keepdims=True)
                column = jnp.sum(a * ra, axis=0, keepdims=True) + jnp.sum(b * rb, axis=0, keepdims=True)
                scale = jnp.where(valid, 1.0 / column, 0.0)
            b = b * scale
            codes.append(b / jnp.sum(b, axis=1, keepdims=True))
    targets = []
    for m in range(micro):
        targets.append(jnp.dot(match[m], codes[m * CROPS + 1], precision=HIGH))
        targets.append(jnp.dot(match[m].T, codes[m * CROPS], precision=HIGH))
    target = jnp.concatenate(targets)
    logits = jnp.where(valid, scores / TEMPER, -1e30)
    logp = jax.nn.log_softmax(logits, axis=1)
    loss = -jnp.sum(jnp.where(valid, target * logp, 0.0)) * (TEMPER * scale_all)
    d_scores = ((jnp.exp(logp) * jnp.sum(target, axis=1, keepdims=True) - target) * scale_all).astype(BF16)
    d_unit = dot(d_scores, protos)
    d_embed = (
        recip * d_unit - embed * (recip * recip * recip) * jnp.sum(d_unit * embed, axis=1, keepdims=True)
    ).astype(BF16)
    d_active = dot_nt(d_embed, w_proj)
    d_y = by_micro(d_active) * slope(y)
    by_x = jnp.sum(d_y * xhat, axis=1, keepdims=True)
    plain = jnp.sum(d_y, axis=1, keepdims=True)
    d_pre = (norm[0] * rstd * (d_y - plain / group - xhat * by_x / group)).astype(BF16).reshape(rows, D)
    bias = jnp.pad(jnp.sum(d_embed.astype(F32), axis=0), (0, D - PROJ))
    grads = jnp.stack([jnp.sum(by_x, axis=(0, 1)), jnp.sum(plain, axis=(0, 1)), bias])
    return loss, grads, active, unit, d_scores, d_embed, d_pre


def valid_lanes():
    lane = lax.broadcasted_iota(jnp.int32, (1, 4 * QUARTER_PAD), 1).astype(F32)
    block = jnp.floor((lane + 0.5) * (1.0 / QUARTER_PAD))
    return lane - block * QUARTER_PAD < QUARTER - 0.5


def lanes_at(b, size):
    return pl.ds(pl.multiple_of(b * size, size), size)


def lanes_at(b, size):
    return pl.ds(pl.multiple_of(b * size, size), size)


def mass_kernel(micro, images, told_offsets, place, table, *refs):
    mass, column, match, rows_s, exps = refs[-5:]
    ndp = len(told_offsets)
    valid = valid_lanes()
    size = mass.shape[0] // ndp
    half = images * ndp
    at, said = 0, jnp.zeros((16, half), F32)
    row = lax.broadcasted_iota(jnp.int32, (PROJ, half), 0)
    lane = lax.broadcasted_iota(jnp.int32, (PROJ, half), 1)
    for ref in refs[:-5]:
        rows = CROPS * size + 16
        for j in range(ref.shape[0] // rows):
            mine = pl.ds(pl.multiple_of(j * rows + place[4] * size, 16), size)
            rows_s[lanes_at(place[7] ^ told_offsets[at], size), :] = ref[mine, :]
            pairs = ref[(j + 1) * rows - 16 : (j + 1) * rows, :]
            spot_at = (place[7] ^ told_offsets[at]) * images
            spot = ((row < images) & (lane == row + spot_at)).astype(F32).astype(BF16)
            said = said + dot(pairs, spot)
            at += 1
    step = 128
    steps = mass.shape[0] // step

    def scored(i, sums):
        own = rows_s[lanes_at(i, step), :]
        out = []
        for a in range(4):
            lanes = slice(a * QUARTER_PAD, (a + 1) * QUARTER_PAD)
            value = jnp.exp(dot_nt(own, table[:, a * PROJ : (a + 1) * PROJ]) * (1.0 / SINK_EPS))
            value = jnp.where(valid[:, lanes], value, 0.0)
            exps[lanes_at(i, step), lanes] = value
            out.append(jnp.sum(value, axis=0, keepdims=True))
        return sums + jnp.concatenate(out, axis=1)

    sums = lax.fori_loop(0, steps, scored, jnp.zeros((1, 4 * QUARTER_PAD), F32))
    column[...] = jnp.broadcast_to(sums, column.shape)
    factor = jnp.where(valid, 1.0 / sums, 0.0)

    def divide(i, carry):
        mass[lanes_at(i, step), :] = (exps[lanes_at(i, step), :] * factor).astype(BF16)
        return carry

    lax.fori_loop(0, steps, divide, 0)

    def over(value, by):
        return jnp.floor((value + 0.5) * (1.0 / by))

    row = lax.broadcasted_iota(jnp.int32, (half, half), 0).astype(F32)
    lane = lax.broadcasted_iota(jnp.int32, (half, half), 1).astype(F32)
    block = over(row, images)
    for m in range(micro):
        same = (jnp.abs(block - over(lane, images)) < 0.5) & (jnp.abs(row - block * images - said[m : m + 1, :]) < 0.5)
        there = same.astype(F32)
        match[m] = jnp.where(place[4] == 0, there, there.T).astype(BF16)


def tables_kernel(packed, proj, table, rows, buffer, sem):
    size = THIRD - FIRST + 2
    copy = pltpu.make_async_copy(packed.at[pl.ds(FIRST, size), :], rows, sem)
    copy.start()
    copy.wait()
    wide = SECOND - FIRST
    for a in range(4):
        buffer[pl.ds(a, wide, stride=4), :] = rows[:wide, a * PROJ : (a + 1) * PROJ].astype(F32)
    proj[...] = buffer[...].astype(BF16)
    row = lax.broadcasted_iota(jnp.int32, (size - wide, WIDTH), 0)
    kept = jnp.where(row < QUARTER, rows[wide:, :].astype(F32), 0.0).astype(BF16)
    table[: size - wide, :] = kept
    table[size - wide :, :] = jnp.zeros((QUARTER_PAD - (size - wide), WIDTH), BF16)


def exact_dot(choose, value):
    parts, left = [], value
    for _ in range(3):
        term = left.astype(BF16)
        left = left - term.astype(F32)
        parts.append(term)
    return dot(jnp.concatenate([choose] * 3, axis=1), jnp.concatenate(parts, axis=0))


def by_micro_rows(value, ndp, micro):
    return value.reshape(ndp, micro, value.shape[0] // (ndp * micro), value.shape[1])


def total_of(value):
    return jnp.sum(jnp.sum(value, axis=0), axis=0, keepdims=True)


def regroup(rows, own, images, to_groups):
    ndp = rows // own
    row = lax.broadcasted_iota(jnp.int32, (rows, rows), 0).astype(F32)
    lane = lax.broadcasted_iota(jnp.int32, (rows, rows), 1).astype(F32)
    source, target = (lane, row) if to_groups else (row, lane)
    block = jnp.floor((source + 0.5) * (1.0 / own))
    inner = source - block * own
    part = jnp.floor((inner + 0.5) * (1.0 / images))
    moved = (part * ndp + block) * images + inner - part * images
    return (jnp.abs(moved - target) < 0.5).astype(F32).astype(BF16)


def head_kernel(
    micro, images, offsets, place, pooled_a, pooled_b, w_head, w_proj, table, norm, mass, column, match,
    pooled, active, unit, d_scores, embed, xhat_s, y_s, rstd_s, said,
    scores, own_mass, total, factor,
):
    ndp = len(offsets)
    rows = pooled.shape[0]
    group = rows // micro
    half = group // CROPS
    own = rows // ndp
    queued = mass.shape[0]
    scale_all = 1.0 / (TEMPER * CROPS * half * micro)
    chunk = WIDTH
    chunks = D // chunk
    core = place[4]
    for j, offset in enumerate(offsets):
        source = (pooled_a, pooled_b)[j * own // pooled_a.shape[0]]
        at = j * own % pooled_a.shape[0]
        pooled[lanes_at(place[7] ^ offset, own), :] = source[at : at + own, :]
    low = pooled[...]

    def forward(b, carry):
        lanes = lanes_at(b, chunk)
        pre = by_micro_rows(dot(low, w_head[:, lanes]), ndp, micro)
        gain, shift = norm[0:1, lanes], norm[1:2, lanes]
        xhats, ys = [], []
        for m in range(micro):
            v = pre[:, m]
            mean = total_of(v) * (1.0 / group)
            square = total_of(v * v) * (1.0 / group)
            rstd = lax.rsqrt(square - mean * mean + NORM_EPS)
            xhat = (v - mean) * rstd
            rstd_s[m : m + 1, lanes] = rstd
            xhats.append(xhat)
            ys.append(xhat * gain + shift)
        xhat_s[:, lanes] = jnp.stack(xhats, axis=1).reshape(rows, chunk)
        y = jnp.stack(ys, axis=1).reshape(rows, chunk)
        y_s[:, lanes] = y
        active[:, lanes] = (y * sigmoid(y)).astype(BF16)
        return carry

    lax.fori_loop(0, chunks, forward, 0)
    value = dot(active[...], w_proj[...]) + norm[2:3, :PROJ]
    embed[...] = value
    recip = lax.rsqrt(jnp.sum(value * value, axis=1, keepdims=True) + UNIT_EPS)
    unit_v = dot(regroup(rows, own, images, True), (value * recip).astype(BF16)).astype(BF16)
    unit[...] = unit_v
    valid = valid_lanes()
    for a in range(4):
        lanes = slice(a * QUARTER_PAD, (a + 1) * QUARTER_PAD)
        scores[:, lanes] = dot_nt(unit_v, table[:, a * PROJ : (a + 1) * PROJ])

    step = 128

    def divided(a):
        return a * (1.0 / jnp.sum(a, axis=1, keepdims=True))

    def folded(a):
        return jnp.sum(a.reshape(a.shape[0] // 8, 8, a.shape[1]), axis=0)

    def own_rows(m):
        return slice(m * half, (m + 1) * half)

    queue_sum = column[0:1, :]
    for m in range(micro):
        a = scores[lanes_at(m * CROPS + core, half), :]
        a = jnp.where(valid, jnp.exp(a * (1.0 / SINK_EPS)), 0.0)
        inverse = jnp.where(valid, 1.0 / (queue_sum + jnp.sum(a, axis=0, keepdims=True)), 0.0)
        factor[m : m + 1, :] = queue_sum * inverse
        factor[micro + m : micro + m + 1, :] = jnp.ones_like(inverse)
        own_mass[own_rows(m), :] = a * inverse

    def turn(i, carry):
        def block(i, carry):
            at = lanes_at(i, step)
            e_of = [mass[at, b * PART : (b + 1) * PART].astype(F32) for b in range(4 * QUARTER_PAD // PART)]
            rows_by = []
            for m in range(micro):
                sums = None
                for b, e in enumerate(e_of):
                    more = e * factor[m : m + 1, b * PART : (b + 1) * PART]
                    sums = more if sums is None else sums + more
                rows_by.append(1.0 / jnp.sum(sums, axis=1, keepdims=True))
            for b in range(4 * QUARTER_PAD // PART):
                lanes = slice(b * PART, (b + 1) * PART)
                e = mass[at, lanes].astype(F32)
                for m in range(micro):
                    total[m, :, lanes] += folded(e * rows_by[m])
            return carry

        total[...] = jnp.zeros_like(total)
        lax.fori_loop(0, queued // step, block, 0)
        for m in range(micro):
            scale = factor[micro + m : micro + m + 1, :]
            a = divided(own_mass[own_rows(m), :] * scale)
            sums = jnp.sum(total[m], axis=0, keepdims=True) * factor[m : m + 1, :]
            more = jnp.where(valid, 1.0 / (sums + jnp.sum(a, axis=0, keepdims=True)), 0.0)
            factor[m : m + 1, :] = factor[m : m + 1, :] * more
            factor[micro + m : micro + m + 1, :] = scale * more
        return carry

    lax.fori_loop(0, 2, turn, 0)

    def losses(m, loss):
        mine, there = lanes_at(m, half), lanes_at(m * CROPS + 1 - core, half)
        codes = divided(own_mass[mine, :] * factor[pl.ds(micro + m, 1), :])
        goal = exact_dot(match[m], codes)
        logits = jnp.where(valid, scores[there, :] * (1.0 / TEMPER), -1e30)
        logits = logits - jnp.max(logits, axis=1, keepdims=True)
        power = jnp.exp(logits)
        summed = jnp.sum(power, axis=1, keepdims=True)
        weight = jnp.sum(goal, axis=1, keepdims=True) / summed
        d_low = ((power * weight - goal) * scale_all).astype(BF16)
        d_scores[mine, :] = d_low
        d_unit = None
        for a in range(4):
            more = dot(d_low[:, a * QUARTER_PAD : (a + 1) * QUARTER_PAD], table[:, a * PROJ : (a + 1) * PROJ])
            d_unit = more if d_unit is None else d_unit + more
        said[mine, :] = d_unit
        return loss + jnp.sum(goal * (logits - jnp.log(summed)), axis=1, keepdims=True)

    loss = lax.fori_loop(0, micro, losses, jnp.zeros((half, 1), F32))
    loss = jnp.sum(loss, axis=0, keepdims=True) * (-TEMPER * scale_all)
    said[micro * half :, :] = jnp.broadcast_to(loss, (8, PROJ))


def head_back_kernel(
    micro, images, ndp, place, here, there, embed, w_proj, w_head, norm, xhat_s, y_s, rstd_s,
    d0, d1, d2, d3, notes, d_embed, d_pre, d_unit, d_own,
):
    rows = embed.shape[0]
    group = rows // micro
    half = group // CROPS
    own = rows // ndp
    chunk = WIDTH
    chunks = D // chunk
    for m in range(micro):
        d_unit[lanes_at(m * CROPS + place[5], half), :] = here[m * half : (m + 1) * half, :]
        d_unit[lanes_at(m * CROPS + place[4], half), :] = there[m * half : (m + 1) * half, :]
    value = embed[...]
    recip = lax.rsqrt(jnp.sum(value * value, axis=1, keepdims=True) + UNIT_EPS)
    d_back = exact_dot(regroup(rows, own, images, False), d_unit[...])
    along = jnp.sum(d_back * value, axis=1, keepdims=True)
    d_low = (recip * d_back - value * (recip * recip * recip) * along).astype(BF16)
    d_embed[...] = d_low
    notes[...] = jnp.zeros_like(notes)
    notes[2:3, :PROJ] = jnp.sum(d_low.astype(F32), axis=0, keepdims=True)
    loss = here[micro * half : micro * half + 1, :] + there[micro * half : micro * half + 1, :]
    notes[3:4, :PROJ] = loss

    def backward(b, carry):
        lanes = lanes_at(b, chunk)
        d_y = by_micro_rows(dot_nt(d_low, w_proj[lanes, :]) * slope(y_s[:, lanes]), ndp, micro)
        xhat = by_micro_rows(xhat_s[:, lanes], ndp, micro)
        gain = norm[0:1, lanes]
        values, by_xs, plains = [], None, None
        for m in range(micro):
            by_x = total_of(d_y[:, m] * xhat[:, m])
            plain = total_of(d_y[:, m])
            by_xs = by_x if by_xs is None else by_xs + by_x
            plains = plain if plains is None else plains + plain
            value = d_y[:, m] - plain * (1.0 / group) - xhat[:, m] * (by_x * (1.0 / group))
            values.append(gain * rstd_s[m : m + 1, lanes] * value)
        notes[0:1, lanes] = by_xs
        notes[1:2, lanes] = plains
        d_pre[:, lanes] = jnp.stack(values, axis=1).reshape(rows, chunk).astype(BF16)
        return carry

    lax.fori_loop(0, chunks, backward, 0)
    mine = d_pre[lanes_at(place[7], own), :]

    def to_pooled(b, carry):
        d_own[:, lanes_at(b, chunk)] = dot_nt(mine, w_head[lanes_at(b, chunk), :]).astype(BF16)
        return carry

    lax.fori_loop(0, chunks, to_pooled, 0)
    for j, out in enumerate((d0, d1, d2, d3)):
        out[...] = d_own[:, j * WIDE : (j + 1) * WIDE]


def interleave(width):
    row = lax.broadcasted_iota(jnp.int32, (4 * width, 4 * width), 0)
    column = lax.broadcasted_iota(jnp.int32, (4 * width, 4 * width), 1)
    return (column == 4 * (row & (width - 1)) + (row >> (width.bit_length() - 1))).astype(F32).astype(BF16)


def own_columns(place, own):
    row = lax.broadcasted_iota(jnp.int32, (WIDTH, own), 0)
    lane = lax.broadcasted_iota(jnp.int32, (WIDTH, own), 1)
    return (row == lane + place[7] * own).astype(F32).astype(BF16)


def head_grads_kernel(place, pooled, active, unit, d_here, d_there, d_embed, d_pre, out, parts, apart):
    @pl.when(place[0] != SECTIONS - 1)
    def _():
        out[...] = jnp.zeros_like(out)

    @pl.when(place[0] == SECTIONS - 1)
    def _():
        own = out.shape[0]
        choose = own_columns(place, own)
        weave = interleave(PART)
        block = PART

        def product(q, carry):
            own_d = dot(d_pre[:, lanes_at(q, WIDTH)], choose).astype(BF16)
            parts[q] = dot_tn(own_d, pooled[...]).astype(BF16)
            return carry

        lax.fori_loop(0, 4, product, 0)

        def mix(b, carry):
            mixed = jnp.concatenate([parts[q, :, lanes_at(b, block)] for q in range(4)], axis=1)
            out[:, lanes_at(b, 4 * block)] = dot(mixed, weave)
            return carry

        lax.fori_loop(0, D // block, mix, 0)

        def part(b, carry):
            apart[b] = dot_nt(active[:, lanes_at(b, WIDTH)], weave).astype(BF16)
            return carry

        lax.fori_loop(0, 4, part, 0)
        half = d_here.shape[0] // 2
        units = []
        for core in (place[5], place[4]):
            units.append(jnp.concatenate([unit[lanes_at(m * CROPS + core, half), :] for m in range(2)], axis=0))
        proj = jnp.zeros((own, WIDTH), F32)
        proto = jnp.zeros((own, QUARTER_PAD), F32)
        for a in range(4):
            some = choose[a * PROJ : (a + 1) * PROJ, :]
            own_e = dot(d_embed[...], some).astype(BF16)
            column = jnp.concatenate([apart[b, :, a * block : (a + 1) * block] for b in range(4)], axis=1)
            proj = proj + dot_tn(own_e, column)
            for own_unit, d_scores in zip(units, (d_here, d_there)):
                own_u = dot(own_unit, some).astype(BF16)
                proto = proto + dot_tn(own_u, d_scores[:, a * QUARTER_PAD : (a + 1) * QUARTER_PAD])
        out[:, FIRST:SECOND] = proj
        out[:, SECOND:] = proto[:, : out.shape[1] - SECOND]


def finish_kernel(place, base, reduce, conv, expand, m1, m2, m3, out, buffer, sem):
    mixed = (None, m1, m2, m3)
    t = place[0]

    def write(lanes):
        copy = pltpu.make_async_copy(buffer.at[:, pl.ds(0, lanes)], out.at[:, pl.ds(0, lanes)], sem)
        copy.start()
        copy.wait()

    @pl.when(t == 0)
    def _():
        for u in range(SECTIONS):
            piece = reduce if u == 0 else mixed[u]
            buffer[:, u * WIDE : (u + 1) * WIDE] = piece[:, :WIDE].astype(F32)
        write(D)

    @pl.when(t == 1)
    def _():
        for u in range(SECTIONS):
            piece = conv if u == 1 else mixed[u ^ 1]
            for tap in range(9):
                at = tap * WIDTH + u * PART
                buffer[:, at : at + PART] = piece[:, tap * PART : (tap + 1) * PART].astype(F32)
        write(9 * WIDTH)

    @pl.when(t == 2)
    def _():
        four = [expand if u == 2 else mixed[u ^ 2] for u in range(SECTIONS)]
        weave = interleave(PART)
        for b in range(WIDTH // PART):
            lanes = slice(b * PART, (b + 1) * PART)
            row = jnp.concatenate([f[:, lanes] for f in four], axis=1)
            buffer[:, 4 * b * PART : 4 * (b + 1) * PART] = dot(row, weave)
        write(D)


def unpack_kernel(packed, out, buffer):
    rows = packed.shape[0]
    for b in range(4):
        buffer[b] = packed[:, b * PART : (b + 1) * PART].astype(F32)
    for q in range(4):
        for b in range(4):
            at = q * WIDTH + b * PART
            out[:, at : at + PART] = buffer[b, pl.ds(q, rows // 4, stride=4), :].astype(BF16)


def unpack(packed, rows):
    step = 1024
    return pl.pallas_call(
        unpack_kernel,
        name="unpack",
        out_shape=shape((rows // 4, 4 * WIDTH), BF16),
        grid=(rows // step,),
        in_specs=[pl.BlockSpec((step, WIDTH), lambda i: (i, 0))],
        out_specs=pl.BlockSpec((step // 4, 4 * WIDTH), lambda i: (i, 0)),
        scratch_shapes=[pltpu.VMEM((4, step, PART), F32)],
        compiler_params=pltpu.CompilerParams(vmem_limit_bytes=16 * 2**20),
        cost_estimate=cost(4),
    )(packed)


def pack_kernel(place, packed, norm, o0, o1, o2, o3, rows, buffer, sem):
    outs = (o0, o1, o2, o3)
    t, core = place[0], place[4]

    def run(copies):
        for copy in copies:
            copy.start()
        return copies

    def lanes_of(target, lanes):
        return pl.ds(target * lanes, lanes)

    @pl.when(t == 0)
    def _():
        half = D // 2
        copies = []
        for k, out in enumerate(outs):
            source = packed.at[pl.ds(pl.multiple_of(core * half, half), half), lanes_of(k, PART)]
            copies.append(pltpu.make_async_copy(source, out.at[pl.ds(16, half), :], sem.at[k]))
        run(copies)
        for k, out in enumerate(outs):
            out[:16, :] = tell_norm(norm[:, k * PART : (k + 1) * PART])
        for copy in copies:
            copy.wait()

    @pl.when(t == 1)
    def _():
        quarter = WIDTH // 4
        copies = []
        for k, out in enumerate(outs):
            for tap in range(9):
                at = pl.multiple_of(tap * WIDTH + place[8] * quarter, quarter)
                source = packed.at[pl.ds(at, quarter), lanes_of(1 ^ k, PART)]
                target = out.at[pl.ds(16 + tap * quarter, quarter), :]
                copies.append(pltpu.make_async_copy(source, target, sem.at[9 * k + tap]))
        run(copies)
        for k, out in enumerate(outs):
            out[:16, :] = tell_norm(norm[:, (1 ^ k) * PART : ((1 ^ k) + 1) * PART])
        for copy in copies:
            copy.wait()

    @pl.when(t == 2)
    def _():
        size = rows.shape[0]
        copy = pltpu.make_async_copy(packed.at[pl.ds(pl.multiple_of(core * size, size), size), :], rows, sem.at[0])
        copy.start()
        copy.wait()
        for b in range(4):
            buffer[b] = rows[:, b * PART : (b + 1) * PART].astype(F32)
        for k, out in enumerate(outs):
            u = 2 ^ k
            for b in range(4):
                at = b * HALF_EXPAND
                lane = u * WIDE + b * PART
                out[at : at + 16, :] = tell_norm(norm[:, lane : lane + PART])
                out[at + 16 : at + HALF_EXPAND, :] = buffer[b, pl.ds(u, size // 4, stride=4), :].astype(BF16)


def pack(place, packed, norm):
    rows = 4 * (WIDTH // 2)
    return pl.pallas_call(
        pack_kernel,
        name="pack",
        out_shape=[shape((QUARTER_CONV, PART), BF16)] * 4,
        in_specs=[
            pl.BlockSpec(memory_space=pltpu.SMEM),
            pl.BlockSpec(memory_space=pltpu.HBM),
            pl.BlockSpec(memory_space=pltpu.VMEM),
        ],
        out_specs=[pl.BlockSpec(memory_space=pltpu.VMEM)] * 4,
        scratch_shapes=[
            pltpu.VMEM((rows, WIDTH), BF16), pltpu.VMEM((4, rows, PART), F32), pltpu.SemaphoreType.DMA((36,)),
        ],
        compiler_params=pltpu.CompilerParams(vmem_limit_bytes=12 * 2**20),
        cost_estimate=cost(2),
    )(place, hbm(packed), norm)


def multiple(value, step):
    return value if isinstance(value, int) else pl.multiple_of(value, step)


def pair_kernel(place, a, b, keep, out, full):
    full[...] = dot_tn(a[...], b[...])
    own = keep.shape[1]
    for z in range(keep.shape[0]):
        mine = (2 * z + place[4]) * own
        other = (2 * z + place[5]) * own
        keep[z] = full[pl.ds(pl.multiple_of(mine, own), own), :]
        out[z] = full[pl.ds(pl.multiple_of(other, own), own), :].astype(BF16)


def image_pair_kernel(place, d0, d1, d2, d3, image, keep, out, d_full, full):
    fill(place, (d0, d1, d2, d3), d_full)
    lanes = pl.ds(pl.multiple_of(place[0] * WIDE, WIDE), WIDE)
    pair_kernel(place, d_full, image.at[:, lanes], keep, out, full)


def cross_kernel(place, keep, came, own, o1, o2, o3):
    for k, o in enumerate((own, o1, o2, o3)):
        z = place[6] ^ k
        o[...] = (keep[z] + came[z].astype(F32)).astype(o.dtype)


def add_kernel(own, r1, r2, r3, out):
    out[...] = ((own[...] + r1[...].astype(F32)) + (r2[...].astype(F32) + r3[...].astype(F32))).astype(BF16)


def after(value, *others):
    return lax.optimization_barrier((value, *others))[0]


def body(image, section_weights, section_norms, queue, pairing):
    micro, images = image.shape[0], image.shape[2]
    ndp = lax.axis_size("dp")
    t = lax.axis_index("section")
    dp = lax.axis_index("dp")
    core = dp % 2
    place = jnp.stack([t ^ k for k in range(SECTIONS)] + [core, 1 - core, dp // 2, dp, dp % 4]).astype(jnp.int32)
    cells = CROPS * PLACES * images
    rows = micro * cells
    count = float(cells * ndp)
    packed = section_weights[0]
    norm3 = section_norms[0]
    param_rows = packed.shape[0]
    own = WIDTH // ndp
    k = functools.partial

    def pieces_of(width, dtype):
        return shape((rows, width), dtype)

    own_message, *messages = pack(place, packed, norm3)
    came = [own_message]
    for j in range(1, SECTIONS):
        came.append(lax.ppermute(messages[j - 1], "section", [(u, u ^ j) for u in range(3)]))
    flat = call(
        retile_kernel, shape((rows, D), BF16),
        image.transpose(0, 1, 3, 4, 2, 5).reshape(rows // images, images, D),
        us=2,
    )
    queue_size = CROPS * queue.shape[1]
    note = call(note_kernel, shape((queue_size + 16, PROJ), BF16), pairing, queue, us=0.5)
    told, told_offsets = gather_dp(note, dp_stages())
    *came, flat, told[0] = lax.optimization_barrier((*came, flat, *told))[:6]
    conv_part, pair_part = call(
        pick_kernel,
        (shape((QUARTER_CONV, PART), BF16), shape((HALF_REDUCE + 4 * HALF_EXPAND, PART), BF16)),
        place, *came,
    )
    pair_parts = (pair_part, flip(pair_part, "dp", 1))
    conv_near = flip(conv_part, "dp", 2)
    sums_of = shape((8, PART), F32)
    pre0, part = call(
        k(reduce_kernel, micro), (pieces_of(PART, F32), sums_of), place, flat, *pair_parts, us=2
    )
    sums0 = sum_dp(part)
    active0 = call(k(active_kernel, micro, count), pieces_of(PART, BF16), pre0, sums0, pair_part, us=1)
    actives0 = gather_xor(active0, "section")

    conv_part = rows_of([conv_part, after(conv_near, active0)])
    w_conv = (conv_part, flip(conv_part, "dp", 1))
    w_proj, table = pl.pallas_call(
        tables_kernel,
        name="tables",
        out_shape=(shape((D, PROJ), BF16), shape((QUARTER_PAD, WIDTH), BF16)),
        in_specs=[pl.BlockSpec(memory_space=pltpu.HBM)],
        out_specs=(pl.BlockSpec(memory_space=pltpu.VMEM), pl.BlockSpec(memory_space=pltpu.VMEM)),
        scratch_shapes=[
            pltpu.VMEM((THIRD - FIRST + 2, WIDTH), BF16), pltpu.VMEM((D, PROJ), F32), pltpu.SemaphoreType.DMA,
        ],
        compiler_params=pltpu.CompilerParams(vmem_limit_bytes=12 * 2**20),
        cost_estimate=cost(1.5),
    )(hbm(after(packed, active0)))
    head_rows = rows // PLACES * ndp
    lanes = 4 * QUARTER_PAD
    stages = dp_stages()
    head_stages = stages[1:] + stages[:1]
    offsets = [0]
    for steps in head_stages:
        offsets = offsets + [o ^ step for step in steps for o in offsets]
    small = head_rows <= 128 and images * ndp == 32 and queue.shape[1] * ndp <= 512
    if small:
        queued = ndp * queue.shape[1]
        mass, column, match = call(
            k(mass_kernel, micro, images, sum(told_offsets, [])),
            (
                shape((queued, lanes), BF16), shape((8, lanes), F32),
                shape((micro, images * ndp, images * ndp), BF16),
            ),
            place, table, *told,
            scratch=[pltpu.VMEM((queued, PROJ), BF16), pltpu.VMEM((queued, lanes), F32)],
            vmem=16, us=5,
        )
        *actives0, mass = lax.optimization_barrier((*actives0, mass))
    pre1, part = call(
        k(conv_kernel, micro, images),
        (pieces_of(PART, F32), sums_of),
        place, *actives0, *w_conv,
        scratch=[pltpu.VMEM((rows, WIDTH), BF16), pltpu.VMEM((WIDTH, 9 * PART), BF16)],
        us=3,
    )
    sums1 = sum_dp(part)
    active1_own = call(k(active_kernel, micro, count), pieces_of(PART, BF16), pre1, sums1, conv_part, us=1)
    actives1 = gather_xor(active1_own, "section")
    natural = unpack(after(packed, active1_own), FIRST)
    taps = call(k(taps_kernel, images), pieces_of(9 * PART, BF16), after(active0, active1_own), us=1.3)
    *actives1, natural, taps = lax.optimization_barrier((*actives1, natural, taps))
    active1, pre2, part, w_expand = call(
        k(expand_kernel, micro),
        (pieces_of(WIDTH, BF16), pieces_of(WIDE, F32), shape((8, WIDE), F32), shape((WIDTH, WIDE), BF16)),
        place, *actives1, *pair_parts,
        us=2,
    )
    back_rows = 9 * PART // 2 + WIDE // 2
    back_own = call(
        back_parts_kernel, [shape((back_rows, PART), BF16)] * 4, place, *w_conv, *pair_parts, us=1
    )
    back_own = lax.optimization_barrier((*back_own, part))[:4]
    back_came = [back_own[0]] + [flip(back_own[j], "section", j) for j in range(1, SECTIONS)]

    sums2 = sum_dp(part)
    pooled = call(
        k(pool_kernel, micro, images, count),
        shape((rows // PLACES, WIDE), BF16),
        place, pre2, sums2, pair_part, flat,
        us=1.6,
    )

    per_dp = rows // PLACES
    came_p = gather_xor(pooled, "section")[::-1]
    pooled_here = call(lanes_kernel, shape((per_dp, D), BF16), *came_p, us=0.3)
    parts, _ = gather_dp(pooled_here, head_stages)
    if small:
        all_pooled, active3, unit, d_scores, embed, *kept, said = call(
            k(head_kernel, micro, images, offsets),
            [
                shape((head_rows, D), BF16), shape((head_rows, D), BF16), shape((head_rows, PROJ), BF16),
                shape((head_rows // 2, lanes), BF16), shape((head_rows, PROJ), F32), shape((head_rows, D), F32),
                shape((head_rows, D), F32), shape((8, D), F32), shape((head_rows // 2 + 8, PROJ), F32),
            ],
            place, *parts, natural, w_proj, table, norm3, mass, column, match,
            scratch=[
                pltpu.VMEM((head_rows, lanes), F32), pltpu.VMEM((head_rows // 2, lanes), F32),
                pltpu.VMEM((micro, 8, lanes), F32), pltpu.VMEM((8, lanes), F32),
            ],
            vmem=15, us=12,
        )
        *d_pooled, notes3, d_embed, d_pre3 = call(
            k(head_back_kernel, micro, images, ndp),
            [shape((per_dp, WIDE), BF16)] * 4
            + [shape((8, D), F32), shape((head_rows, PROJ), BF16), shape((head_rows, D), BF16)],
            place, said, flip(said, "dp", 1), embed, w_proj, natural, norm3, *kept,
            scratch=[pltpu.VMEM((head_rows, PROJ), F32), pltpu.VMEM((per_dp, D), BF16)],
            us=5,
        )
    else:
        all_pooled = jnp.concatenate(parts)
        offset = jnp.array(offsets, jnp.int32)
        head_order = jnp.arange(head_rows, dtype=jnp.int32)
        block, inner = head_order // per_dp, head_order % per_dp
        group, single = inner // images, inner % images
        position = (group * ndp + (offset[block] ^ dp)) * images + single
        order = (position[None, :] == head_order[:, None]).astype(BF16)
        told = jnp.concatenate(told).reshape(ndp, queue_size + 16, PROJ)
        pairs = told[:, queue_size : queue_size + micro, :images].astype(jnp.int32)
        told_offset = jnp.array(sum(told_offsets, []), jnp.int32)
        pairs_dp = (told_offset ^ dp)[None, :] == jnp.arange(ndp, dtype=jnp.int32)[:, None]
        pairs = jnp.sum(jnp.where(pairs_dp[:, :, None, None], pairs[None], 0), axis=1)
        left = jnp.arange(images * ndp, dtype=jnp.int32)
        pairs = pairs.transpose(1, 0, 2).reshape(micro, ndp * images)
        match = ((left // images * images + pairs)[:, :, None] == left[None, None, :]).astype(F32)
        all_pooled = dot(order, all_pooled).astype(BF16)
        protos = jnp.concatenate([table[:, a * PROJ : (a + 1) * PROJ] for a in range(4)], axis=0)
        queue_all = told[:, :queue_size].reshape(ndp, CROPS, queue.shape[1], PROJ)
        queue_rows = queue_all.transpose(1, 0, 2, 3).reshape(CROPS, -1, PROJ)
        loss, grads3, active3, unit, d_scores, d_embed, d_pre3 = head(
            all_pooled, natural, w_proj, protos, norm3, queue_rows, match, micro, images, dp
        )
        notes3 = jnp.concatenate([grads3, jnp.full((5, D), loss)])
        d_pooled = dot_nt(dot_tn(order[:, :per_dp], d_pre3).astype(BF16), natural).astype(BF16)
        d_pooled = [d_pooled[:, j * WIDE : (j + 1) * WIDE] for j in range(SECTIONS)]
        d_scores = d_scores.reshape(micro, CROPS, head_rows // 4, lanes)
        d_scores = lax.dynamic_index_in_dim(d_scores, 1 - core, 1, keepdims=False).reshape(-1, lanes)

    came_d = [send(d_pooled[j], 3, j) for j in range(3)]
    back_half = call(stack_kernel, shape((SECTIONS, back_rows, PART), BF16), *back_came, us=0.6)
    back_halves = (back_half, flip(back_half, "dp", 1))
    d_z, part = call(
        k(out_back_kernel, micro, images, count),
        (pieces_of(WIDE, F32), shape((8, WIDE), F32)),
        place, pre2, sums2, pair_part, flat, d_pooled[3], *came_d,
        us=1.8,
    )
    back2 = sum_dp(part)
    d_pre2, *partial = call(
        k(expand_back_kernel, micro, count),
        [pieces_of(WIDE, BF16)] + [pieces_of(PART, BF16)] * 4,
        place, pre2, sums2, d_z, back2, pair_part, w_expand,
        scratch=[pltpu.VMEM((rows, WIDTH), F32)],
        us=2,
    )
    partial = [partial[0]] + [flip(partial[j], "section", j) for j in range(1, SECTIONS)]

    def scatter_start(a, b, width):
        if ndp != 8:
            return dot_tn(a, b)
        keep, out = call(
            pair_kernel,
            (shape((4, own, width), F32), shape((4, own, width), BF16)),
            place, a, b,
            scratch=[pltpu.VMEM((WIDTH, width), F32)],
            us=2.5,
        )
        return keep, flip(out, "dp", 1)

    def scatter_cross(started, *others):
        if ndp != 8:
            return [lax.psum_scatter(started.astype(BF16), "dp", scatter_dimension=0, tiled=True)]
        keep, came = started
        if others:
            keep = after(keep, *others)
        dims = keep.shape[1:]
        kept, *out = call(
            cross_kernel, [shape(dims, F32)] + [shape(dims, BF16)] * 3, place, keep, came
        )
        return [kept] + [flip(out[j], "dp", 2 * (j + 1)) for j in range(3)]

    def scatter_finish(crossed):
        if ndp != 8:
            return crossed[0].astype(BF16)
        return call(add_kernel, shape(crossed[0].shape, BF16), *crossed, us=0.6)

    expand_started = scatter_start(d_pre2, active1, WIDTH)
    base = call(
        head_grads_kernel,
        shape((own, param_rows), F32),
        place, after(all_pooled, d_pre2), active3, unit, d_scores, flip(d_scores, "dp", 1), d_embed, d_pre3,
        scratch=[pltpu.VMEM((4, own, D), BF16), pltpu.VMEM((4, all_pooled.shape[0], WIDTH), BF16)],
        us=6,
    )
    partial = lax.optimization_barrier((*partial, base))[:4]

    d_y1, part = call(
        k(silu_back_kernel, micro, count),
        (pieces_of(PART, F32), sums_of),
        *partial, pre1, sums1, conv_part,
    )
    back1 = sum_dp(part)
    d_pre1_own = call(
        k(norm_back_kernel, micro, count), pieces_of(PART, BF16), d_y1, pre1, sums1, back1, conv_part
    )
    d_pre1s = gather_xor(d_pre1_own, "section")
    expand_crossed = scatter_cross(expand_started, d_pre1_own)
    joined = lax.optimization_barrier((*d_pre1s, *expand_crossed))
    d_pre1s, expand_crossed = joined[:SECTIONS], joined[SECTIONS:]
    d_pre1, d_y0, part = call(
        k(conv_back_kernel, micro, images, count),
        (pieces_of(WIDTH, BF16), pieces_of(PART, F32), sums_of),
        place, *d_pre1s, *back_halves, pre0, sums0, pair_part,
        scratch=[pltpu.VMEM((9 * PART, WIDTH), BF16)],
        us=3.5,
    )
    back0, paired = sum_dp_steps(part)
    conv_started = scatter_start(after(d_pre1, paired), taps, 9 * PART)
    d_pre0_own = call(
        k(last_norm_back_kernel, micro, count),
        shape((rows + NOTE_ROWS, PART), BF16),
        place, d_y0, pre0, sums0, back0, pair_part, back2, back1, notes3,
    )
    d_pre0s = gather_xor(d_pre0_own, "section")
    conv_crossed = scatter_cross(conv_started, d_pre0_own)
    joined = lax.optimization_barrier((*d_pre0s, *conv_crossed))
    d_pre0s, conv_crossed = joined[:SECTIONS], joined[SECTIONS:]

    if ndp == 8:
        keep, out, d_pre0 = call(
            image_pair_kernel,
            (shape((4, own, WIDE), F32), shape((4, own, WIDE), BF16), pieces_of(WIDTH, BF16)),
            place, *d_pre0s, flat,
            scratch=[pltpu.VMEM((WIDTH, WIDE), F32)],
            us=2.5,
        )
        reduce_started = keep, flip(out, "dp", 1)
    else:
        d_pre0 = jnp.stack(d_pre0s)[place[:SECTIONS], :rows].transpose(1, 0, 2).reshape(rows, WIDTH)
        reduce_started = dot_tn(d_pre0, lax.dynamic_slice_in_dim(flat, t * WIDE, WIDE, 1))
    reduce_crossed = scatter_cross(reduce_started)
    grad_in = call(
        reduce_back_kernel,
        shape((rows // images, images, WIDE), F32),
        place, d_pre0, *back_halves, d_z,
        scratch=[pltpu.VMEM((WIDE, WIDTH), BF16)],
        us=2,
    )
    norm_grads, loss = call(
        told_kernel, (shape((3, D), F32), shape((8, PROJ), F32)), place, *d_pre0s, notes3, us=0.5
    )
    g_conv = scatter_finish(conv_crossed)
    g_expand = scatter_finish(expand_crossed)
    joined = lax.optimization_barrier((*reduce_crossed, grad_in, norm_grads, g_conv, g_expand))
    *reduce_crossed, grad_in, norm_grads, g_conv, g_expand = joined
    g_reduce = scatter_finish(reduce_crossed)
    mixed = call(mixed_kernel, [shape(g_conv.shape, BF16)] * 3, place, g_reduce, g_conv, g_expand, us=0.3)
    mixed = [
        lax.ppermute(mixed[j - 1], "section", [(u ^ j, u) for u in range(3)]) for j in range(1, SECTIONS)
    ]
    weight_grads = pl.pallas_call(
        finish_kernel,
        name="finish",
        out_shape=shape((own, param_rows), F32),
        in_specs=[pl.BlockSpec(memory_space=pltpu.SMEM), pl.BlockSpec(memory_space=pltpu.HBM)]
        + [pl.BlockSpec(memory_space=pltpu.VMEM)] * 6,
        out_specs=pl.BlockSpec(memory_space=pltpu.HBM),
        scratch_shapes=[pltpu.VMEM((own, 9 * WIDTH), F32), pltpu.SemaphoreType.DMA],
        input_output_aliases={1: 0},
        compiler_params=pltpu.CompilerParams(vmem_limit_bytes=12 * 2**20),
        cost_estimate=cost(2),
    )(place, base, g_reduce, g_conv, g_expand, *mixed)
    grad_in = grad_in.reshape(micro, CROPS, SIDE, SIDE, images, WIDE).transpose(0, 1, 4, 2, 3, 5)
    return (loss[0, 0], grad_in, weight_grads.T[None], norm_grads[None])


def solution(mesh):
    in_specs = (
        P(None, None, "dp", None, None, None),
        P("section", None, None),
        P("section", None, None),
        P(None, "dp", None),
        P(None, "dp"),
    )
    out_specs = (
        P(),
        P(None, None, "dp", None, None, "section"),
        P("section", None, "dp"),
        P("section", None, None),
    )
    return jax.shard_map(body, mesh=mesh, in_specs=in_specs, out_specs=out_specs, check_vma=False)
```

profile of v0, /device:TPU:2, one launch (start us, length us, event | category | flops | bytes accessed | tf_op | source)
XLA Modules:
  0.0 244.8 jit_solution(16841176671510368195)
XLA Ops:
  1.5 2.4 pack.1
  7.3 5.9 %collective-permute-start.2 = (bf16[1168,128]{1,0:T(8,128)(2,1)S(1)}, bf16[1168,128]{1,0:T(8,128)(2,1)S(1)}, u32[]{:S(2)}, u32[]{:S(2)}) collective-permute-start(bf16[1168,128]{1,0:T(8,128)(2,1)S(1)} %get-tuple-element.139), channel_id=1, source_target_pairs={{0,24},{8,16},{16,8},{1,25},{9,17},{17,9},{2,26},{10,18},{18,10},{... | collective-permute-start | bytes 897032 | tf_op jit(solution)/shard_map/ppermute | solution.py:1195
  15.1 3.6 %collective-permute-start.6 = (bf16[288,128]{1,0:T(8,128)(2,1)S(1)}, bf16[288,128]{1,0:T(8,128)(2,1)S(1)}, u32[]{:S(2)}, u32[]{:S(2)}) collective-permute-start(bf16[288,128]{1,0:T(8,128)(2,1)S(1)} %rows_kernel.3.refs_0_), channel_id=1, source_target_pairs={{0,6},{1,7},{2,4},{3,5},{4,2},{5,3},{6,0},{7,1},{8,14},{9,15},{10,... | collective-permute-start | bytes 221192 | tf_op jit(solution)/shard_map/ppermute | solution.py:55
  18.7 3.0 %collective-permute-done.6.refs_3_ = bf16[288,128]{1,0:T(8,128)(2,1)S(1)} collective-permute-done((bf16[288,128]{1,0:T(8,128)(2,1)S(1)}, bf16[288,128]{1,0:T(8,128)(2,1)S(1)}, u32[]{:S(2)}, u32[]{:S(2)}) %collective-permute-start.6) | collective-permute-done | bytes 73760 | tf_op jit(solution)/shard_map/ppermute | solution.py:55
  21.7 3.1 %collective-permute-start.4 = (bf16[288,128]{1,0:T(8,128)(2,1)S(1)}, bf16[288,128]{1,0:T(8,128)(2,1)S(1)}, u32[]{:S(2)}, u32[]{:S(2)}) collective-permute-start(bf16[288,128]{1,0:T(8,128)(2,1)S(1)} %rows_kernel.3.refs_0_), channel_id=1, source_target_pairs={{0,2},{1,3},{2,0},{3,1},{4,6},{5,7},{6,4},{7,5},{8,10},{9,11},{10,... | collective-permute-start | bytes 221192 | tf_op jit(solution)/shard_map/ppermute | solution.py:55
  32.8 2.7 %collective-permute-start.11 = (f32[8,128]{1,0:T(8,128)S(1)}, f32[8,128]{1,0:T(8,128)S(1)}, u32[]{:S(2)}, u32[]{:S(2)}) collective-permute-start(f32[8,128]{1,0:T(8,128)S(1)} %add.82), channel_id=1, source_target_pairs={{0,6},{1,7},{2,4},{3,5},{4,2},{5,3},{6,0},{7,1},{8,14},{9,15},{10,... | collective-permute-start | bytes 12296 | tf_op jit(solution)/shard_map/ppermute | solution.py:55
  40.5 3.4 %collective-permute-start.12 = (bf16[784,128]{1,0:T(8,128)(2,1)S(1)}, bf16[784,128]{1,0:T(8,128)(2,1)S(1)}, u32[]{:S(2)}, u32[]{:S(2)}) collective-permute-start(bf16[784,128]{1,0:T(8,128)(2,1)S(1)} %active_kernel.2.a0.active), channel_id=1, source_target_pairs={{0,8},{8,0},{16,24},{24,16},{1,9},{9,1},{17,25},{25,17},{2,10},{10... | collective-permute-start | bytes 602120 | tf_op jit(solution)/shard_map/ppermute | solution.py:55
  45.5 3.0 %mass_kernel.1 = (bf16[512,3072]{1,0:T(8,128)(2,1)S(1)}, f32[8,3072]{1,0:T(8,128)S(1)}, bf16[2,32,32]{2,1,0:T(8,128)(2,1)S(1)}) custom-call(s32[9]{0:T(128)S(1)} %stack.39.place, bf16[768,512]{1,0:T(8,128)(2,1)S(1)} %get-tuple-element.149.table, bf16[288,128]{1,0:T(8,128)(2,1)S(1)} %rows_kernel.3.refs_0_, ...), custom_call_target="tpu_custom_call" | custom-call | bytes 15000000 | tf_op jit(solution)/shard_map/mass_kernel/pallas_call | solution.py:139
  49.2 2.9 %collective-permute-done.13.a2 = bf16[784,128]{1,0:T(8,128)(2,1)S(1)} collective-permute-done((bf16[784,128]{1,0:T(8,128)(2,1)S(1)}, bf16[784,128]{1,0:T(8,128)(2,1)S(1)}, u32[]{:S(2)}, u32[]{:S(2)}) %collective-permute-start.13) | collective-permute-done | bytes 200736 | tf_op jit(solution)/shard_map/ppermute | solution.py:55
  52.1 2.5 %conv_kernel.1 = (f32[784,128]{1,0:T(8,128)S(1)}, f32[8,128]{1,0:T(8,128)S(1)}) custom-call(s32[9]{0:T(128)S(1)} %stack.39.place, bf16[784,128]{1,0:T(8,128)(2,1)S(1)} %active_kernel.2.a0.active, bf16[784,128]{1,0:T(8,128)(2,1)S(1)} %collective-permute-done.12.a1, bf16[784,128]{1,0:T(8,128)(2,1)S(1)} %collective-permute-done.13.a2, ...), custom_call_target="tpu_custom_call" | custom-call | bytes 9000000 | tf_op jit(solution)/shard_map/conv_kernel/pallas_call | solution.py:139
  66.9 3.7 %unpack.1.w_head = bf16[2048,2048]{1,0:T(8,128)(2,1)S(1)} custom-call(bf16[9456,512]{1,0:T(8,128)(2,1)S(1)} %bitcast.28), custom_call_target="tpu_custom_call" | custom-call | bytes 12000000 | tf_op jit(solution)/shard_map/unpack/pallas_call | solution.py:1048
  88.4 2.3 collective-permute-done.28.refs_0_
  103.2 10.8 %head_kernel.1 = (bf16[128,2048]{1,0:T(8,128)(2,1)S(1)}, bf16[128,2048]{1,0:T(8,128)(2,1)S(1)}, bf16[128,128]{1,0:T(8,128)(2,1)S(1)}, bf16[64,3072]{1,0:T(8,128)...) custom-call(s32[9]{0:T(128)S(1)} %stack.39.place, ...), custom_call_target="tpu_custom_call" | custom-call | bytes 36000000 | tf_op jit(solution)/shard_map/head_kernel/pallas_call | solution.py:139
  115.3 4.5 %head_back_kernel.1 = (bf16[16,512]{1,0:T(8,128)(2,1)S(1)}, bf16[16,512]{1,0:T(8,128)(2,1)S(1)}, bf16[16,512]{1,0:T(8,128)(2,1)S(1)}, bf16[16,512]{1,0:T(8,128)(...) custom-call(s32[9]{0:T(128)S(1)} %stack.39.place, ...), custom_call_target="tpu_custom_call" | custom-call | bytes 15000000 | tf_op jit(solution)/shard_map/head_back_kernel/pallas_call | solution.py:139
  122.5 4.7 %collective-permute-done.37.r1 = bf16[16,512]{1,0:T(8,128)(2,1)S(1)} collective-permute-done((bf16[16,512]{1,0:T(8,128)(2,1)S(1)}, bf16[16,512]{1,0:T(8,128)(2,1)S(1)}, u32[]{:S(2)}, u32[]{:S(2)}) %collective-permute-start.37) | collective-permute-done | bytes 16416 | tf_op jit(solution)/shard_map/ppermute | solution.py:59
  139.4 2.6 %collective-permute-start.44 = (bf16[784,128]{1,0:T(8,128)(2,1)S(1)}, bf16[784,128]{1,0:T(8,128)(2,1)S(1)}, u32[]{:S(2)}, u32[]{:S(2)}) collective-permute-start(bf16[784,128]{1,0:T(8,128)(2,1)S(1)} %get-tuple-element.187), channel_id=1, source_target_pairs={{0,16},{8,24},{16,0},{24,8},{1,17},{9,25},{17,1},{25,9},{2,18},{10... | collective-permute-start | bytes 602120 | tf_op jit(solution)/shard_map/ppermute | solution.py:55
  143.5 2.4 head_grads_kernel.1.base
  146.1 3.9 %collective-permute-done.44.q2 = bf16[784,128]{1,0:T(8,128)(2,1)S(1)} collective-permute-done((bf16[784,128]{1,0:T(8,128)(2,1)S(1)}, bf16[784,128]{1,0:T(8,128)(2,1)S(1)}, u32[]{:S(2)}, u32[]{:S(2)}) %collective-permute-start.44) | collective-permute-done | bytes 200736 | tf_op jit(solution)/shard_map/ppermute | solution.py:55
  159.7 4.6 %collective-permute-start.52 = (bf16[784,128]{1,0:T(8,128)(2,1)S(1)}, bf16[784,128]{1,0:T(8,128)(2,1)S(1)}, u32[]{:S(2)}, u32[]{:S(2)}) collective-permute-start(bf16[784,128]{1,0:T(8,128)(2,1)S(1)} %norm_back_kernel.1.d0), channel_id=1, source_target_pairs={{0,16},{8,24},{16,0},{24,8},{1,17},{9,25},{17,1},{25,9},{2,18},{10... | collective-permute-start | bytes 602120 | tf_op jit(solution)/shard_map/ppermute | solution.py:55
  168.0 2.6 %collective-permute-done.55.r1 = bf16[64,512]{1,0:T(8,128)(2,1)S(1)} collective-permute-done((bf16[64,512]{1,0:T(8,128)(2,1)S(1)}, bf16[64,512]{1,0:T(8,128)(2,1)S(1)}, u32[]{:S(2)}, u32[]{:S(2)}) %collective-permute-start.55) | collective-permute-done | bytes 65568 | tf_op jit(solution)/shard_map/ppermute | solution.py:55
  172.5 3.4 %collective-permute-done.56.r2 = bf16[64,512]{1,0:T(8,128)(2,1)S(1)} collective-permute-done((bf16[64,512]{1,0:T(8,128)(2,1)S(1)}, bf16[64,512]{1,0:T(8,128)(2,1)S(1)}, u32[]{:S(2)}, u32[]{:S(2)}) %collective-permute-start.56) | collective-permute-done | bytes 65568 | tf_op jit(solution)/shard_map/ppermute | solution.py:55
  175.8 4.1 %collective-permute-start.57 = (bf16[64,512]{1,0:T(8,128)(2,1)S(1)}, bf16[64,512]{1,0:T(8,128)(2,1)S(1)}, u32[]{:S(2)}, u32[]{:S(2)}) collective-permute-start(bf16[64,512]{1,0:T(8,128)(2,1)S(1)} %get-tuple-element.210), channel_id=1, source_target_pairs={{0,6},{1,7},{2,4},{3,5},{4,2},{5,3},{6,0},{7,1},{8,14},{9,15},{10,... | collective-permute-start | bytes 196616 | tf_op jit(solution)/shard_map/ppermute | solution.py:55
  179.9 2.3 collective-permute-done.57.r3
  182.3 2.9 %conv_back_kernel.1 = (bf16[784,512]{1,0:T(8,128)(2,1)S(1)}, f32[784,128]{1,0:T(8,128)S(1)}, f32[8,128]{1,0:T(8,128)S(1)}) custom-call(s32[9]{0:T(128)S(1)} %stack.39.place, bf16[784,128]{1,0:T(8,128)(2,1)S(1)} %norm_back_kernel.1.d0, bf16[784,128]{1,0:T(8,128)(2,1)S(1)} %collective-permute-done.51.d1, bf16[784,128]{1,0:T(8,128)(2,1)S(1)} %collective-permute-done.52.d2, ...), custom_call_target="tpu_custom_call" | custom-call | bytes 10500000 | tf_op jit(solution)/shard_map/conv_back_kernel/pallas_call | solution.py:139
  188.8 3.7 %collective-permute-start.65 = (f32[8,128]{1,0:T(8,128)S(1)}, f32[8,128]{1,0:T(8,128)S(1)}, u32[]{:S(2)}, u32[]{:S(2)}) collective-permute-start(f32[8,128]{1,0:T(8,128)S(1)} %add.102), channel_id=1, source_target_pairs={{0,6},{1,7},{2,4},{3,5},{4,2},{5,3},{6,0},{7,1},{8,14},{9,15},{10,... | collective-permute-start | bytes 12296 | tf_op jit(solution)/shard_map/ppermute | solution.py:55
  194.3 2.8 %collective-permute-done.64 = f32[8,128]{1,0:T(8,128)S(1)} collective-permute-done((f32[8,128]{1,0:T(8,128)S(1)}, f32[8,128]{1,0:T(8,128)S(1)}, u32[]{:S(2)}, u32[]{:S(2)}) %collective-permute-start.64) | collective-permute-done | bytes 4128 | tf_op jit(solution)/shard_map/ppermute | solution.py:55
  204.3 2.7 %collective-permute-done.68.n3.d3 = bf16[832,128]{1,0:T(8,128)(2,1)S(1)} collective-permute-done((bf16[832,128]{1,0:T(8,128)(2,1)S(1)}, bf16[832,128]{1,0:T(8,128)(2,1)S(1)}, u32[]{:S(2)}, u32[]{:S(2)}) %collective-permute-start.68) | collective-permute-done | bytes 213024 | tf_op jit(solution)/shard_map/ppermute | solution.py:55
  210.1 5.2 %collective-permute-done.71.r2 = bf16[64,1152]{1,0:T(8,128)(2,1)S(1)} collective-permute-done((bf16[64,1152]{1,0:T(8,128)(2,1)S(1)}, bf16[64,1152]{1,0:T(8,128)(2,1)S(1)}, u32[]{:S(2)}, u32[]{:S(2)}) %collective-permute-start.71) | collective-permute-done | bytes 147488 | tf_op jit(solution)/shard_map/ppermute | solution.py:55
  224.8 2.5 %reduce_back_kernel.1 = f32[196,4,512]{2,1,0:T(4,128)} custom-call(s32[9]{0:T(128)S(1)} %stack.39.place, bf16[784,512]{1,0:T(8,128)(2,1)S(1)} %get-tuple-element.247.d_full, bf16[4,832,128]{2,1,0:T(8,128)(2,1)S(1)} %stack_kernel.1.back0, bf16[4,832,128]{2,1,0:T(8,128)(2,1)S(1)} %collective-permute-done.61.back1, f32[784,512]{1,0:T(8,128)S(1)} %get-tuple-element.182.d_z), custom_call_target="tpu_custom_call" | custom-call | bytes 6000000 | tf_op jit(solution)/shard_map/reduce_back_kernel/pallas_call | solution.py:139
  230.1 2.6 %collective-permute-start.77 = (bf16[64,1152]{1,0:T(8,128)(2,1)S(1)}, bf16[64,1152]{1,0:T(8,128)(2,1)S(1)}, u32[]{:S(2)}, u32[]{:S(2)}) collective-permute-start(bf16[64,1152]{1,0:T(8,128)(2,1)S(1)} %get-tuple-element.264), channel_id=1, source_target_pairs={{8,0},{0,8},{24,16},{9,1},{1,9},{25,17},{10,2},{2,10},{26,18},{11,... | collective-permute-start | bytes 442376 | tf_op jit(solution)/shard_map/ppermute | solution.py:1465
  234.0 5.4 %collective-permute-start.79 = (bf16[64,1152]{1,0:T(8,128)(2,1)S(1)}, bf16[64,1152]{1,0:T(8,128)(2,1)S(1)}, u32[]{:S(2)}, u32[]{:S(2)}) collective-permute-start(bf16[64,1152]{1,0:T(8,128)(2,1)S(1)} %get-tuple-element.266), channel_id=1, source_target_pairs={{24,0},{16,8},{8,16},{25,1},{17,9},{9,17},{26,2},{18,10},{10,18},{... | collective-permute-start | bytes 442376 | tf_op jit(solution)/shard_map/ppermute | solution.py:1465
  240.5 2.4 collective-permute-done.78.m2
  (199 shorter events, 128.8 us)
Async XLA Ops:
  3.9 23.2 %collective-permute-start = (bf16[1168,128]{1,0:T(8,128)(2,1)S(1)}, bf16[1168,128]{1,0:T(8,128)(2,1)S(1)}, u32[]{:S(2)}, u32[]{:S(2)}) collective-permute-start(bf16[1168,128]{1,0:T(8,128)(2,1)S(1)} %get-tuple-element.137), channel_id=1, source_target_pairs={{0,8},{8,0},{16,24},{1,9},{9,1},{17,25},{2,10},{10,2},{18,26},{3,1... | collective-permute-start | bytes 897032 | tf_op jit(solution)/shard_map/ppermute | solution.py:1195
  5.9 21.3 %collective-permute-start.1 = (bf16[1168,128]{1,0:T(8,128)(2,1)S(1)}, bf16[1168,128]{1,0:T(8,128)(2,1)S(1)}, u32[]{:S(2)}, u32[]{:S(2)}) collective-permute-start(bf16[1168,128]{1,0:T(8,128)(2,1)S(1)} %get-tuple-element.138), channel_id=1, source_target_pairs={{0,16},{8,24},{16,0},{1,17},{9,25},{17,1},{2,18},{10,26},{18,2},{3... | collective-permute-start | bytes 897032 | tf_op jit(solution)/shard_map/ppermute | solution.py:1195
  7.3 19.8 %collective-permute-start.2 = (bf16[1168,128]{1,0:T(8,128)(2,1)S(1)}, bf16[1168,128]{1,0:T(8,128)(2,1)S(1)}, u32[]{:S(2)}, u32[]{:S(2)}) collective-permute-start(bf16[1168,128]{1,0:T(8,128)(2,1)S(1)} %get-tuple-element.139), channel_id=1, source_target_pairs={{0,24},{8,16},{16,8},{1,25},{9,17},{17,9},{2,26},{10,18},{18,10},{... | collective-permute-start | bytes 897032 | tf_op jit(solution)/shard_map/ppermute | solution.py:1195
  27.9 12.3 %collective-permute-start.15 = (bf16[1168,128]{1,0:T(8,128)(2,1)S(1)}, bf16[1168,128]{1,0:T(8,128)(2,1)S(1)}, u32[]{:S(2)}, u32[]{:S(2)}) collective-permute-start(bf16[1168,128]{1,0:T(8,128)(2,1)S(1)} %get-tuple-element.156.refs_0_), channel_id=1, source_target_pairs={{0,2},{1,3},{2,0},{3,1},{4,6},{5,7},{6,4},{7,5},{8,10},{9,11},{10,... | collective-permute-start | bytes 897032 | tf_op jit(solution)/shard_map/ppermute | solution.py:55
  40.3 11.8 %collective-permute-start.16 = (bf16[2336,128]{1,0:T(8,128)(2,1)S(1)}, bf16[2336,128]{1,0:T(8,128)(2,1)S(1)}, u32[]{:S(2)}, u32[]{:S(2)}) collective-permute-start(bf16[2336,128]{1,0:T(8,128)(2,1)S(1)} %rows_kernel.4.wa.told.conv_a), channel_id=1, source_target_pairs={{0,1},{1,0},{2,3},{3,2},{4,5},{5,4},{6,7},{7,6},{8,9},{9,8},{10,11... | collective-permute-start | bytes 1794056 | tf_op jit(solution)/shard_map/ppermute | solution.py:55
  40.4 8.8 %collective-permute-start.14 = (bf16[784,128]{1,0:T(8,128)(2,1)S(1)}, bf16[784,128]{1,0:T(8,128)(2,1)S(1)}, u32[]{:S(2)}, u32[]{:S(2)}) collective-permute-start(bf16[784,128]{1,0:T(8,128)(2,1)S(1)} %active_kernel.2.a0.active), channel_id=1, source_target_pairs={{0,24},{8,16},{16,8},{24,0},{1,25},{9,17},{17,9},{25,1},{2,26},{10... | collective-permute-start | bytes 602120 | tf_op jit(solution)/shard_map/ppermute | solution.py:55
  40.4 11.6 %collective-permute-start.13 = (bf16[784,128]{1,0:T(8,128)(2,1)S(1)}, bf16[784,128]{1,0:T(8,128)(2,1)S(1)}, u32[]{:S(2)}, u32[]{:S(2)}) collective-permute-start(bf16[784,128]{1,0:T(8,128)(2,1)S(1)} %active_kernel.2.a0.active), channel_id=1, source_target_pairs={{0,16},{8,24},{16,0},{24,8},{1,17},{9,25},{17,1},{25,9},{2,18},{10... | collective-permute-start | bytes 602120 | tf_op jit(solution)/shard_map/ppermute | solution.py:55
  40.5 11.5 %collective-permute-start.12 = (bf16[784,128]{1,0:T(8,128)(2,1)S(1)}, bf16[784,128]{1,0:T(8,128)(2,1)S(1)}, u32[]{:S(2)}, u32[]{:S(2)}) collective-permute-start(bf16[784,128]{1,0:T(8,128)(2,1)S(1)} %active_kernel.2.a0.active), channel_id=1, source_target_pairs={{0,8},{8,0},{16,24},{24,16},{1,9},{9,1},{17,25},{25,17},{2,10},{10... | collective-permute-start | bytes 602120 | tf_op jit(solution)/shard_map/ppermute | solution.py:55
  62.0 8.9 %collective-permute-start.23 = (bf16[784,128]{1,0:T(8,128)(2,1)S(1)}, bf16[784,128]{1,0:T(8,128)(2,1)S(1)}, u32[]{:S(2)}, u32[]{:S(2)}) collective-permute-start(bf16[784,128]{1,0:T(8,128)(2,1)S(1)} %active_kernel.3.a0), channel_id=1, source_target_pairs={{0,24},{8,16},{16,8},{24,0},{1,25},{9,17},{17,9},{25,1},{2,26},{10... | collective-permute-start | bytes 602120 | tf_op jit(solution)/shard_map/ppermute | solution.py:55
  63.3 9.9 %collective-permute-start.22 = (bf16[784,128]{1,0:T(8,128)(2,1)S(1)}, bf16[784,128]{1,0:T(8,128)(2,1)S(1)}, u32[]{:S(2)}, u32[]{:S(2)}) collective-permute-start(bf16[784,128]{1,0:T(8,128)(2,1)S(1)} %active_kernel.3.a0), channel_id=1, source_target_pairs={{0,16},{8,24},{16,0},{24,8},{1,17},{9,25},{17,1},{25,9},{2,18},{10... | collective-permute-start | bytes 602120 | tf_op jit(solution)/shard_map/ppermute | solution.py:55
  63.9 9.4 %collective-permute-start.21 = (bf16[784,128]{1,0:T(8,128)(2,1)S(1)}, bf16[784,128]{1,0:T(8,128)(2,1)S(1)}, u32[]{:S(2)}, u32[]{:S(2)}) collective-permute-start(bf16[784,128]{1,0:T(8,128)(2,1)S(1)} %active_kernel.3.a0), channel_id=1, source_target_pairs={{0,8},{8,0},{16,24},{24,16},{1,9},{9,1},{17,25},{25,17},{2,10},{10... | collective-permute-start | bytes 602120 | tf_op jit(solution)/shard_map/ppermute | solution.py:55
  99.7 33.2 %collective-permute-start.58 = (bf16[832,128]{1,0:T(8,128)(2,1)S(1)}, bf16[832,128]{1,0:T(8,128)(2,1)S(1)}, u32[]{:S(2)}, u32[]{:S(2)}) collective-permute-start(bf16[832,128]{1,0:T(8,128)(2,1)S(1)} %get-tuple-element.220), channel_id=1, source_target_pairs={{0,8},{8,0},{16,24},{24,16},{1,9},{9,1},{17,25},{25,17},{2,10},{10... | collective-permute-start | bytes 638984 | tf_op jit(solution)/shard_map/ppermute | solution.py:55
  100.7 34.0 %collective-permute-start.59 = (bf16[832,128]{1,0:T(8,128)(2,1)S(1)}, bf16[832,128]{1,0:T(8,128)(2,1)S(1)}, u32[]{:S(2)}, u32[]{:S(2)}) collective-permute-start(bf16[832,128]{1,0:T(8,128)(2,1)S(1)} %get-tuple-element.221), channel_id=1, source_target_pairs={{0,16},{8,24},{16,0},{24,8},{1,17},{9,25},{17,1},{25,9},{2,18},{10... | collective-permute-start | bytes 638984 | tf_op jit(solution)/shard_map/ppermute | solution.py:55
  102.1 32.6 %collective-permute-start.60 = (bf16[832,128]{1,0:T(8,128)(2,1)S(1)}, bf16[832,128]{1,0:T(8,128)(2,1)S(1)}, u32[]{:S(2)}, u32[]{:S(2)}) collective-permute-start(bf16[832,128]{1,0:T(8,128)(2,1)S(1)} %get-tuple-element.222), channel_id=1, source_target_pairs={{0,24},{8,16},{16,8},{24,0},{1,25},{9,17},{17,9},{25,1},{2,26},{10... | collective-permute-start | bytes 638984 | tf_op jit(solution)/shard_map/ppermute | solution.py:55
  134.7 47.5 %collective-permute-start.61 = (bf16[4,832,128]{2,1,0:T(8,128)(2,1)S(1)}, bf16[4,832,128]{2,1,0:T(8,128)(2,1)S(1)}, u32[]{:S(2)}, u32[]{:S(2)}) collective-permute-start(bf16[4,832,128]{2,1,0:T(8,128)(2,1)S(1)} %stack_kernel.1.back0), channel_id=1, source_target_pairs={{0,1},{1,0},{2,3},{3,2},{4,5},{5,4},{6,7},{7,6},{8,9},{9,8},{10,11... | collective-permute-start | bytes 2555912 | tf_op jit(solution)/shard_map/ppermute | solution.py:55
  134.8 8.6 %collective-permute-start.46 = (bf16[64,3072]{1,0:T(8,128)(2,1)S(1)}, bf16[64,3072]{1,0:T(8,128)(2,1)S(1)}, u32[]{:S(2)}, u32[]{:S(2)}) collective-permute-start(bf16[64,3072]{1,0:T(8,128)(2,1)S(1)} %get-tuple-element.194.d_here), channel_id=1, source_target_pairs={{0,1},{1,0},{2,3},{3,2},{4,5},{5,4},{6,7},{7,6},{8,9},{9,8},{10,11... | collective-permute-start | bytes 1179656 | tf_op jit(solution)/shard_map/ppermute | solution.py:55
  139.4 10.6 %collective-permute-start.44 = (bf16[784,128]{1,0:T(8,128)(2,1)S(1)}, bf16[784,128]{1,0:T(8,128)(2,1)S(1)}, u32[]{:S(2)}, u32[]{:S(2)}) collective-permute-start(bf16[784,128]{1,0:T(8,128)(2,1)S(1)} %get-tuple-element.187), channel_id=1, source_target_pairs={{0,16},{8,24},{16,0},{24,8},{1,17},{9,25},{17,1},{25,9},{2,18},{10... | collective-permute-start | bytes 602120 | tf_op jit(solution)/shard_map/ppermute | solution.py:55
  143.4 22.3 %collective-permute-start.54 = (bf16[4,64,512]{2,1,0:T(8,128)(2,1)S(1)}, bf16[4,64,512]{2,1,0:T(8,128)(2,1)S(1)}, u32[]{:S(2)}, u32[]{:S(2)}) collective-permute-start(bf16[4,64,512]{2,1,0:T(8,128)(2,1)S(1)} %get-tuple-element.206), channel_id=1, source_target_pairs={{0,1},{1,0},{2,3},{3,2},{4,5},{5,4},{6,7},{7,6},{8,9},{9,8},{10,11... | collective-permute-start | bytes 786440 | tf_op jit(solution)/shard_map/ppermute | solution.py:55
  158.1 24.1 %collective-permute-start.53 = (bf16[784,128]{1,0:T(8,128)(2,1)S(1)}, bf16[784,128]{1,0:T(8,128)(2,1)S(1)}, u32[]{:S(2)}, u32[]{:S(2)}) collective-permute-start(bf16[784,128]{1,0:T(8,128)(2,1)S(1)} %norm_back_kernel.1.d0), channel_id=1, source_target_pairs={{0,24},{8,16},{16,8},{24,0},{1,25},{9,17},{17,9},{25,1},{2,26},{10... | collective-permute-start | bytes 602120 | tf_op jit(solution)/shard_map/ppermute | solution.py:55
  159.7 22.5 %collective-permute-start.52 = (bf16[784,128]{1,0:T(8,128)(2,1)S(1)}, bf16[784,128]{1,0:T(8,128)(2,1)S(1)}, u32[]{:S(2)}, u32[]{:S(2)}) collective-permute-start(bf16[784,128]{1,0:T(8,128)(2,1)S(1)} %norm_back_kernel.1.d0), channel_id=1, source_target_pairs={{0,16},{8,24},{16,0},{24,8},{1,17},{9,25},{17,1},{25,9},{2,18},{10... | collective-permute-start | bytes 602120 | tf_op jit(solution)/shard_map/ppermute | solution.py:55
  164.3 17.9 %collective-permute-start.51 = (bf16[784,128]{1,0:T(8,128)(2,1)S(1)}, bf16[784,128]{1,0:T(8,128)(2,1)S(1)}, u32[]{:S(2)}, u32[]{:S(2)}) collective-permute-start(bf16[784,128]{1,0:T(8,128)(2,1)S(1)} %norm_back_kernel.1.d0), channel_id=1, source_target_pairs={{0,8},{8,0},{16,24},{24,16},{1,9},{9,1},{17,25},{25,17},{2,10},{10... | collective-permute-start | bytes 602120 | tf_op jit(solution)/shard_map/ppermute | solution.py:55
  188.6 12.8 %collective-permute-start.69 = (bf16[4,64,1152]{2,1,0:T(8,128)(2,1)S(1)}, bf16[4,64,1152]{2,1,0:T(8,128)(2,1)S(1)}, u32[]{:S(2)}, u32[]{:S(2)}) collective-permute-start(bf16[4,64,1152]{2,1,0:T(8,128)(2,1)S(1)} %get-tuple-element.231), channel_id=1, source_target_pairs={{0,1},{1,0},{2,3},{3,2},{4,5},{5,4},{6,7},{7,6},{8,9},{9,8},{10,11... | collective-permute-start | bytes 1769480 | tf_op jit(solution)/shard_map/ppermute | solution.py:55
  197.8 9.2 %collective-permute-start.68 = (bf16[832,128]{1,0:T(8,128)(2,1)S(1)}, bf16[832,128]{1,0:T(8,128)(2,1)S(1)}, u32[]{:S(2)}, u32[]{:S(2)}) collective-permute-start(bf16[832,128]{1,0:T(8,128)(2,1)S(1)} %last_norm_back_kernel.1.n0.d0), channel_id=1, source_target_pairs={{0,24},{8,16},{16,8},{24,0},{1,25},{9,17},{17,9},{25,1},{2,26},{10... | collective-permute-start | bytes 638984 | tf_op jit(solution)/shard_map/ppermute | solution.py:55
  199.3 10.1 %collective-permute-start.67 = (bf16[832,128]{1,0:T(8,128)(2,1)S(1)}, bf16[832,128]{1,0:T(8,128)(2,1)S(1)}, u32[]{:S(2)}, u32[]{:S(2)}) collective-permute-start(bf16[832,128]{1,0:T(8,128)(2,1)S(1)} %last_norm_back_kernel.1.n0.d0), channel_id=1, source_target_pairs={{0,16},{8,24},{16,0},{24,8},{1,17},{9,25},{17,1},{25,9},{2,18},{10... | collective-permute-start | bytes 638984 | tf_op jit(solution)/shard_map/ppermute | solution.py:55
  200.1 10.0 %collective-permute-start.66 = (bf16[832,128]{1,0:T(8,128)(2,1)S(1)}, bf16[832,128]{1,0:T(8,128)(2,1)S(1)}, u32[]{:S(2)}, u32[]{:S(2)}) collective-permute-start(bf16[832,128]{1,0:T(8,128)(2,1)S(1)} %last_norm_back_kernel.1.n0.d0), channel_id=1, source_target_pairs={{0,8},{8,0},{16,24},{24,16},{1,9},{9,1},{17,25},{25,17},{2,10},{10... | collective-permute-start | bytes 638984 | tf_op jit(solution)/shard_map/ppermute | solution.py:55
  202.2 13.1 %collective-permute-start.71 = (bf16[64,1152]{1,0:T(8,128)(2,1)S(1)}, bf16[64,1152]{1,0:T(8,128)(2,1)S(1)}, u32[]{:S(2)}, u32[]{:S(2)}) collective-permute-start(bf16[64,1152]{1,0:T(8,128)(2,1)S(1)} %get-tuple-element.234), channel_id=1, source_target_pairs={{0,4},{1,5},{2,6},{3,7},{4,0},{5,1},{6,2},{7,3},{8,12},{9,13},{10,... | collective-permute-start | bytes 442376 | tf_op jit(solution)/shard_map/ppermute | solution.py:55
  207.0 8.3 %collective-permute-start.72 = (bf16[64,1152]{1,0:T(8,128)(2,1)S(1)}, bf16[64,1152]{1,0:T(8,128)(2,1)S(1)}, u32[]{:S(2)}, u32[]{:S(2)}) collective-permute-start(bf16[64,1152]{1,0:T(8,128)(2,1)S(1)} %get-tuple-element.235), channel_id=1, source_target_pairs={{0,6},{1,7},{2,4},{3,5},{4,2},{5,3},{6,0},{7,1},{8,14},{9,15},{10,... | collective-permute-start | bytes 442376 | tf_op jit(solution)/shard_map/ppermute | solution.py:55
  219.0 8.2 %collective-permute-start.74 = (bf16[64,512]{1,0:T(8,128)(2,1)S(1)}, bf16[64,512]{1,0:T(8,128)(2,1)S(1)}, u32[]{:S(2)}, u32[]{:S(2)}) collective-permute-start(bf16[64,512]{1,0:T(8,128)(2,1)S(1)} %get-tuple-element.244), channel_id=1, source_target_pairs={{0,2},{1,3},{2,0},{3,1},{4,6},{5,7},{6,4},{7,5},{8,10},{9,11},{10,... | collective-permute-start | bytes 196616 | tf_op jit(solution)/shard_map/ppermute | solution.py:55
  221.2 8.2 %collective-permute-start.75 = (bf16[64,512]{1,0:T(8,128)(2,1)S(1)}, bf16[64,512]{1,0:T(8,128)(2,1)S(1)}, u32[]{:S(2)}, u32[]{:S(2)}) collective-permute-start(bf16[64,512]{1,0:T(8,128)(2,1)S(1)} %get-tuple-element.245), channel_id=1, source_target_pairs={{0,4},{1,5},{2,6},{3,7},{4,0},{5,1},{6,2},{7,3},{8,12},{9,13},{10,... | collective-permute-start | bytes 196616 | tf_op jit(solution)/shard_map/ppermute | solution.py:55
  230.1 10.4 %collective-permute-start.77 = (bf16[64,1152]{1,0:T(8,128)(2,1)S(1)}, bf16[64,1152]{1,0:T(8,128)(2,1)S(1)}, u32[]{:S(2)}, u32[]{:S(2)}) collective-permute-start(bf16[64,1152]{1,0:T(8,128)(2,1)S(1)} %get-tuple-element.264), channel_id=1, source_target_pairs={{8,0},{0,8},{24,16},{9,1},{1,9},{25,17},{10,2},{2,10},{26,18},{11,... | collective-permute-start | bytes 442376 | tf_op jit(solution)/shard_map/ppermute | solution.py:1465
  232.7 10.2 %collective-permute-start.78 = (bf16[64,1152]{1,0:T(8,128)(2,1)S(1)}, bf16[64,1152]{1,0:T(8,128)(2,1)S(1)}, u32[]{:S(2)}, u32[]{:S(2)}) collective-permute-start(bf16[64,1152]{1,0:T(8,128)(2,1)S(1)} %get-tuple-element.265), channel_id=1, source_target_pairs={{16,0},{24,8},{0,16},{17,1},{25,9},{1,17},{18,2},{26,10},{2,18},{1... | collective-permute-start | bytes 442376 | tf_op jit(solution)/shard_map/ppermute | solution.py:1465
  234.0 8.9 %collective-permute-start.79 = (bf16[64,1152]{1,0:T(8,128)(2,1)S(1)}, bf16[64,1152]{1,0:T(8,128)(2,1)S(1)}, u32[]{:S(2)}, u32[]{:S(2)}) collective-permute-start(bf16[64,1152]{1,0:T(8,128)(2,1)S(1)} %get-tuple-element.266), channel_id=1, source_target_pairs={{24,0},{16,8},{8,16},{25,1},{17,9},{9,17},{26,2},{18,10},{10,18},{... | collective-permute-start | bytes 442376 | tf_op jit(solution)/shard_map/ppermute | solution.py:1465
  (54 other events, 348.1 us)
where the time goes:
time: 247 us; the launch traced here: 245 us
  starting transfers between devices  108 us (44%)
  waiting for transfers between devices  73.9 us (30%)
  Pallas kernels  59.6 us (24%)
    ppermute x71, starting transfers between devices, flip(): lax.ppermute(value, axis, [(source, source ^ step) for source in range(co...  86.6 us
    ppermute x71, waiting for transfers between devices, flip(): lax.ppermute(value, axis, [(source, source ^ step) for source in range(co...  66.9 us
    pallas_call x38, Pallas kernels, call(): pl.pallas_call(kernel, name=getattr(kernel, 'func', kernel).__name__, out...  50.3 us
    ppermute x3, starting transfers between devices, body(): lax.ppermute(mixed[j - 1], 'section', [(u ^ j, u) for u in range(3)])  9.21 us
    ppermute x3, starting transfers between devices, body(): lax.ppermute(messages[j - 1], 'section', [(u, u ^ j) for u in range(3)])  9.21 us
  transfers between devices with their start and end apart: 80, of which 47 were waited for; matrix products, arithmetic and copies ran while one was open for 0% of the time, Pallas kernels for 17%

commit v1 on v0

--- a/solution.py
+++ b/solution.py
@@ -357,8 +357,10 @@
     lanes = pl.ds(pl.multiple_of(place[0] * WIDE, WIDE), WIDE)
     rows = pre.shape[0]
     gain, shift = told_wide(told)
-    came = (r0[...].astype(F32) + r1[...].astype(F32) + r2[...].astype(F32)).astype(BF16)
-    d_pooled = jnp.where(place[0] == SECTIONS - 1, own[...], came)
+    d_pooled = own[...].astype(F32)
+    for k, came in enumerate((r0, r1, r2)):
+        d_pooled = jnp.where(place[k + 1] == SECTIONS - 1, came[...].astype(F32), d_pooled)
+    d_pooled = d_pooled.astype(BF16)
     spread = dot_tn(crop_rows(rows, images), d_pooled) * (1.0 / PLACES)
     xhats = [x for x, _ in normalized(pre[...], sums[...], micro, count)]
     z = join([x * gain + shift for x in xhats]) + image[:, lanes].astype(F32)
@@ -948,7 +950,7 @@
     return (row == lane + place[7] * own).astype(F32).astype(BF16)
 
 
-def head_grads_kernel(place, pooled, active, unit, d_here, d_there, d_embed, d_pre, out, parts, apart):
+def head_grads_kernel(place, pooled, active, unit, d_here, d_there, d_embed, d_pre, out, parts):
     @pl.when(place[0] != SECTIONS - 1)
     def _():
         out[...] = jnp.zeros_like(out)
@@ -958,27 +960,31 @@
         own = out.shape[0]
         choose = own_columns(place, own)
         weave = interleave(PART)
-        block = PART
-
-        def product(q, carry):
-            own_d = dot(d_pre[:, lanes_at(q, WIDTH)], choose).astype(BF16)
-            parts[q] = dot_tn(own_d, pooled[...]).astype(BF16)
+        own_d = [dot(d_pre[:, q * WIDTH : (q + 1) * WIDTH], choose).astype(BF16) for q in range(4)]
+        own_d = jnp.concatenate(own_d, axis=1)
+
+        def product(b, carry):
+            parts[:, lanes_at(b, WIDTH)] = dot_tn(own_d, pooled[:, lanes_at(b, WIDTH)]).astype(BF16)
             return carry
 
         lax.fori_loop(0, 4, product, 0)
 
         def mix(b, carry):
-            mixed = jnp.concatenate([parts[q, :, lanes_at(b, block)] for q in range(4)], axis=1)
-            out[:, lanes_at(b, 4 * block)] = dot(mixed, weave)
+            mixed = []
+            for j in range(4):
+                lanes = pl.ds(pl.multiple_of(b * WIDTH + j * PART, PART), PART)
+                four = [parts[q * own : (q + 1) * own, lanes] for q in range(4)]
+                mixed.append(jnp.concatenate(four, axis=1))
+            mixed = dot(jnp.concatenate(mixed, axis=0), weave)
+            for j in range(4):
+                lanes = pl.ds(pl.multiple_of((4 * b + j) * WIDTH, WIDTH), WIDTH)
+                out[:, lanes] = mixed[j * own : (j + 1) * own, :]
             return carry
 
-        lax.fori_loop(0, D // block, mix, 0)
-
-        def part(b, carry):
-            apart[b] = dot_nt(active[:, lanes_at(b, WIDTH)], weave).astype(BF16)
-            return carry
-
-        lax.fori_loop(0, 4, part, 0)
+        lax.fori_loop(0, 4, mix, 0)
+        rows = active.shape[0]
+        wide = jnp.concatenate([active[:, b * WIDTH : (b + 1) * WIDTH] for b in range(4)], axis=0)
+        wide = dot_nt(wide, weave).astype(BF16)
         half = d_here.shape[0] // 2
         units = []
         for core in (place[5], place[4]):
@@ -988,8 +994,8 @@
         for a in range(4):
             some = choose[a * PROJ : (a + 1) * PROJ, :]
             own_e = dot(d_embed[...], some).astype(BF16)
-            column = jnp.concatenate([apart[b, :, a * block : (a + 1) * block] for b in range(4)], axis=1)
-            proj = proj + dot_tn(own_e, column)
+            column = [wide[b * rows : (b + 1) * rows, a * PART : (a + 1) * PART] for b in range(4)]
+            proj = proj + dot_tn(own_e, jnp.concatenate(column, axis=1))
             for own_unit, d_scores in zip(units, (d_here, d_there)):
                 own_u = dot(own_unit, some).astype(BF16)
                 proto = proto + dot_tn(own_u, d_scores[:, a * QUARTER_PAD : (a + 1) * QUARTER_PAD])
@@ -1160,6 +1166,22 @@
     for k, o in enumerate((own, o1, o2, o3)):
         z = place[6] ^ k
         o[...] = (keep[z] + came[z].astype(F32)).astype(o.dtype)
+
+
+def near_kernel(place, keep, came, kept, out):
+    for j in range(2):
+        mine, other = place[6] ^ (2 * j), place[6] ^ (2 * j + 1)
+        kept[j] = keep[mine] + came[mine].astype(F32)
+        out[j] = (keep[other] + came[other].astype(F32)).astype(BF16)
+
+
+def far_kernel(keep, came, kept, out):
+    kept[...] = keep[0] + came[0].astype(F32)
+    out[...] = (keep[1] + came[1].astype(F32)).astype(BF16)
+
+
+def last_kernel(keep, came, out):
+    out[...] = (keep[...] + came[...].astype(F32)).astype(BF16)
 
 
 def add_kernel(own, r1, r2, r3, out):
@@ -1264,16 +1286,17 @@
     actives1 = gather_xor(active1_own, "section")
     natural = unpack(after(packed, active1_own), FIRST)
     taps = call(k(taps_kernel, images), pieces_of(9 * PART, BF16), after(active0, active1_own), us=1.3)
-    *actives1, natural, taps = lax.optimization_barrier((*actives1, natural, taps))
+    back_rows = 9 * PART // 2 + WIDE // 2
+    back_own = call(
+        back_parts_kernel, [shape((back_rows, PART), BF16)] * 4, place, *w_conv, *pair_parts, us=1
+    )
+    joined = lax.optimization_barrier((*actives1, natural, taps, *back_own))
+    actives1, natural, taps, back_own = joined[:4], joined[4], joined[5], joined[6:]
     active1, pre2, part, w_expand = call(
         k(expand_kernel, micro),
         (pieces_of(WIDTH, BF16), pieces_of(WIDE, F32), shape((8, WIDE), F32), shape((WIDTH, WIDE), BF16)),
         place, *actives1, *pair_parts,
         us=2,
-    )
-    back_rows = 9 * PART // 2 + WIDE // 2
-    back_own = call(
-        back_parts_kernel, [shape((back_rows, PART), BF16)] * 4, place, *w_conv, *pair_parts, us=1
     )
     back_own = lax.optimization_barrier((*back_own, part))[:4]
     back_came = [back_own[0]] + [flip(back_own[j], "section", j) for j in range(1, SECTIONS)]
@@ -1342,7 +1365,9 @@
         d_scores = d_scores.reshape(micro, CROPS, head_rows // 4, lanes)
         d_scores = lax.dynamic_index_in_dim(d_scores, 1 - core, 1, keepdims=False).reshape(-1, lanes)
 
-    came_d = [send(d_pooled[j], 3, j) for j in range(3)]
+    joined = lax.optimization_barrier((*d_pooled, *back_came))
+    d_pooled, back_came = joined[:SECTIONS], joined[SECTIONS:]
+    came_d = [flip(d_pooled[3 ^ j], "section", j) for j in range(1, SECTIONS)]
     back_half = call(stack_kernel, shape((SECTIONS, back_rows, PART), BF16), *back_came, us=0.6)
     back_halves = (back_half, flip(back_half, "dp", 1))
     d_z, part = call(
@@ -1385,20 +1410,46 @@
         )
         return [kept] + [flip(out[j], "dp", 2 * (j + 1)) for j in range(3)]
 
+    def scatter_near(started, *others):
+        if ndp != 8:
+            return lax.psum_scatter(started.astype(BF16), "dp", scatter_dimension=0, tiled=True), None
+        keep, came = started
+        if others:
+            keep = after(keep, *others)
+        dims = (2, *keep.shape[1:])
+        kept, out = call(near_kernel, (shape(dims, F32), shape(dims, BF16)), place, keep, came, us=0.7)
+        return kept, flip(out, "dp", 2)
+
+    def scatter_far(started, *others):
+        if ndp != 8:
+            return started
+        keep, came = started
+        if others:
+            keep = after(keep, *others)
+        dims = keep.shape[1:]
+        kept, out = call(far_kernel, (shape(dims, F32), shape(dims, BF16)), keep, came, us=0.5)
+        return kept, flip(out, "dp", 4)
+
+    def scatter_last(started):
+        if ndp != 8:
+            return started[0].astype(BF16)
+        return call(last_kernel, shape(started[0].shape, BF16), *started, us=0.4)
+
     def scatter_finish(crossed):
         if ndp != 8:
             return crossed[0].astype(BF16)
         return call(add_kernel, shape(crossed[0].shape, BF16), *crossed, us=0.6)
 
-    expand_started = scatter_start(d_pre2, active1, WIDTH)
+    expand_near = scatter_near(scatter_start(d_pre2, active1, WIDTH))
     base = call(
         head_grads_kernel,
         shape((own, param_rows), F32),
         place, after(all_pooled, d_pre2), active3, unit, d_scores, flip(d_scores, "dp", 1), d_embed, d_pre3,
-        scratch=[pltpu.VMEM((4, own, D), BF16), pltpu.VMEM((4, all_pooled.shape[0], WIDTH), BF16)],
+        scratch=[pltpu.VMEM((4 * own, D), BF16)],
         us=6,
     )
-    partial = lax.optimization_barrier((*partial, base))[:4]
+    joined = lax.optimization_barrier((*partial, base, *expand_near[: 2 if ndp == 8 else 1]))
+    partial, base, expand_near = joined[:SECTIONS], joined[SECTIONS], joined[SECTIONS + 1 :]
 
     d_y1, part = call(
         k(silu_back_kernel, micro, count),
@@ -1410,9 +1461,9 @@
         k(norm_back_kernel, micro, count), pieces_of(PART, BF16), d_y1, pre1, sums1, back1, conv_part
     )
     d_pre1s = gather_xor(d_pre1_own, "section")
-    expand_crossed = scatter_cross(expand_started, d_pre1_own)
-    joined = lax.optimization_barrier((*d_pre1s, *expand_crossed))
-    d_pre1s, expand_crossed = joined[:SECTIONS], joined[SECTIONS:]
+    expand_far = scatter_far(expand_near, d_pre1_own)
+    joined = lax.optimization_barrier((*d_pre1s, *expand_far))
+    d_pre1s, expand_far = joined[:SECTIONS], joined[SECTIONS:]
     d_pre1, d_y0, part = call(
         k(conv_back_kernel, micro, images, count),
         (pieces_of(WIDTH, BF16), pieces_of(PART, F32), sums_of),
@@ -1420,17 +1471,17 @@
         scratch=[pltpu.VMEM((9 * PART, WIDTH), BF16)],
         us=3.5,
     )
-    back0, paired = sum_dp_steps(part)
-    conv_started = scatter_start(after(d_pre1, paired), taps, 9 * PART)
+    back0 = sum_dp(part)
     d_pre0_own = call(
         k(last_norm_back_kernel, micro, count),
         shape((rows + NOTE_ROWS, PART), BF16),
         place, d_y0, pre0, sums0, back0, pair_part, back2, back1, notes3,
     )
     d_pre0s = gather_xor(d_pre0_own, "section")
-    conv_crossed = scatter_cross(conv_started, d_pre0_own)
-    joined = lax.optimization_barrier((*d_pre0s, *conv_crossed))
-    d_pre0s, conv_crossed = joined[:SECTIONS], joined[SECTIONS:]
+    conv_near_sum = scatter_near(scatter_start(after(d_pre1, d_pre0_own), taps, 9 * PART))
+    joined = lax.optimization_barrier((*d_pre0s, conv_near_sum[0]))
+    d_pre0s, conv_near_sum = joined[:SECTIONS], (joined[SECTIONS], conv_near_sum[1])
+    conv_far = scatter_far(conv_near_sum)
 
     if ndp == 8:
         keep, out, d_pre0 = call(
@@ -1455,8 +1506,8 @@
     norm_grads, loss = call(
         told_kernel, (shape((3, D), F32), shape((8, PROJ), F32)), place, *d_pre0s, notes3, us=0.5
     )
-    g_conv = scatter_finish(conv_crossed)
-    g_expand = scatter_finish(expand_crossed)
+    g_conv = scatter_last(conv_far)
+    g_expand = scatter_last(expand_far)
     joined = lax.optimization_barrier((*reduce_crossed, grad_in, norm_grads, g_conv, g_expand))
     *reduce_crossed, grad_in, norm_grads, g_conv, g_expand = joined
     g_reduce = scatter_finish(reduce_crossed)

time: 247 us -> 231 us (0.935)
  starting transfers between devices: 108 us -> 100 us
  waiting for transfers between devices: 73.9 us -> 65.9 us
    ppermute x71 -> x72, starting transfers between devices: 86.6 us -> 81.7 us  [flip(): lax.ppermute(value, axis, [(source, source ^ step) for source in range(co...]
    ppermute x3 -> x0, waiting for transfers between devices: 4.67 us -> none  [send(): return lax.ppermute(value, 'section', [(source, target)])]
    ppermute x71 -> x72, waiting for transfers between devices: 66.9 us -> 63 us  [flip(): lax.ppermute(value, axis, [(source, source ^ step) for source in range(co...]
    ppermute x3 -> x0, starting transfers between devices: 2.62 us -> none  [send(): return lax.ppermute(value, 'section', [(source, target)])]
    pallas_call x38 -> x40, Pallas kernels: 50.3 us -> 50.4 us  [call(): pl.pallas_call(kernel, name=getattr(kernel, 'func', kernel).__name__, out...]
  transfers between devices with their start and end apart: 80 -> 78, of which waited for: 47 -> 47; matrix products, arithmetic and copies ran while one was open for 0% -> 1% of each run, Pallas kernels for 17% -> 18%
where the time goes in v1:
time: 231 us; the launch traced here: 229 us
  starting transfers between devices  100 us (43%)
  waiting for transfers between devices  65.9 us (29%)
  Pallas kernels  59.7 us (26%)
    ppermute x72, starting transfers between devices, flip(): lax.ppermute(value, axis, [(source, source ^ step) for source in range(co...  81.7 us
    ppermute x72, waiting for transfers between devices, flip(): lax.ppermute(value, axis, [(source, source ^ step) for source in range(co...  63 us
    pallas_call x40, Pallas kernels, call(): pl.pallas_call(kernel, name=getattr(kernel, 'func', kernel).__name__, out...  50.4 us
    ppermute x3, starting transfers between devices, body(): lax.ppermute(mixed[j - 1], 'section', [(u ^ j, u) for u in range(3)])  9.21 us
    ppermute x3, starting transfers between devices, body(): lax.ppermute(messages[j - 1], 'section', [(u, u ^ j) for u in range(3)])  9.21 us
  transfers between devices with their start and end apart: 78, of which 47 were waited for; matrix products, arithmetic and copies ran while one was open for 1% of the time, Pallas kernels for 18%

profile of v1, /device:TPU:2, one launch (start us, length us, event | category | flops | bytes accessed | tf_op | source)
XLA Modules:
  0.0 229.3 jit_solution(8059930443735764495)
XLA Ops:
  1.5 2.4 %pack.1 = (bf16[1168,128]{1,0:T(8,128)(2,1)S(1)}, bf16[1168,128]{1,0:T(8,128)(2,1)S(1)}, bf16[1168,128]{1,0:T(8,128)(2,1)S(1)}, bf16[1168,128]{1,0:T(8,128)(2,1)S(1)}) custom-call(s32[9]{0:T(128)S(1)} %stack.39.place, bf16[9456,512]{1,0:T(8,128)(2,1)} %bitcast.24, f32[3,2048]{1,0:T(4,128)S(1)} %bitcast.30), custom_call_target="tpu_custom_call" | custom-call | bytes 6000000 | tf_op jit(solution)/shard_map/pack/pallas_call | solution.py:1127
  7.3 5.9 %collective-permute-start.2 = (bf16[1168,128]{1,0:T(8,128)(2,1)S(1)}, bf16[1168,128]{1,0:T(8,128)(2,1)S(1)}, u32[]{:S(2)}, u32[]{:S(2)}) collective-permute-start(bf16[1168,128]{1,0:T(8,128)(2,1)S(1)} %get-tuple-element.148), channel_id=1, source_target_pairs={{0,24},{8,16},{16,8},{1,25},{9,17},{17,9},{2,26},{10,18},{18,10},{... | collective-permute-start | bytes 897032 | tf_op jit(solution)/shard_map/ppermute | solution.py:1217
  15.1 3.6 %collective-permute-start.6 = (bf16[288,128]{1,0:T(8,128)(2,1)S(1)}, bf16[288,128]{1,0:T(8,128)(2,1)S(1)}, u32[]{:S(2)}, u32[]{:S(2)}) collective-permute-start(bf16[288,128]{1,0:T(8,128)(2,1)S(1)} %rows_kernel.3.refs_0_), channel_id=1, source_target_pairs={{0,6},{1,7},{2,4},{3,5},{4,2},{5,3},{6,0},{7,1},{8,14},{9,15},{10,... | collective-permute-start | bytes 221192 | tf_op jit(solution)/shard_map/ppermute | solution.py:55
  18.7 3.0 %collective-permute-done.6.refs_3_ = bf16[288,128]{1,0:T(8,128)(2,1)S(1)} collective-permute-done((bf16[288,128]{1,0:T(8,128)(2,1)S(1)}, bf16[288,128]{1,0:T(8,128)(2,1)S(1)}, u32[]{:S(2)}, u32[]{:S(2)}) %collective-permute-start.6) | collective-permute-done | bytes 73760 | tf_op jit(solution)/shard_map/ppermute | solution.py:55
  21.7 3.1 %collective-permute-start.4 = (bf16[288,128]{1,0:T(8,128)(2,1)S(1)}, bf16[288,128]{1,0:T(8,128)(2,1)S(1)}, u32[]{:S(2)}, u32[]{:S(2)}) collective-permute-start(bf16[288,128]{1,0:T(8,128)(2,1)S(1)} %rows_kernel.3.refs_0_), channel_id=1, source_target_pairs={{0,2},{1,3},{2,0},{3,1},{4,6},{5,7},{6,4},{7,5},{8,10},{9,11},{10,... | collective-permute-start | bytes 221192 | tf_op jit(solution)/shard_map/ppermute | solution.py:55
  27.9 2.1 collective-permute-start.15
  32.8 2.7 %collective-permute-start.11 = (f32[8,128]{1,0:T(8,128)S(1)}, f32[8,128]{1,0:T(8,128)S(1)}, u32[]{:S(2)}, u32[]{:S(2)}) collective-permute-start(f32[8,128]{1,0:T(8,128)S(1)} %add.82), channel_id=1, source_target_pairs={{0,6},{1,7},{2,4},{3,5},{4,2},{5,3},{6,0},{7,1},{8,14},{9,15},{10,... | collective-permute-start | bytes 12296 | tf_op jit(solution)/shard_map/ppermute | solution.py:55
  40.5 3.4 %collective-permute-start.12 = (bf16[784,128]{1,0:T(8,128)(2,1)S(1)}, bf16[784,128]{1,0:T(8,128)(2,1)S(1)}, u32[]{:S(2)}, u32[]{:S(2)}) collective-permute-start(bf16[784,128]{1,0:T(8,128)(2,1)S(1)} %active_kernel.2.a0.active), channel_id=1, source_target_pairs={{0,8},{8,0},{16,24},{24,16},{1,9},{9,1},{17,25},{25,17},{2,10},{10... | collective-permute-start | bytes 602120 | tf_op jit(solution)/shard_map/ppermute | solution.py:55
  45.5 3.0 %mass_kernel.1 = (bf16[512,3072]{1,0:T(8,128)(2,1)S(1)}, f32[8,3072]{1,0:T(8,128)S(1)}, bf16[2,32,32]{2,1,0:T(8,128)(2,1)S(1)}) custom-call(s32[9]{0:T(128)S(1)} %stack.39.place, bf16[768,512]{1,0:T(8,128)(2,1)S(1)} %get-tuple-element.158.table, bf16[288,128]{1,0:T(8,128)(2,1)S(1)} %rows_kernel.3.refs_0_, ...), custom_call_target="tpu_custom_call" | custom-call | bytes 15000000 | tf_op jit(solution)/shard_map/mass_kernel/pallas_call | solution.py:139
  49.2 2.9 %collective-permute-done.13.a2 = bf16[784,128]{1,0:T(8,128)(2,1)S(1)} collective-permute-done((bf16[784,128]{1,0:T(8,128)(2,1)S(1)}, bf16[784,128]{1,0:T(8,128)(2,1)S(1)}, u32[]{:S(2)}, u32[]{:S(2)}) %collective-permute-start.13) | collective-permute-done | bytes 200736 | tf_op jit(solution)/shard_map/ppermute | solution.py:55
  52.1 2.5 %conv_kernel.1 = (f32[784,128]{1,0:T(8,128)S(1)}, f32[8,128]{1,0:T(8,128)S(1)}) custom-call(s32[9]{0:T(128)S(1)} %stack.39.place, bf16[784,128]{1,0:T(8,128)(2,1)S(1)} %active_kernel.2.a0.active, bf16[784,128]{1,0:T(8,128)(2,1)S(1)} %collective-permute-done.12.a1, bf16[784,128]{1,0:T(8,128)(2,1)S(1)} %collective-permute-done.13.a2, ...), custom_call_target="tpu_custom_call" | custom-call | bytes 9000000 | tf_op jit(solution)/shard_map/conv_kernel/pallas_call | solution.py:139
  58.0 2.2 collective-permute-start.18
  68.2 3.7 %unpack.1.w_head = bf16[2048,2048]{1,0:T(8,128)(2,1)S(1)} custom-call(bf16[9456,512]{1,0:T(8,128)(2,1)S(1)} %bitcast.28), custom_call_target="tpu_custom_call" | custom-call | bytes 12000000 | tf_op jit(solution)/shard_map/unpack/pallas_call | solution.py:1054
  88.4 2.2 collective-permute-done.28.refs_0_
  101.9 10.8 %head_kernel.1 = (bf16[128,2048]{1,0:T(8,128)(2,1)S(1)}, bf16[128,2048]{1,0:T(8,128)(2,1)S(1)}, bf16[128,128]{1,0:T(8,128)(2,1)S(1)}, bf16[64,3072]{1,0:T(8,128)...) custom-call(s32[9]{0:T(128)S(1)} %stack.39.place, ...), custom_call_target="tpu_custom_call" | custom-call | bytes 36000000 | tf_op jit(solution)/shard_map/head_kernel/pallas_call | solution.py:139
  114.1 4.6 %head_back_kernel.1 = (bf16[16,512]{1,0:T(8,128)(2,1)S(1)}, bf16[16,512]{1,0:T(8,128)(2,1)S(1)}, bf16[16,512]{1,0:T(8,128)(2,1)S(1)}, bf16[16,512]{1,0:T(8,128)(...) custom-call(s32[9]{0:T(128)S(1)} %stack.39.place, ...), custom_call_target="tpu_custom_call" | custom-call | bytes 15000000 | tf_op jit(solution)/shard_map/head_back_kernel/pallas_call | solution.py:139
  123.4 2.3 %collective-permute-done.41.r2 = bf16[16,512]{1,0:T(8,128)(2,1)S(1)} collective-permute-done((bf16[16,512]{1,0:T(8,128)(2,1)S(1)}, bf16[16,512]{1,0:T(8,128)(2,1)S(1)}, u32[]{:S(2)}, u32[]{:S(2)}) %collective-permute-start.41) | collective-permute-done | bytes 16416 | tf_op jit(solution)/shard_map/ppermute | solution.py:55
  128.8 2.2 collective-permute-start.45
  144.5 2.4 %head_grads_kernel.1.base = f32[64,9456]{1,0:T(8,128)} custom-call(s32[9]{0:T(128)S(1)} %stack.39.place, bf16[128,2048]{1,0:T(8,128)(2,1)S(1)} %get-tuple-element.216.pooled, bf16[128,2048]{1,0:T(8,128)(2,1)S(1)} %get-tuple-element.217.active, bf16[128,128]{1,0:T(8,128)(2,1)S(1)} %get-tuple-element.218.unit, bf16[64,3072]{1,0:T(8,128)(2,1)S(1)} %get-tuple-element.219.d_here, ...), custom_call_target="tpu_custom_call" | custom-call | bytes 18000000 | tf_op jit(solution)/shard_map/head_grads_kernel/pallas_call | solution.py:139
  147.0 3.4 %collective-permute-done.48.q3 = bf16[784,128]{1,0:T(8,128)(2,1)S(1)} collective-permute-done((bf16[784,128]{1,0:T(8,128)(2,1)S(1)}, bf16[784,128]{1,0:T(8,128)(2,1)S(1)}, u32[]{:S(2)}, u32[]{:S(2)}) %collective-permute-start.48) | collective-permute-done | bytes 200736 | tf_op jit(solution)/shard_map/ppermute | solution.py:55
  162.6 2.1 collective-permute-start.59
  164.7 3.1 %collective-permute-done.59.came = bf16[64,512]{1,0:T(8,128)(2,1)S(1)} collective-permute-done((bf16[64,512]{1,0:T(8,128)(2,1)S(1)}, bf16[64,512]{1,0:T(8,128)(2,1)S(1)}, u32[]{:S(2)}, u32[]{:S(2)}) %collective-permute-start.59) | collective-permute-done | bytes 65568 | tf_op jit(solution)/shard_map/ppermute | solution.py:55
  170.6 2.9 %conv_back_kernel.1 = (bf16[784,512]{1,0:T(8,128)(2,1)S(1)}, f32[784,128]{1,0:T(8,128)S(1)}, f32[8,128]{1,0:T(8,128)S(1)}) custom-call(s32[9]{0:T(128)S(1)} %stack.39.place, bf16[784,128]{1,0:T(8,128)(2,1)S(1)} %norm_back_kernel.1.d0, bf16[784,128]{1,0:T(8,128)(2,1)S(1)} %collective-permute-done.56.d1, bf16[784,128]{1,0:T(8,128)(2,1)S(1)} %collective-permute-done.57.d2, ...), custom_call_target="tpu_custom_call" | custom-call | bytes 10500000 | tf_op jit(solution)/shard_map/conv_back_kernel/pallas_call | solution.py:139
  181.8 2.2 pair_kernel.3
  190.0 3.1 %collective-permute-done.67.n3.d3 = bf16[832,128]{1,0:T(8,128)(2,1)S(1)} collective-permute-done((bf16[832,128]{1,0:T(8,128)(2,1)S(1)}, bf16[832,128]{1,0:T(8,128)(2,1)S(1)}, u32[]{:S(2)}, u32[]{:S(2)}) %collective-permute-start.67) | collective-permute-done | bytes 213024 | tf_op jit(solution)/shard_map/ppermute | solution.py:55
  193.2 3.6 %collective-permute-done.66.n2.d2 = bf16[832,128]{1,0:T(8,128)(2,1)S(1)} collective-permute-done((bf16[832,128]{1,0:T(8,128)(2,1)S(1)}, bf16[832,128]{1,0:T(8,128)(2,1)S(1)}, u32[]{:S(2)}, u32[]{:S(2)}) %collective-permute-start.66) | collective-permute-done | bytes 213024 | tf_op jit(solution)/shard_map/ppermute | solution.py:55
  198.5 2.1 collective-permute-start.74
  206.3 2.5 %reduce_back_kernel.1 = f32[196,4,512]{2,1,0:T(4,128)} custom-call(s32[9]{0:T(128)S(1)} %stack.39.place, bf16[784,512]{1,0:T(8,128)(2,1)S(1)} %get-tuple-element.266.d_full, bf16[4,832,128]{2,1,0:T(8,128)(2,1)S(1)} %stack_kernel.1.back0, bf16[4,832,128]{2,1,0:T(8,128)(2,1)S(1)} %collective-permute-done.60.back1, f32[784,512]{1,0:T(8,128)S(1)} %get-tuple-element.207.d_z), custom_call_target="tpu_custom_call" | custom-call | bytes 6000000 | tf_op jit(solution)/shard_map/reduce_back_kernel/pallas_call | solution.py:139
  208.7 3.3 %collective-permute-done.74.came = bf16[64,1152]{1,0:T(8,128)(2,1)S(1)} collective-permute-done((bf16[64,1152]{1,0:T(8,128)(2,1)S(1)}, bf16[64,1152]{1,0:T(8,128)(2,1)S(1)}, u32[]{:S(2)}, u32[]{:S(2)}) %collective-permute-start.74) | collective-permute-done | bytes 147488 | tf_op jit(solution)/shard_map/ppermute | solution.py:55
  214.1 3.1 %collective-permute-start.75 = (bf16[64,1152]{1,0:T(8,128)(2,1)S(1)}, bf16[64,1152]{1,0:T(8,128)(2,1)S(1)}, u32[]{:S(2)}, u32[]{:S(2)}) collective-permute-start(bf16[64,1152]{1,0:T(8,128)(2,1)S(1)} %get-tuple-element.282), channel_id=1, source_target_pairs={{8,0},{0,8},{24,16},{9,1},{1,9},{25,17},{10,2},{2,10},{26,18},{11,... | collective-permute-start | bytes 442376 | tf_op jit(solution)/shard_map/ppermute | solution.py:1516
  218.5 4.9 %collective-permute-start.77 = (bf16[64,1152]{1,0:T(8,128)(2,1)S(1)}, bf16[64,1152]{1,0:T(8,128)(2,1)S(1)}, u32[]{:S(2)}, u32[]{:S(2)}) collective-permute-start(bf16[64,1152]{1,0:T(8,128)(2,1)S(1)} %get-tuple-element.284), channel_id=1, source_target_pairs={{24,0},{16,8},{8,16},{25,1},{17,9},{9,17},{26,2},{18,10},{10,18},{... | collective-permute-start | bytes 442376 | tf_op jit(solution)/shard_map/ppermute | solution.py:1516
  224.5 2.9 %collective-permute-done.76.m2 = bf16[64,1152]{1,0:T(8,128)(2,1)S(1)} collective-permute-done((bf16[64,1152]{1,0:T(8,128)(2,1)S(1)}, bf16[64,1152]{1,0:T(8,128)(2,1)S(1)}, u32[]{:S(2)}, u32[]{:S(2)}) %collective-permute-start.76) | collective-permute-done | bytes 147488 | tf_op jit(solution)/shard_map/ppermute | solution.py:1516
  (197 shorter events, 123.8 us)
Async XLA Ops:
  3.9 23.2 %collective-permute-start = (bf16[1168,128]{1,0:T(8,128)(2,1)S(1)}, bf16[1168,128]{1,0:T(8,128)(2,1)S(1)}, u32[]{:S(2)}, u32[]{:S(2)}) collective-permute-start(bf16[1168,128]{1,0:T(8,128)(2,1)S(1)} %get-tuple-element.146), channel_id=1, source_target_pairs={{0,8},{8,0},{16,24},{1,9},{9,1},{17,25},{2,10},{10,2},{18,26},{3,1... | collective-permute-start | bytes 897032 | tf_op jit(solution)/shard_map/ppermute | solution.py:1217
  5.9 21.3 %collective-permute-start.1 = (bf16[1168,128]{1,0:T(8,128)(2,1)S(1)}, bf16[1168,128]{1,0:T(8,128)(2,1)S(1)}, u32[]{:S(2)}, u32[]{:S(2)}) collective-permute-start(bf16[1168,128]{1,0:T(8,128)(2,1)S(1)} %get-tuple-element.147), channel_id=1, source_target_pairs={{0,16},{8,24},{16,0},{1,17},{9,25},{17,1},{2,18},{10,26},{18,2},{3... | collective-permute-start | bytes 897032 | tf_op jit(solution)/shard_map/ppermute | solution.py:1217
  7.3 19.8 %collective-permute-start.2 = (bf16[1168,128]{1,0:T(8,128)(2,1)S(1)}, bf16[1168,128]{1,0:T(8,128)(2,1)S(1)}, u32[]{:S(2)}, u32[]{:S(2)}) collective-permute-start(bf16[1168,128]{1,0:T(8,128)(2,1)S(1)} %get-tuple-element.148), channel_id=1, source_target_pairs={{0,24},{8,16},{16,8},{1,25},{9,17},{17,9},{2,26},{10,18},{18,10},{... | collective-permute-start | bytes 897032 | tf_op jit(solution)/shard_map/ppermute | solution.py:1217
  27.9 12.3 %collective-permute-start.15 = (bf16[1168,128]{1,0:T(8,128)(2,1)S(1)}, bf16[1168,128]{1,0:T(8,128)(2,1)S(1)}, u32[]{:S(2)}, u32[]{:S(2)}) collective-permute-start(bf16[1168,128]{1,0:T(8,128)(2,1)S(1)} %get-tuple-element.165.refs_0_), channel_id=1, source_target_pairs={{0,2},{1,3},{2,0},{3,1},{4,6},{5,7},{6,4},{7,5},{8,10},{9,11},{10,... | collective-permute-start | bytes 897032 | tf_op jit(solution)/shard_map/ppermute | solution.py:55
  40.3 11.8 %collective-permute-start.16 = (bf16[2336,128]{1,0:T(8,128)(2,1)S(1)}, bf16[2336,128]{1,0:T(8,128)(2,1)S(1)}, u32[]{:S(2)}, u32[]{:S(2)}) collective-permute-start(bf16[2336,128]{1,0:T(8,128)(2,1)S(1)} %rows_kernel.4.wa.told.conv_a), channel_id=1, source_target_pairs={{0,1},{1,0},{2,3},{3,2},{4,5},{5,4},{6,7},{7,6},{8,9},{9,8},{10,11... | collective-permute-start | bytes 1794056 | tf_op jit(solution)/shard_map/ppermute | solution.py:55
  40.4 8.8 %collective-permute-start.14 = (bf16[784,128]{1,0:T(8,128)(2,1)S(1)}, bf16[784,128]{1,0:T(8,128)(2,1)S(1)}, u32[]{:S(2)}, u32[]{:S(2)}) collective-permute-start(bf16[784,128]{1,0:T(8,128)(2,1)S(1)} %active_kernel.2.a0.active), channel_id=1, source_target_pairs={{0,24},{8,16},{16,8},{24,0},{1,25},{9,17},{17,9},{25,1},{2,26},{10... | collective-permute-start | bytes 602120 | tf_op jit(solution)/shard_map/ppermute | solution.py:55
  40.4 11.6 %collective-permute-start.13 = (bf16[784,128]{1,0:T(8,128)(2,1)S(1)}, bf16[784,128]{1,0:T(8,128)(2,1)S(1)}, u32[]{:S(2)}, u32[]{:S(2)}) collective-permute-start(bf16[784,128]{1,0:T(8,128)(2,1)S(1)} %active_kernel.2.a0.active), channel_id=1, source_target_pairs={{0,16},{8,24},{16,0},{24,8},{1,17},{9,25},{17,1},{25,9},{2,18},{10... | collective-permute-start | bytes 602120 | tf_op jit(solution)/shard_map/ppermute | solution.py:55
  40.5 11.5 %collective-permute-start.12 = (bf16[784,128]{1,0:T(8,128)(2,1)S(1)}, bf16[784,128]{1,0:T(8,128)(2,1)S(1)}, u32[]{:S(2)}, u32[]{:S(2)}) collective-permute-start(bf16[784,128]{1,0:T(8,128)(2,1)S(1)} %active_kernel.2.a0.active), channel_id=1, source_target_pairs={{0,8},{8,0},{16,24},{24,16},{1,9},{9,1},{17,25},{25,17},{2,10},{10... | collective-permute-start | bytes 602120 | tf_op jit(solution)/shard_map/ppermute | solution.py:55
  62.0 9.8 %collective-permute-start.23 = (bf16[784,128]{1,0:T(8,128)(2,1)S(1)}, bf16[784,128]{1,0:T(8,128)(2,1)S(1)}, u32[]{:S(2)}, u32[]{:S(2)}) collective-permute-start(bf16[784,128]{1,0:T(8,128)(2,1)S(1)} %active_kernel.3.a0), channel_id=1, source_target_pairs={{0,24},{8,16},{16,8},{24,0},{1,25},{9,17},{17,9},{25,1},{2,26},{10... | collective-permute-start | bytes 602120 | tf_op jit(solution)/shard_map/ppermute | solution.py:55
  63.3 9.9 %collective-permute-start.22 = (bf16[784,128]{1,0:T(8,128)(2,1)S(1)}, bf16[784,128]{1,0:T(8,128)(2,1)S(1)}, u32[]{:S(2)}, u32[]{:S(2)}) collective-permute-start(bf16[784,128]{1,0:T(8,128)(2,1)S(1)} %active_kernel.3.a0), channel_id=1, source_target_pairs={{0,16},{8,24},{16,0},{24,8},{1,17},{9,25},{17,1},{25,9},{2,18},{10... | collective-permute-start | bytes 602120 | tf_op jit(solution)/shard_map/ppermute | solution.py:55
  63.9 9.4 %collective-permute-start.21 = (bf16[784,128]{1,0:T(8,128)(2,1)S(1)}, bf16[784,128]{1,0:T(8,128)(2,1)S(1)}, u32[]{:S(2)}, u32[]{:S(2)}) collective-permute-start(bf16[784,128]{1,0:T(8,128)(2,1)S(1)} %active_kernel.3.a0), channel_id=1, source_target_pairs={{0,8},{8,0},{16,24},{24,16},{1,9},{9,1},{17,25},{25,17},{2,10},{10... | collective-permute-start | bytes 602120 | tf_op jit(solution)/shard_map/ppermute | solution.py:55
  98.4 20.2 %collective-permute-start.36 = (bf16[832,128]{1,0:T(8,128)(2,1)S(1)}, bf16[832,128]{1,0:T(8,128)(2,1)S(1)}, u32[]{:S(2)}, u32[]{:S(2)}) collective-permute-start(bf16[832,128]{1,0:T(8,128)(2,1)S(1)} %get-tuple-element.200), channel_id=1, source_target_pairs={{0,8},{8,0},{16,24},{24,16},{1,9},{9,1},{17,25},{25,17},{2,10},{10... | collective-permute-start | bytes 638984 | tf_op jit(solution)/shard_map/ppermute | solution.py:55
  99.4 19.3 %collective-permute-start.37 = (bf16[832,128]{1,0:T(8,128)(2,1)S(1)}, bf16[832,128]{1,0:T(8,128)(2,1)S(1)}, u32[]{:S(2)}, u32[]{:S(2)}) collective-permute-start(bf16[832,128]{1,0:T(8,128)(2,1)S(1)} %get-tuple-element.201), channel_id=1, source_target_pairs={{0,16},{8,24},{16,0},{24,8},{1,17},{9,25},{17,1},{25,9},{2,18},{10... | collective-permute-start | bytes 638984 | tf_op jit(solution)/shard_map/ppermute | solution.py:55
  100.8 17.9 %collective-permute-start.38 = (bf16[832,128]{1,0:T(8,128)(2,1)S(1)}, bf16[832,128]{1,0:T(8,128)(2,1)S(1)}, u32[]{:S(2)}, u32[]{:S(2)}) collective-permute-start(bf16[832,128]{1,0:T(8,128)(2,1)S(1)} %get-tuple-element.202), channel_id=1, source_target_pairs={{0,24},{8,16},{16,8},{24,0},{1,25},{9,17},{17,9},{25,1},{2,26},{10... | collective-permute-start | bytes 638984 | tf_op jit(solution)/shard_map/ppermute | solution.py:55
  133.1 10.0 %collective-permute-start.49 = (bf16[64,3072]{1,0:T(8,128)(2,1)S(1)}, bf16[64,3072]{1,0:T(8,128)(2,1)S(1)}, u32[]{:S(2)}, u32[]{:S(2)}) collective-permute-start(bf16[64,3072]{1,0:T(8,128)(2,1)S(1)} %get-tuple-element.219.d_here), channel_id=1, source_target_pairs={{0,1},{1,0},{2,3},{3,2},{4,5},{5,4},{6,7},{7,6},{8,9},{9,8},{10,11... | collective-permute-start | bytes 1179656 | tf_op jit(solution)/shard_map/ppermute | solution.py:55
  138.5 32.1 %collective-permute-start.60 = (bf16[4,832,128]{2,1,0:T(8,128)(2,1)S(1)}, bf16[4,832,128]{2,1,0:T(8,128)(2,1)S(1)}, u32[]{:S(2)}, u32[]{:S(2)}) collective-permute-start(bf16[4,832,128]{2,1,0:T(8,128)(2,1)S(1)} %stack_kernel.1.back0), channel_id=1, source_target_pairs={{0,1},{1,0},{2,3},{3,2},{4,5},{5,4},{6,7},{7,6},{8,9},{9,8},{10,11... | collective-permute-start | bytes 2555912 | tf_op jit(solution)/shard_map/ppermute | solution.py:55
  139.1 7.8 %collective-permute-start.46 = (bf16[784,128]{1,0:T(8,128)(2,1)S(1)}, bf16[784,128]{1,0:T(8,128)(2,1)S(1)}, u32[]{:S(2)}, u32[]{:S(2)}) collective-permute-start(bf16[784,128]{1,0:T(8,128)(2,1)S(1)} %get-tuple-element.211), channel_id=1, source_target_pairs={{0,8},{8,0},{16,24},{24,16},{1,9},{9,1},{17,25},{25,17},{2,10},{10... | collective-permute-start | bytes 602120 | tf_op jit(solution)/shard_map/ppermute | solution.py:55
  140.7 9.7 %collective-permute-start.48 = (bf16[784,128]{1,0:T(8,128)(2,1)S(1)}, bf16[784,128]{1,0:T(8,128)(2,1)S(1)}, u32[]{:S(2)}, u32[]{:S(2)}) collective-permute-start(bf16[784,128]{1,0:T(8,128)(2,1)S(1)} %get-tuple-element.213), channel_id=1, source_target_pairs={{0,24},{8,16},{16,8},{24,0},{1,25},{9,17},{17,9},{25,1},{2,26},{10... | collective-permute-start | bytes 602120 | tf_op jit(solution)/shard_map/ppermute | solution.py:55
  158.5 9.3 %collective-permute-start.58 = (bf16[784,128]{1,0:T(8,128)(2,1)S(1)}, bf16[784,128]{1,0:T(8,128)(2,1)S(1)}, u32[]{:S(2)}, u32[]{:S(2)}) collective-permute-start(bf16[784,128]{1,0:T(8,128)(2,1)S(1)} %norm_back_kernel.1.d0), channel_id=1, source_target_pairs={{0,24},{8,16},{16,8},{24,0},{1,25},{9,17},{17,9},{25,1},{2,26},{10... | collective-permute-start | bytes 602120 | tf_op jit(solution)/shard_map/ppermute | solution.py:55
  160.3 9.2 %collective-permute-start.57 = (bf16[784,128]{1,0:T(8,128)(2,1)S(1)}, bf16[784,128]{1,0:T(8,128)(2,1)S(1)}, u32[]{:S(2)}, u32[]{:S(2)}) collective-permute-start(bf16[784,128]{1,0:T(8,128)(2,1)S(1)} %norm_back_kernel.1.d0), channel_id=1, source_target_pairs={{0,16},{8,24},{16,0},{24,8},{1,17},{9,25},{17,1},{25,9},{2,18},{10... | collective-permute-start | bytes 602120 | tf_op jit(solution)/shard_map/ppermute | solution.py:55
  161.7 8.9 %collective-permute-start.56 = (bf16[784,128]{1,0:T(8,128)(2,1)S(1)}, bf16[784,128]{1,0:T(8,128)(2,1)S(1)}, u32[]{:S(2)}, u32[]{:S(2)}) collective-permute-start(bf16[784,128]{1,0:T(8,128)(2,1)S(1)} %norm_back_kernel.1.d0), channel_id=1, source_target_pairs={{0,8},{8,0},{16,24},{24,16},{1,9},{9,1},{17,25},{25,17},{2,10},{10... | collective-permute-start | bytes 602120 | tf_op jit(solution)/shard_map/ppermute | solution.py:55
  184.1 9.1 %collective-permute-start.67 = (bf16[832,128]{1,0:T(8,128)(2,1)S(1)}, bf16[832,128]{1,0:T(8,128)(2,1)S(1)}, u32[]{:S(2)}, u32[]{:S(2)}) collective-permute-start(bf16[832,128]{1,0:T(8,128)(2,1)S(1)} %last_norm_back_kernel.1.n0.d0), channel_id=1, source_target_pairs={{0,24},{8,16},{16,8},{24,0},{1,25},{9,17},{17,9},{25,1},{2,26},{10... | collective-permute-start | bytes 638984 | tf_op jit(solution)/shard_map/ppermute | solution.py:55
  184.9 11.9 %collective-permute-start.66 = (bf16[832,128]{1,0:T(8,128)(2,1)S(1)}, bf16[832,128]{1,0:T(8,128)(2,1)S(1)}, u32[]{:S(2)}, u32[]{:S(2)}) collective-permute-start(bf16[832,128]{1,0:T(8,128)(2,1)S(1)} %last_norm_back_kernel.1.n0.d0), channel_id=1, source_target_pairs={{0,16},{8,24},{16,0},{24,8},{1,17},{9,25},{17,1},{25,9},{2,18},{10... | collective-permute-start | bytes 638984 | tf_op jit(solution)/shard_map/ppermute | solution.py:55
  186.3 10.5 %collective-permute-start.65 = (bf16[832,128]{1,0:T(8,128)(2,1)S(1)}, bf16[832,128]{1,0:T(8,128)(2,1)S(1)}, u32[]{:S(2)}, u32[]{:S(2)}) collective-permute-start(bf16[832,128]{1,0:T(8,128)(2,1)S(1)} %last_norm_back_kernel.1.n0.d0), channel_id=1, source_target_pairs={{0,8},{8,0},{16,24},{24,16},{1,9},{9,1},{17,25},{25,17},{2,10},{10... | collective-permute-start | bytes 638984 | tf_op jit(solution)/shard_map/ppermute | solution.py:55
  188.3 10.1 %collective-permute-start.73 = (bf16[2,64,1152]{2,1,0:T(8,128)(2,1)S(1)}, bf16[2,64,1152]{2,1,0:T(8,128)(2,1)S(1)}, u32[]{:S(2)}, u32[]{:S(2)}) collective-permute-start(bf16[2,64,1152]{2,1,0:T(8,128)(2,1)S(1)} %get-tuple-element.269), channel_id=1, source_target_pairs={{0,2},{1,3},{2,0},{3,1},{4,6},{5,7},{6,4},{7,5},{8,10},{9,11},{10,... | collective-permute-start | bytes 884744 | tf_op jit(solution)/shard_map/ppermute | solution.py:55
  198.5 13.6 %collective-permute-start.74 = (bf16[64,1152]{1,0:T(8,128)(2,1)S(1)}, bf16[64,1152]{1,0:T(8,128)(2,1)S(1)}, u32[]{:S(2)}, u32[]{:S(2)}) collective-permute-start(bf16[64,1152]{1,0:T(8,128)(2,1)S(1)} %get-tuple-element.271), channel_id=1, source_target_pairs={{0,4},{1,5},{2,6},{3,7},{4,0},{5,1},{6,2},{7,3},{8,12},{9,13},{10,... | collective-permute-start | bytes 442376 | tf_op jit(solution)/shard_map/ppermute | solution.py:55
  201.2 10.9 %collective-permute-start.70 = (bf16[64,512]{1,0:T(8,128)(2,1)S(1)}, bf16[64,512]{1,0:T(8,128)(2,1)S(1)}, u32[]{:S(2)}, u32[]{:S(2)}) collective-permute-start(bf16[64,512]{1,0:T(8,128)(2,1)S(1)} %get-tuple-element.263), channel_id=1, source_target_pairs={{0,2},{1,3},{2,0},{3,1},{4,6},{5,7},{6,4},{7,5},{8,10},{9,11},{10,... | collective-permute-start | bytes 196616 | tf_op jit(solution)/shard_map/ppermute | solution.py:55
  202.1 11.4 %collective-permute-start.71 = (bf16[64,512]{1,0:T(8,128)(2,1)S(1)}, bf16[64,512]{1,0:T(8,128)(2,1)S(1)}, u32[]{:S(2)}, u32[]{:S(2)}) collective-permute-start(bf16[64,512]{1,0:T(8,128)(2,1)S(1)} %get-tuple-element.264), channel_id=1, source_target_pairs={{0,4},{1,5},{2,6},{3,7},{4,0},{5,1},{6,2},{7,3},{8,12},{9,13},{10,... | collective-permute-start | bytes 196616 | tf_op jit(solution)/shard_map/ppermute | solution.py:55
  203.6 9.8 %collective-permute-start.72 = (bf16[64,512]{1,0:T(8,128)(2,1)S(1)}, bf16[64,512]{1,0:T(8,128)(2,1)S(1)}, u32[]{:S(2)}, u32[]{:S(2)}) collective-permute-start(bf16[64,512]{1,0:T(8,128)(2,1)S(1)} %get-tuple-element.265), channel_id=1, source_target_pairs={{0,6},{1,7},{2,4},{3,5},{4,2},{5,3},{6,0},{7,1},{8,14},{9,15},{10,... | collective-permute-start | bytes 196616 | tf_op jit(solution)/shard_map/ppermute | solution.py:55
  214.1 10.4 %collective-permute-start.75 = (bf16[64,1152]{1,0:T(8,128)(2,1)S(1)}, bf16[64,1152]{1,0:T(8,128)(2,1)S(1)}, u32[]{:S(2)}, u32[]{:S(2)}) collective-permute-start(bf16[64,1152]{1,0:T(8,128)(2,1)S(1)} %get-tuple-element.282), channel_id=1, source_target_pairs={{8,0},{0,8},{24,16},{9,1},{1,9},{25,17},{10,2},{2,10},{26,18},{11,... | collective-permute-start | bytes 442376 | tf_op jit(solution)/shard_map/ppermute | solution.py:1516
  217.2 10.2 %collective-permute-start.76 = (bf16[64,1152]{1,0:T(8,128)(2,1)S(1)}, bf16[64,1152]{1,0:T(8,128)(2,1)S(1)}, u32[]{:S(2)}, u32[]{:S(2)}) collective-permute-start(bf16[64,1152]{1,0:T(8,128)(2,1)S(1)} %get-tuple-element.283), channel_id=1, source_target_pairs={{16,0},{24,8},{0,16},{17,1},{25,9},{1,17},{18,2},{26,10},{2,18},{1... | collective-permute-start | bytes 442376 | tf_op jit(solution)/shard_map/ppermute | solution.py:1516
  218.5 8.9 %collective-permute-start.77 = (bf16[64,1152]{1,0:T(8,128)(2,1)S(1)}, bf16[64,1152]{1,0:T(8,128)(2,1)S(1)}, u32[]{:S(2)}, u32[]{:S(2)}) collective-permute-start(bf16[64,1152]{1,0:T(8,128)(2,1)S(1)} %get-tuple-element.284), channel_id=1, source_target_pairs={{24,0},{16,8},{8,16},{25,1},{17,9},{9,17},{26,2},{18,10},{10,18},{... | collective-permute-start | bytes 442376 | tf_op jit(solution)/shard_map/ppermute | solution.py:1516
  (52 other events, 323.8 us)

commit v2 on v1

--- a/solution.py
+++ b/solution.py
@@ -109,7 +109,7 @@
 
 
 def sigmoid(v):
-    return 1.0 / (1.0 + jnp.exp(-v))
+    return 0.5 * jnp.tanh(0.5 * v) + 0.5
 
 
 def slope(v):
@@ -219,25 +219,26 @@
     return jnp.concatenate(parts, axis=0)
 
 
-def tap_valid(rows, images, tap, sign):
+def map_places(rows, images):
     row = lax.broadcasted_iota(jnp.int32, (rows, PART), 0).astype(F32)
     cell = jnp.floor((row + 0.5) * (1.0 / images))
     crop = jnp.floor((cell + 0.5) * (1.0 / PLACES))
     place = cell - crop * PLACES
     y = jnp.floor((place + 0.5) * (1.0 / SIDE))
-    x = place - y * SIDE
-    y = y + float(sign * (tap // 3 - 1))
-    x = x + float(sign * (tap % 3 - 1))
-    return (y > -0.5) & (y < SIDE - 0.5) & (x > -0.5) & (x < SIDE - 0.5)
-
-
-def tap_shift(value, images, tap, sign):
+    return y, place - y * SIDE
+
+
+def tap_shift(value, images, tap, sign, y, x):
     rows = value.shape[0]
-    offset = sign * images * (SIDE * (tap // 3 - 1) + (tap % 3 - 1))
+    down, right = sign * (tap // 3 - 1), sign * (tap % 3 - 1)
+    offset = images * (SIDE * down + right)
     moved = value if offset == 0 else pltpu.roll(value, (-offset) % rows, 0)
-    if tap == 4:
-        return moved
-    return jnp.where(tap_valid(rows, images, tap, sign), moved, 0.0)
+    for step, at in ((down, y), (right, x)):
+        if step < 0:
+            moved = jnp.where(at > 0.5, moved, 0.0)
+        elif step > 0:
+            moved = jnp.where(at < SIDE - 1.5, moved, 0.0)
+    return moved
 
 
 def told_norm(message, at=0):
@@ -259,9 +260,11 @@
     return out
 
 
-def tell_norm(rows):
-    out = terms(rows[0:1]) + terms(rows[1:2])
-    out.append(jnp.zeros((10, rows.shape[1]), F32))
+def tell_norm(norm, lane):
+    out = []
+    for r in range(2):
+        out += terms(norm[r, :, lane : lane + PART])
+    out.append(jnp.zeros((10, PART), F32))
     return jnp.concatenate(out, axis=0).astype(BF16)
 
 
@@ -304,11 +307,12 @@
             first = (j % 2) * QUARTER_CONV + 16 + tap * quarter
             weight[pl.ds(at, quarter), lanes] = w[first : first + quarter, :]
     total = None
+    y, x = map_places(full.shape[0], images)
     for first in range(0, 9, 2):
         taps = [tap for tap in (first, first + 1) if tap < 9]
         part = dot(full[...], weight[:, first * PART : (taps[-1] + 1) * PART])
         for j, tap in enumerate(taps):
-            moved = tap_shift(part[:, j * PART : (j + 1) * PART], images, tap, 1)
+            moved = tap_shift(part[:, j * PART : (j + 1) * PART], images, tap, 1, y, x)
             total = moved if total is None else total + moved
     pre[...] = total
     parts = per_micro(total, micro)
@@ -450,11 +454,12 @@
                 rows = pl.ds(pl.multiple_of(tap * PART + place[4 + j] * half, half), half)
                 weight[rows, lanes] = back[k, tap * half : (tap + 1) * half, :]
     total = None
+    y, x = map_places(d_low.shape[0], images)
     for first in range(0, 9, 2):
         taps = [tap for tap in (first, first + 1) if tap < 9]
         part = dot_nt(d_low, weight[first * PART : (taps[-1] + 1) * PART, :])
         for j, tap in enumerate(taps):
-            moved = tap_shift(part[:, j * PART : (j + 1) * PART], images, tap, -1)
+            moved = tap_shift(part[:, j * PART : (j + 1) * PART], images, tap, -1, y, x)
             total = moved if total is None else total + moved
     d_active = total.astype(BF16).astype(F32)
     finish_silu(micro, count, d_active, pre, sums, told_norm(told), d_y, sums_out)
@@ -531,7 +536,8 @@
 
     @pl.when(t == SECTIONS - 1)
     def _():
-        out[...] = notes[:3, :]
+        for r in range(3):
+            out[r] = notes[r : r + 1, :]
 
     total = None
     for k, note in enumerate((n0, n1, n2, n3)):
@@ -548,7 +554,7 @@
             for r in range(2):
                 for b in range(4):
                     lanes = pl.ds(pl.multiple_of(u * WIDE + b * PART, PART), PART)
-                    out[r : r + 1, lanes] = said(4 * r + b)
+                    out[r, :, lanes] = said(4 * r + b)
 
         for section in range(2):
 
@@ -556,7 +562,7 @@
             def _():
                 for r in range(2):
                     lanes = pl.ds(pl.multiple_of(u * PART, PART), PART)
-                    out[r : r + 1, lanes] = said((10, 8)[section] + r)
+                    out[r, :, lanes] = said((10, 8)[section] + r)
 
     loss[...] = jnp.broadcast_to(total, loss.shape)
 
@@ -579,8 +585,9 @@
 
 def taps_kernel(images, active, out):
     value = active[...].astype(F32)
+    y, x = map_places(value.shape[0], images)
     for tap in range(9):
-        out[:, tap * PART : (tap + 1) * PART] = tap_shift(value, images, tap, 1).astype(BF16)
+        out[:, tap * PART : (tap + 1) * PART] = tap_shift(value, images, tap, 1, y, x).astype(BF16)
 
 
 def head(pooled, w_head, w_proj, protos, norm, queue, match, micro, images, dp):
@@ -782,7 +789,7 @@
     def forward(b, carry):
         lanes = lanes_at(b, chunk)
         pre = by_micro_rows(dot(low, w_head[:, lanes]), ndp, micro)
-        gain, shift = norm[0:1, lanes], norm[1:2, lanes]
+        gain, shift = norm[0, :, lanes], norm[1, :, lanes]
         xhats, ys = [], []
         for m in range(micro):
             v = pre[:, m]
@@ -800,7 +807,7 @@
         return carry
 
     lax.fori_loop(0, chunks, forward, 0)
-    value = dot(active[...], w_proj[...]) + norm[2:3, :PROJ]
+    value = dot(active[...], w_proj[...]) + norm[2, :, :PROJ]
     embed[...] = value
     recip = lax.rsqrt(jnp.sum(value * value, axis=1, keepdims=True) + UNIT_EPS)
     unit_v = dot(regroup(rows, own, images, True), (value * recip).astype(BF16)).astype(BF16)
@@ -912,7 +919,7 @@
         lanes = lanes_at(b, chunk)
         d_y = by_micro_rows(dot_nt(d_low, w_proj[lanes, :]) * slope(y_s[:, lanes]), ndp, micro)
         xhat = by_micro_rows(xhat_s[:, lanes], ndp, micro)
-        gain = norm[0:1, lanes]
+        gain = norm[0, :, lanes]
         values, by_xs, plains = [], None, None
         for m in range(micro):
             by_x = total_of(d_y[:, m] * xhat[:, m])
@@ -950,41 +957,14 @@
     return (row == lane + place[7] * own).astype(F32).astype(BF16)
 
 
-def head_grads_kernel(place, pooled, active, unit, d_here, d_there, d_embed, d_pre, out, parts):
-    @pl.when(place[0] != SECTIONS - 1)
-    def _():
-        out[...] = jnp.zeros_like(out)
-
+def tail_grads_kernel(place, active, unit, d_here, d_there, d_embed, out):
     @pl.when(place[0] == SECTIONS - 1)
     def _():
         own = out.shape[0]
         choose = own_columns(place, own)
-        weave = interleave(PART)
-        own_d = [dot(d_pre[:, q * WIDTH : (q + 1) * WIDTH], choose).astype(BF16) for q in range(4)]
-        own_d = jnp.concatenate(own_d, axis=1)
-
-        def product(b, carry):
-            parts[:, lanes_at(b, WIDTH)] = dot_tn(own_d, pooled[:, lanes_at(b, WIDTH)]).astype(BF16)
-            return carry
-
-        lax.fori_loop(0, 4, product, 0)
-
-        def mix(b, carry):
-            mixed = []
-            for j in range(4):
-                lanes = pl.ds(pl.multiple_of(b * WIDTH + j * PART, PART), PART)
-                four = [parts[q * own : (q + 1) * own, lanes] for q in range(4)]
-                mixed.append(jnp.concatenate(four, axis=1))
-            mixed = dot(jnp.concatenate(mixed, axis=0), weave)
-            for j in range(4):
-                lanes = pl.ds(pl.multiple_of((4 * b + j) * WIDTH, WIDTH), WIDTH)
-                out[:, lanes] = mixed[j * own : (j + 1) * own, :]
-            return carry
-
-        lax.fori_loop(0, 4, mix, 0)
         rows = active.shape[0]
         wide = jnp.concatenate([active[:, b * WIDTH : (b + 1) * WIDTH] for b in range(4)], axis=0)
-        wide = dot_nt(wide, weave).astype(BF16)
+        wide = dot_nt(wide, interleave(PART)).astype(BF16)
         half = d_here.shape[0] // 2
         units = []
         for core in (place[5], place[4]):
@@ -999,8 +979,43 @@
             for own_unit, d_scores in zip(units, (d_here, d_there)):
                 own_u = dot(own_unit, some).astype(BF16)
                 proto = proto + dot_tn(own_u, d_scores[:, a * QUARTER_PAD : (a + 1) * QUARTER_PAD])
-        out[:, FIRST:SECOND] = proj
-        out[:, SECOND:] = proto[:, : out.shape[1] - SECOND]
+        out[:, :WIDTH] = proj
+        out[:, WIDTH:] = proto
+
+
+def head_grads_kernel(place, pooled, d_pre, tail, out, parts):
+    @pl.when(place[0] != SECTIONS - 1)
+    def _():
+        out[...] = jnp.zeros_like(out)
+
+    @pl.when(place[0] == SECTIONS - 1)
+    def _():
+        own = out.shape[0]
+        choose = own_columns(place, own)
+        weave = interleave(PART)
+        own_d = [dot(d_pre[:, q * WIDTH : (q + 1) * WIDTH], choose).astype(BF16) for q in range(4)]
+        own_d = jnp.concatenate(own_d, axis=1)
+
+        def product(b, carry):
+            parts[:, lanes_at(b, WIDTH)] = dot_tn(own_d, pooled[:, lanes_at(b, WIDTH)]).astype(BF16)
+            return carry
+
+        lax.fori_loop(0, 4, product, 0)
+
+        def mix(b, carry):
+            mixed = []
+            for j in range(4):
+                lanes = pl.ds(pl.multiple_of(b * WIDTH + j * PART, PART), PART)
+                four = [parts[q * own : (q + 1) * own, lanes] for q in range(4)]
+                mixed.append(jnp.concatenate(four, axis=1))
+            mixed = dot(jnp.concatenate(mixed, axis=0), weave)
+            for j in range(4):
+                lanes = pl.ds(pl.multiple_of((4 * b + j) * WIDTH, WIDTH), WIDTH)
+                out[:, lanes] = mixed[j * own : (j + 1) * own, :]
+            return carry
+
+        lax.fori_loop(0, 4, mix, 0)
+        out[:, FIRST:] = tail[:, : out.shape[1] - FIRST]
 
 
 def finish_kernel(place, base, reduce, conv, expand, m1, m2, m3, out, buffer, sem):
@@ -1085,7 +1100,7 @@
             copies.append(pltpu.make_async_copy(source, out.at[pl.ds(16, half), :], sem.at[k]))
         run(copies)
         for k, out in enumerate(outs):
-            out[:16, :] = tell_norm(norm[:, k * PART : (k + 1) * PART])
+            out[:16, :] = tell_norm(norm, k * PART)
         for copy in copies:
             copy.wait()
 
@@ -1101,7 +1116,7 @@
                 copies.append(pltpu.make_async_copy(source, target, sem.at[9 * k + tap]))
         run(copies)
         for k, out in enumerate(outs):
-            out[:16, :] = tell_norm(norm[:, (1 ^ k) * PART : ((1 ^ k) + 1) * PART])
+            out[:16, :] = tell_norm(norm, (1 ^ k) * PART)
         for copy in copies:
             copy.wait()
 
@@ -1118,7 +1133,7 @@
             for b in range(4):
                 at = b * HALF_EXPAND
                 lane = u * WIDE + b * PART
-                out[at : at + 16, :] = tell_norm(norm[:, lane : lane + PART])
+                out[at : at + 16, :] = tell_norm(norm, lane)
                 out[at + 16 : at + HALF_EXPAND, :] = buffer[b, pl.ds(u, size // 4, stride=4), :].astype(BF16)
 
 
@@ -1203,7 +1218,7 @@
     rows = micro * cells
     count = float(cells * ndp)
     packed = section_weights[0]
-    norm3 = section_norms[0]
+    norm3 = section_norms.transpose(1, 0, 2)
     param_rows = packed.shape[0]
     own = WIDTH // ndp
     k = functools.partial
@@ -1222,8 +1237,10 @@
     )
     queue_size = CROPS * queue.shape[1]
     note = call(note_kernel, shape((queue_size + 16, PROJ), BF16), pairing, queue, us=0.5)
-    told, told_offsets = gather_dp(note, dp_stages())
+    steps = [1 << bit for bit in range(ndp.bit_length() - 1)]
+    told, told_offsets = gather_dp(note, [(step,) for step in steps[:-1]])
     *came, flat, told[0] = lax.optimization_barrier((*came, flat, *told))[:6]
+    told, told_offsets = [rows_of(told)], [sum(told_offsets, [])]
     conv_part, pair_part = call(
         pick_kernel,
         (shape((QUARTER_CONV, PART), BF16), shape((HALF_REDUCE + 4 * HALF_EXPAND, PART), BF16)),
@@ -1241,6 +1258,8 @@
 
     conv_part = rows_of([conv_part, after(conv_near, active0)])
     w_conv = (conv_part, flip(conv_part, "dp", 1))
+    told.append(flip(after(told[0], active0), "dp", steps[-1]))
+    told_offsets.append([offset ^ steps[-1] for offset in told_offsets[0]])
     w_proj, table = pl.pallas_call(
         tables_kernel,
         name="tables",
@@ -1253,6 +1272,24 @@
         compiler_params=pltpu.CompilerParams(vmem_limit_bytes=12 * 2**20),
         cost_estimate=cost(1.5),
     )(hbm(after(packed, active0)))
+    taps = call(k(taps_kernel, images), pieces_of(9 * PART, BF16), active0, us=1.3)
+    back_rows = 9 * PART // 2 + WIDE // 2
+    back_own = call(
+        back_parts_kernel, [shape((back_rows, PART), BF16)] * 4, place, *w_conv, *pair_parts, us=1
+    )
+    joined = lax.optimization_barrier((*actives0, table, taps, told[1], *back_own))
+    actives0, (table, taps, told[1]), back_own = joined[:4], joined[4:7], joined[7:]
+    pre1, part = call(
+        k(conv_kernel, micro, images),
+        (pieces_of(PART, F32), sums_of),
+        place, *actives0, *w_conv,
+        scratch=[pltpu.VMEM((rows, WIDTH), BF16), pltpu.VMEM((WIDTH, 9 * PART), BF16)],
+        us=3,
+    )
+    sums1 = sum_dp(part)
+    active1_own = call(k(active_kernel, micro, count), pieces_of(PART, BF16), pre1, sums1, conv_part, us=1)
+    actives1 = gather_xor(active1_own, "section")
+    natural = unpack(after(packed, active1_own), FIRST)
     head_rows = rows // PLACES * ndp
     lanes = 4 * QUARTER_PAD
     stages = dp_stages()
@@ -1269,29 +1306,13 @@
                 shape((queued, lanes), BF16), shape((8, lanes), F32),
                 shape((micro, images * ndp, images * ndp), BF16),
             ),
-            place, table, *told,
+            place, after(table, active1_own), *told,
             scratch=[pltpu.VMEM((queued, PROJ), BF16), pltpu.VMEM((queued, lanes), F32)],
             vmem=16, us=5,
         )
-        *actives0, mass = lax.optimization_barrier((*actives0, mass))
-    pre1, part = call(
-        k(conv_kernel, micro, images),
-        (pieces_of(PART, F32), sums_of),
-        place, *actives0, *w_conv,
-        scratch=[pltpu.VMEM((rows, WIDTH), BF16), pltpu.VMEM((WIDTH, 9 * PART), BF16)],
-        us=3,
-    )
-    sums1 = sum_dp(part)
-    active1_own = call(k(active_kernel, micro, count), pieces_of(PART, BF16), pre1, sums1, conv_part, us=1)
-    actives1 = gather_xor(active1_own, "section")
-    natural = unpack(after(packed, active1_own), FIRST)
-    taps = call(k(taps_kernel, images), pieces_of(9 * PART, BF16), after(active0, active1_own), us=1.3)
-    back_rows = 9 * PART // 2 + WIDE // 2
-    back_own = call(
-        back_parts_kernel, [shape((back_rows, PART), BF16)] * 4, place, *w_conv, *pair_parts, us=1
-    )
-    joined = lax.optimization_barrier((*actives1, natural, taps, *back_own))
-    actives1, natural, taps, back_own = joined[:4], joined[4], joined[5], joined[6:]
+    joined = lax.optimization_barrier((*actives1, natural, *([mass] if small else [])))
+    actives1, natural = joined[:4], joined[4]
+    mass = joined[5] if small else None
     active1, pre2, part, w_expand = call(
         k(expand_kernel, micro),
         (pieces_of(WIDTH, BF16), pieces_of(WIDE, F32), shape((8, WIDE), F32), shape((WIDTH, WIDE), BF16)),
@@ -1357,7 +1378,7 @@
         queue_all = told[:, :queue_size].reshape(ndp, CROPS, queue.shape[1], PROJ)
         queue_rows = queue_all.transpose(1, 0, 2, 3).reshape(CROPS, -1, PROJ)
         loss, grads3, active3, unit, d_scores, d_embed, d_pre3 = head(
-            all_pooled, natural, w_proj, protos, norm3, queue_rows, match, micro, images, dp
+            all_pooled, natural, w_proj, protos, norm3[:, 0], queue_rows, match, micro, images, dp
         )
         notes3 = jnp.concatenate([grads3, jnp.full((5, D), loss)])
         d_pooled = dot_nt(dot_tn(order[:, :per_dp], d_pre3).astype(BF16), natural).astype(BF16)
@@ -1441,15 +1462,14 @@
         return call(add_kernel, shape(crossed[0].shape, BF16), *crossed, us=0.6)
 
     expand_near = scatter_near(scatter_start(d_pre2, active1, WIDTH))
-    base = call(
-        head_grads_kernel,
-        shape((own, param_rows), F32),
-        place, after(all_pooled, d_pre2), active3, unit, d_scores, flip(d_scores, "dp", 1), d_embed, d_pre3,
-        scratch=[pltpu.VMEM((4 * own, D), BF16)],
-        us=6,
-    )
-    joined = lax.optimization_barrier((*partial, base, *expand_near[: 2 if ndp == 8 else 1]))
-    partial, base, expand_near = joined[:SECTIONS], joined[SECTIONS], joined[SECTIONS + 1 :]
+    tail = call(
+        tail_grads_kernel,
+        shape((own, WIDTH + QUARTER_PAD), F32),
+        place, after(active3, d_pre2), unit, d_scores, flip(d_scores, "dp", 1), d_embed,
+        us=3,
+    )
+    joined = lax.optimization_barrier((*partial, tail, *expand_near[: 2 if ndp == 8 else 1]))
+    partial, tail, expand_near = joined[:SECTIONS], joined[SECTIONS], joined[SECTIONS + 1 :]
 
     d_y1, part = call(
         k(silu_back_kernel, micro, count),
@@ -1462,8 +1482,15 @@
     )
     d_pre1s = gather_xor(d_pre1_own, "section")
     expand_far = scatter_far(expand_near, d_pre1_own)
-    joined = lax.optimization_barrier((*d_pre1s, *expand_far))
-    d_pre1s, expand_far = joined[:SECTIONS], joined[SECTIONS:]
+    base = call(
+        head_grads_kernel,
+        shape((own, param_rows), F32),
+        place, after(all_pooled, d_pre1_own), d_pre3, tail,
+        scratch=[pltpu.VMEM((4 * own, D), BF16)],
+        us=4,
+    )
+    joined = lax.optimization_barrier((*d_pre1s, base, *expand_far))
+    d_pre1s, base, expand_far = joined[:SECTIONS], joined[SECTIONS], joined[SECTIONS + 1 :]
     d_pre1, d_y0, part = call(
         k(conv_back_kernel, micro, images, count),
         (pieces_of(WIDTH, BF16), pieces_of(PART, F32), sums_of),
@@ -1471,6 +1498,7 @@
         scratch=[pltpu.VMEM((9 * PART, WIDTH), BF16)],
         us=3.5,
     )
+    conv_started = scatter_start(d_pre1, taps, 9 * PART)
     back0 = sum_dp(part)
     d_pre0_own = call(
         k(last_norm_back_kernel, micro, count),
@@ -1478,7 +1506,7 @@
         place, d_y0, pre0, sums0, back0, pair_part, back2, back1, notes3,
     )
     d_pre0s = gather_xor(d_pre0_own, "section")
-    conv_near_sum = scatter_near(scatter_start(after(d_pre1, d_pre0_own), taps, 9 * PART))
+    conv_near_sum = scatter_near(conv_started, d_pre0_own)
     joined = lax.optimization_barrier((*d_pre0s, conv_near_sum[0]))
     d_pre0s, conv_near_sum = joined[:SECTIONS], (joined[SECTIONS], conv_near_sum[1])
     conv_far = scatter_far(conv_near_sum)
@@ -1504,7 +1532,7 @@
         us=2,
     )
     norm_grads, loss = call(
-        told_kernel, (shape((3, D), F32), shape((8, PROJ), F32)), place, *d_pre0s, notes3, us=0.5
+        told_kernel, (shape((3, 1, D), F32), shape((8, PROJ), F32)), place, *d_pre0s, notes3, us=0.5
     )
     g_conv = scatter_last(conv_far)
     g_expand = scatter_last(expand_far)
@@ -1528,7 +1556,7 @@
         cost_estimate=cost(2),
     )(place, base, g_reduce, g_conv, g_expand, *mixed)
     grad_in = grad_in.reshape(micro, CROPS, SIDE, SIDE, images, WIDE).transpose(0, 1, 4, 2, 3, 5)
-    return (loss[0, 0], grad_in, weight_grads.T[None], norm_grads[None])
+    return (loss[0, 0], grad_in, weight_grads.T[None], norm_grads.transpose(1, 0, 2))
 
 
 def solution(mesh):

time: 231 us -> 226 us (0.978)
  starting transfers between devices: 100 us -> 97.3 us
    ppermute x72 -> x71, starting transfers between devices: 81.7 us -> 78.8 us  [flip(): lax.ppermute(value, axis, [(source, source ^ step) for source in range(co...]
    ppermute x72 -> x71, waiting for transfers between devices: 63 us -> 60.4 us  [flip(): lax.ppermute(value, axis, [(source, source ^ step) for source in range(co...]
    pallas_call x40 -> x42, Pallas kernels: 50.4 us -> 49.9 us  [call(): pl.pallas_call(kernel, name=getattr(kernel, 'func', kernel).__name__, out...]
  transfers between devices with their start and end apart: 78 -> 77, of which waited for: 47 -> 45; matrix products, arithmetic and copies ran while one was open for 1% -> 0% of each run, Pallas kernels for 18% -> 19%
where the time goes in v2:
time: 226 us; the launch traced here: 224 us
  starting transfers between devices  97.3 us (43%)
  waiting for transfers between devices  64.6 us (29%)
  Pallas kernels  59.5 us (26%)
    ppermute x71, starting transfers between devices, flip(): lax.ppermute(value, axis, [(source, source ^ step) for source in range(co...  78.8 us
    ppermute x71, waiting for transfers between devices, flip(): lax.ppermute(value, axis, [(source, source ^ step) for source in range(co...  60.4 us
    pallas_call x42, Pallas kernels, call(): pl.pallas_call(kernel, name=getattr(kernel, 'func', kernel).__name__, out...  49.9 us
    ppermute x3, starting transfers between devices, body(): lax.ppermute(mixed[j - 1], 'section', [(u ^ j, u) for u in range(3)])  9.21 us
    ppermute x3, starting transfers between devices, body(): lax.ppermute(messages[j - 1], 'section', [(u, u ^ j) for u in range(3)])  9.21 us
  transfers between devices with their start and end apart: 77, of which 45 were waited for; matrix products, arithmetic and copies ran while one was open for 0% of the time, Pallas kernels for 19%

profile of v2, /device:TPU:2, one launch (start us, length us, event | category | flops | bytes accessed | tf_op | source)
XLA Modules:
  0.0 224.2 jit_solution(8938512000639052907)
XLA Ops:
  1.5 2.4 %pack.1 = (bf16[1168,128]{1,0:T(8,128)(2,1)S(1)}, bf16[1168,128]{1,0:T(8,128)(2,1)S(1)}, bf16[1168,128]{1,0:T(8,128)(2,1)S(1)}, bf16[1168,128]{1,0:T(8,128)(2,1)S(1)}) custom-call(s32[9]{0:T(128)S(1)} %stack.39.place, bf16[9456,512]{1,0:T(8,128)(2,1)} %bitcast.22, f32[3,1,2048]{2,1,0:T(1,128)S(1)} %bitcast.28), custom_call_target="tpu_custom_call" | custom-call | bytes 6000000 | tf_op jit(solution)/shard_map/pack/pallas_call | solution.py:1142
  7.3 5.9 %collective-permute-start.2 = (bf16[1168,128]{1,0:T(8,128)(2,1)S(1)}, bf16[1168,128]{1,0:T(8,128)(2,1)S(1)}, u32[]{:S(2)}, u32[]{:S(2)}) collective-permute-start(bf16[1168,128]{1,0:T(8,128)(2,1)S(1)} %get-tuple-element.153), channel_id=1, source_target_pairs={{0,24},{8,16},{16,8},{1,25},{9,17},{17,9},{2,26},{10,18},{18,10},{... | collective-permute-start | bytes 897032 | tf_op jit(solution)/shard_map/ppermute | solution.py:1232
  16.9 2.5 %collective-permute-done.4.refs_1_ = bf16[288,128]{1,0:T(8,128)(2,1)S(1)} collective-permute-done((bf16[288,128]{1,0:T(8,128)(2,1)S(1)}, bf16[288,128]{1,0:T(8,128)(2,1)S(1)}, u32[]{:S(2)}, u32[]{:S(2)}) %collective-permute-start.4) | collective-permute-done | bytes 73760 | tf_op jit(solution)/shard_map/ppermute | solution.py:55
  26.1 3.6 %collective-permute-start.9 = (f32[8,128]{1,0:T(8,128)S(1)}, f32[8,128]{1,0:T(8,128)S(1)}, u32[]{:S(2)}, u32[]{:S(2)}) collective-permute-start(f32[8,128]{1,0:T(8,128)S(1)} %add.82), channel_id=1, source_target_pairs={{0,6},{1,7},{2,4},{3,5},{4,2},{5,3},{6,0},{7,1},{8,14},{9,15},{10,... | collective-permute-start | bytes 12296 | tf_op jit(solution)/shard_map/ppermute | solution.py:55
  30.5 2.6 %collective-permute-done.9 = f32[8,128]{1,0:T(8,128)S(1)} collective-permute-done((f32[8,128]{1,0:T(8,128)S(1)}, f32[8,128]{1,0:T(8,128)S(1)}, u32[]{:S(2)}, u32[]{:S(2)}) %collective-permute-start.9) | collective-permute-done | bytes 4128 | tf_op jit(solution)/shard_map/ppermute | solution.py:55
  34.5 3.9 %collective-permute-start.12 = (bf16[784,128]{1,0:T(8,128)(2,1)S(1)}, bf16[784,128]{1,0:T(8,128)(2,1)S(1)}, u32[]{:S(2)}, u32[]{:S(2)}) collective-permute-start(bf16[784,128]{1,0:T(8,128)(2,1)S(1)} %active_kernel.2.active.a0), channel_id=1, source_target_pairs={{0,24},{8,16},{16,8},{24,0},{1,25},{9,17},{17,9},{25,1},{2,26},{10... | collective-permute-start | bytes 602120 | tf_op jit(solution)/shard_map/ppermute | solution.py:55
  39.0 2.1 collective-permute-start.13
  44.8 3.3 %collective-permute-done.13.refs_1_ = bf16[576,128]{1,0:T(8,128)(2,1)S(1)} collective-permute-done((bf16[576,128]{1,0:T(8,128)(2,1)S(1)}, bf16[576,128]{1,0:T(8,128)(2,1)S(1)}, u32[]{:S(2)}, u32[]{:S(2)}) %collective-permute-start.13) | collective-permute-done | bytes 147488 | tf_op jit(solution)/shard_map/ppermute | solution.py:55
  48.3 2.2 conv_kernel.1
  53.7 2.4 %collective-permute-start.17 = (f32[8,128]{1,0:T(8,128)S(1)}, f32[8,128]{1,0:T(8,128)S(1)}, u32[]{:S(2)}, u32[]{:S(2)}) collective-permute-start(f32[8,128]{1,0:T(8,128)S(1)} %add.86), channel_id=1, source_target_pairs={{0,2},{1,3},{2,0},{3,1},{4,6},{5,7},{6,4},{7,5},{8,10},{9,11},{10,... | collective-permute-start | bytes 12296 | tf_op jit(solution)/shard_map/ppermute | solution.py:55
  58.2 2.7 %collective-permute-start.22 = (bf16[784,128]{1,0:T(8,128)(2,1)S(1)}, bf16[784,128]{1,0:T(8,128)(2,1)S(1)}, u32[]{:S(2)}, u32[]{:S(2)}) collective-permute-start(bf16[784,128]{1,0:T(8,128)(2,1)S(1)} %active_kernel.3.a0), channel_id=1, source_target_pairs={{0,24},{8,16},{16,8},{24,0},{1,25},{9,17},{17,9},{25,1},{2,26},{10... | collective-permute-start | bytes 602120 | tf_op jit(solution)/shard_map/ppermute | solution.py:55
  61.8 3.8 %unpack.1.w_head = bf16[2048,2048]{1,0:T(8,128)(2,1)S(1)} custom-call(bf16[9456,512]{1,0:T(8,128)(2,1)S(1)} %bitcast.26), custom_call_target="tpu_custom_call" | custom-call | bytes 12000000 | tf_op jit(solution)/shard_map/unpack/pallas_call | solution.py:1069
  65.7 3.0 %mass_kernel.1 = (bf16[512,3072]{1,0:T(8,128)(2,1)S(1)}, f32[8,3072]{1,0:T(8,128)S(1)}, bf16[2,32,32]{2,1,0:T(8,128)(2,1)S(1)}) custom-call(s32[9]{0:T(128)S(1)} %stack.39.place, bf16[768,512]{1,0:T(8,128)(2,1)S(1)} %get-tuple-element.180.table, bf16[576,128]{1,0:T(8,128)(2,1)S(1)} %rows_kernel.5.refs_0_, bf16[576,128]{1,0:T(8,128)(2,1)S(1)} %collective-permute-done.13.refs_1_), custom_call_target="tpu_custom_call" | custom-call | bytes 15000000 | tf_op jit(solution)/shard_map/mass_kernel/pallas_call | solution.py:139
  87.3 2.1 collective-permute-start.32
  96.8 2.1 collective-permute-start.37
  99.0 10.9 %head_kernel.1 = (bf16[128,2048]{1,0:T(8,128)(2,1)S(1)}, bf16[128,2048]{1,0:T(8,128)(2,1)S(1)}, bf16[128,128]{1,0:T(8,128)(2,1)S(1)}, bf16[64,3072]{1,0:T(8,128)...) custom-call(s32[9]{0:T(128)S(1)} %stack.39.place, ...), custom_call_target="tpu_custom_call" | custom-call | bytes 36000000 | tf_op jit(solution)/shard_map/head_kernel/pallas_call | solution.py:139
  111.2 4.5 %head_back_kernel.1 = (bf16[16,512]{1,0:T(8,128)(2,1)S(1)}, bf16[16,512]{1,0:T(8,128)(2,1)S(1)}, bf16[16,512]{1,0:T(8,128)(2,1)S(1)}, bf16[16,512]{1,0:T(8,128)(...) custom-call(s32[9]{0:T(128)S(1)} %stack.39.place, ...), custom_call_target="tpu_custom_call" | custom-call | bytes 15000000 | tf_op jit(solution)/shard_map/head_back_kernel/pallas_call | solution.py:139
  117.1 2.1 collective-permute-start.40
  127.1 2.1 collective-permute-start.42
  142.6 4.7 %collective-permute-done.46.q2 = bf16[784,128]{1,0:T(8,128)(2,1)S(1)} collective-permute-done((bf16[784,128]{1,0:T(8,128)(2,1)S(1)}, bf16[784,128]{1,0:T(8,128)(2,1)S(1)}, u32[]{:S(2)}, u32[]{:S(2)}) %collective-permute-start.46) | collective-permute-done | bytes 200736 | tf_op jit(solution)/shard_map/ppermute | solution.py:55
  148.9 2.0 collective-permute-start.54
  161.3 2.1 head_grads_kernel.1.base
  164.6 2.1 collective-permute-done.56.d2
  166.8 2.4 %conv_back_kernel.1 = (bf16[784,512]{1,0:T(8,128)(2,1)S(1)}, f32[784,128]{1,0:T(8,128)S(1)}, f32[8,128]{1,0:T(8,128)S(1)}) custom-call(s32[9]{0:T(128)S(1)} %stack.39.place, bf16[784,128]{1,0:T(8,128)(2,1)S(1)} %norm_back_kernel.1.d0, bf16[784,128]{1,0:T(8,128)(2,1)S(1)} %collective-permute-done.55.d1, bf16[784,128]{1,0:T(8,128)(2,1)S(1)} %collective-permute-done.56.d2, ...), custom_call_target="tpu_custom_call" | custom-call | bytes 10500000 | tf_op jit(solution)/shard_map/conv_back_kernel/pallas_call | solution.py:139
  169.2 2.2 pair_kernel.3
  186.5 3.2 %collective-permute-done.66.n3.d3 = bf16[832,128]{1,0:T(8,128)(2,1)S(1)} collective-permute-done((bf16[832,128]{1,0:T(8,128)(2,1)S(1)}, bf16[832,128]{1,0:T(8,128)(2,1)S(1)}, u32[]{:S(2)}, u32[]{:S(2)}) %collective-permute-start.66) | collective-permute-done | bytes 213024 | tf_op jit(solution)/shard_map/ppermute | solution.py:55
  189.7 2.5 %collective-permute-done.65.n2.d2 = bf16[832,128]{1,0:T(8,128)(2,1)S(1)} collective-permute-done((bf16[832,128]{1,0:T(8,128)(2,1)S(1)}, bf16[832,128]{1,0:T(8,128)(2,1)S(1)}, u32[]{:S(2)}, u32[]{:S(2)}) %collective-permute-start.65) | collective-permute-done | bytes 213024 | tf_op jit(solution)/shard_map/ppermute | solution.py:55
  202.0 2.5 %reduce_back_kernel.1 = f32[196,4,512]{2,1,0:T(4,128)} custom-call(s32[9]{0:T(128)S(1)} %stack.39.place, bf16[784,512]{1,0:T(8,128)(2,1)S(1)} %get-tuple-element.276.d_full, bf16[4,832,128]{2,1,0:T(8,128)(2,1)S(1)} %stack_kernel.1.back0, bf16[4,832,128]{2,1,0:T(8,128)(2,1)S(1)} %collective-permute-done.59.back1, f32[784,512]{1,0:T(8,128)S(1)} %get-tuple-element.215.d_z), custom_call_target="tpu_custom_call" | custom-call | bytes 6000000 | tf_op jit(solution)/shard_map/reduce_back_kernel/pallas_call | solution.py:139
  204.4 3.1 %collective-permute-done.73.came = bf16[64,1152]{1,0:T(8,128)(2,1)S(1)} collective-permute-done((bf16[64,1152]{1,0:T(8,128)(2,1)S(1)}, bf16[64,1152]{1,0:T(8,128)(2,1)S(1)}, u32[]{:S(2)}, u32[]{:S(2)}) %collective-permute-start.73) | collective-permute-done | bytes 147488 | tf_op jit(solution)/shard_map/ppermute | solution.py:55
  209.6 2.5 %collective-permute-start.74 = (bf16[64,1152]{1,0:T(8,128)(2,1)S(1)}, bf16[64,1152]{1,0:T(8,128)(2,1)S(1)}, u32[]{:S(2)}, u32[]{:S(2)}) collective-permute-start(bf16[64,1152]{1,0:T(8,128)(2,1)S(1)} %get-tuple-element.292), channel_id=1, source_target_pairs={{8,0},{0,8},{24,16},{9,1},{1,9},{25,17},{10,2},{2,10},{26,18},{11,... | collective-permute-start | bytes 442376 | tf_op jit(solution)/shard_map/ppermute | solution.py:1544
  213.4 5.4 %collective-permute-start.76 = (bf16[64,1152]{1,0:T(8,128)(2,1)S(1)}, bf16[64,1152]{1,0:T(8,128)(2,1)S(1)}, u32[]{:S(2)}, u32[]{:S(2)}) collective-permute-start(bf16[64,1152]{1,0:T(8,128)(2,1)S(1)} %get-tuple-element.294), channel_id=1, source_target_pairs={{24,0},{16,8},{8,16},{25,1},{17,9},{9,17},{26,2},{18,10},{10,18},{... | collective-permute-start | bytes 442376 | tf_op jit(solution)/shard_map/ppermute | solution.py:1544
  219.3 3.0 %collective-permute-done.75.m2 = bf16[64,1152]{1,0:T(8,128)(2,1)S(1)} collective-permute-done((bf16[64,1152]{1,0:T(8,128)(2,1)S(1)}, bf16[64,1152]{1,0:T(8,128)(2,1)S(1)}, u32[]{:S(2)}, u32[]{:S(2)}) %collective-permute-start.75) | collective-permute-done | bytes 147488 | tf_op jit(solution)/shard_map/ppermute | solution.py:1544
  (199 shorter events, 120.8 us)
Async XLA Ops:
  3.9 15.5 %collective-permute-start = (bf16[1168,128]{1,0:T(8,128)(2,1)S(1)}, bf16[1168,128]{1,0:T(8,128)(2,1)S(1)}, u32[]{:S(2)}, u32[]{:S(2)}) collective-permute-start(bf16[1168,128]{1,0:T(8,128)(2,1)S(1)} %get-tuple-element.151), channel_id=1, source_target_pairs={{0,8},{8,0},{16,24},{1,9},{9,1},{17,25},{2,10},{10,2},{18,26},{3,1... | collective-permute-start | bytes 897032 | tf_op jit(solution)/shard_map/ppermute | solution.py:1232
  5.8 13.5 %collective-permute-start.1 = (bf16[1168,128]{1,0:T(8,128)(2,1)S(1)}, bf16[1168,128]{1,0:T(8,128)(2,1)S(1)}, u32[]{:S(2)}, u32[]{:S(2)}) collective-permute-start(bf16[1168,128]{1,0:T(8,128)(2,1)S(1)} %get-tuple-element.152), channel_id=1, source_target_pairs={{0,16},{8,24},{16,0},{1,17},{9,25},{17,1},{2,18},{10,26},{18,2},{3... | collective-permute-start | bytes 897032 | tf_op jit(solution)/shard_map/ppermute | solution.py:1232
  7.3 13.3 %collective-permute-start.2 = (bf16[1168,128]{1,0:T(8,128)(2,1)S(1)}, bf16[1168,128]{1,0:T(8,128)(2,1)S(1)}, u32[]{:S(2)}, u32[]{:S(2)}) collective-permute-start(bf16[1168,128]{1,0:T(8,128)(2,1)S(1)} %get-tuple-element.153), channel_id=1, source_target_pairs={{0,24},{8,16},{16,8},{1,25},{9,17},{17,9},{2,26},{10,18},{18,10},{... | collective-permute-start | bytes 897032 | tf_op jit(solution)/shard_map/ppermute | solution.py:1232
  21.4 13.0 %collective-permute-start.14 = (bf16[1168,128]{1,0:T(8,128)(2,1)S(1)}, bf16[1168,128]{1,0:T(8,128)(2,1)S(1)}, u32[]{:S(2)}, u32[]{:S(2)}) collective-permute-start(bf16[1168,128]{1,0:T(8,128)(2,1)S(1)} %get-tuple-element.166.refs_0_), channel_id=1, source_target_pairs={{0,2},{1,3},{2,0},{3,1},{4,6},{5,7},{6,4},{7,5},{8,10},{9,11},{10,... | collective-permute-start | bytes 897032 | tf_op jit(solution)/shard_map/ppermute | solution.py:55
  34.4 9.2 %collective-permute-start.15 = (bf16[2336,128]{1,0:T(8,128)(2,1)S(1)}, bf16[2336,128]{1,0:T(8,128)(2,1)S(1)}, u32[]{:S(2)}, u32[]{:S(2)}) collective-permute-start(bf16[2336,128]{1,0:T(8,128)(2,1)S(1)} %rows_kernel.6.conv_a.wa.told), channel_id=1, source_target_pairs={{0,1},{1,0},{2,3},{3,2},{4,5},{5,4},{6,7},{7,6},{8,9},{9,8},{10,11... | collective-permute-start | bytes 1794056 | tf_op jit(solution)/shard_map/ppermute | solution.py:55
  34.5 13.5 %collective-permute-start.12 = (bf16[784,128]{1,0:T(8,128)(2,1)S(1)}, bf16[784,128]{1,0:T(8,128)(2,1)S(1)}, u32[]{:S(2)}, u32[]{:S(2)}) collective-permute-start(bf16[784,128]{1,0:T(8,128)(2,1)S(1)} %active_kernel.2.active.a0), channel_id=1, source_target_pairs={{0,24},{8,16},{16,8},{24,0},{1,25},{9,17},{17,9},{25,1},{2,26},{10... | collective-permute-start | bytes 602120 | tf_op jit(solution)/shard_map/ppermute | solution.py:55
  38.4 9.9 %collective-permute-start.11 = (bf16[784,128]{1,0:T(8,128)(2,1)S(1)}, bf16[784,128]{1,0:T(8,128)(2,1)S(1)}, u32[]{:S(2)}, u32[]{:S(2)}) collective-permute-start(bf16[784,128]{1,0:T(8,128)(2,1)S(1)} %active_kernel.2.active.a0), channel_id=1, source_target_pairs={{0,16},{8,24},{16,0},{24,8},{1,17},{9,25},{17,1},{25,9},{2,18},{10... | collective-permute-start | bytes 602120 | tf_op jit(solution)/shard_map/ppermute | solution.py:55
  38.4 9.9 %collective-permute-start.10 = (bf16[784,128]{1,0:T(8,128)(2,1)S(1)}, bf16[784,128]{1,0:T(8,128)(2,1)S(1)}, u32[]{:S(2)}, u32[]{:S(2)}) collective-permute-start(bf16[784,128]{1,0:T(8,128)(2,1)S(1)} %active_kernel.2.active.a0), channel_id=1, source_target_pairs={{0,8},{8,0},{16,24},{24,16},{1,9},{9,1},{17,25},{25,17},{2,10},{10... | collective-permute-start | bytes 602120 | tf_op jit(solution)/shard_map/ppermute | solution.py:55
  39.0 9.0 %collective-permute-start.13 = (bf16[576,128]{1,0:T(8,128)(2,1)S(1)}, bf16[576,128]{1,0:T(8,128)(2,1)S(1)}, u32[]{:S(2)}, u32[]{:S(2)}) collective-permute-start(bf16[576,128]{1,0:T(8,128)(2,1)S(1)} %rows_kernel.5.refs_0_), channel_id=1, source_target_pairs={{0,4},{1,5},{2,6},{3,7},{4,0},{5,1},{6,2},{7,3},{8,12},{9,13},{10,... | collective-permute-start | bytes 442376 | tf_op jit(solution)/shard_map/ppermute | solution.py:55
  58.2 10.5 %collective-permute-start.22 = (bf16[784,128]{1,0:T(8,128)(2,1)S(1)}, bf16[784,128]{1,0:T(8,128)(2,1)S(1)}, u32[]{:S(2)}, u32[]{:S(2)}) collective-permute-start(bf16[784,128]{1,0:T(8,128)(2,1)S(1)} %active_kernel.3.a0), channel_id=1, source_target_pairs={{0,24},{8,16},{16,8},{24,0},{1,25},{9,17},{17,9},{25,1},{2,26},{10... | collective-permute-start | bytes 602120 | tf_op jit(solution)/shard_map/ppermute | solution.py:55
  95.4 20.3 %collective-permute-start.35 = (bf16[832,128]{1,0:T(8,128)(2,1)S(1)}, bf16[832,128]{1,0:T(8,128)(2,1)S(1)}, u32[]{:S(2)}, u32[]{:S(2)}) collective-permute-start(bf16[832,128]{1,0:T(8,128)(2,1)S(1)} %get-tuple-element.208), channel_id=1, source_target_pairs={{0,8},{8,0},{16,24},{24,16},{1,9},{9,1},{17,25},{25,17},{2,10},{10... | collective-permute-start | bytes 638984 | tf_op jit(solution)/shard_map/ppermute | solution.py:55
  96.2 19.5 %collective-permute-start.36 = (bf16[832,128]{1,0:T(8,128)(2,1)S(1)}, bf16[832,128]{1,0:T(8,128)(2,1)S(1)}, u32[]{:S(2)}, u32[]{:S(2)}) collective-permute-start(bf16[832,128]{1,0:T(8,128)(2,1)S(1)} %get-tuple-element.209), channel_id=1, source_target_pairs={{0,16},{8,24},{16,0},{24,8},{1,17},{9,25},{17,1},{25,9},{2,18},{10... | collective-permute-start | bytes 638984 | tf_op jit(solution)/shard_map/ppermute | solution.py:55
  96.8 18.9 %collective-permute-start.37 = (bf16[832,128]{1,0:T(8,128)(2,1)S(1)}, bf16[832,128]{1,0:T(8,128)(2,1)S(1)}, u32[]{:S(2)}, u32[]{:S(2)}) collective-permute-start(bf16[832,128]{1,0:T(8,128)(2,1)S(1)} %get-tuple-element.210), channel_id=1, source_target_pairs={{0,24},{8,16},{16,8},{24,0},{1,25},{9,17},{17,9},{25,1},{2,26},{10... | collective-permute-start | bytes 638984 | tf_op jit(solution)/shard_map/ppermute | solution.py:55
  129.1 9.7 %collective-permute-start.48 = (bf16[64,3072]{1,0:T(8,128)(2,1)S(1)}, bf16[64,3072]{1,0:T(8,128)(2,1)S(1)}, u32[]{:S(2)}, u32[]{:S(2)}) collective-permute-start(bf16[64,3072]{1,0:T(8,128)(2,1)S(1)} %get-tuple-element.226.d_here), channel_id=1, source_target_pairs={{0,1},{1,0},{2,3},{3,2},{4,5},{5,4},{6,7},{7,6},{8,9},{9,8},{10,11... | collective-permute-start | bytes 1179656 | tf_op jit(solution)/shard_map/ppermute | solution.py:55
  134.2 32.5 %collective-permute-start.59 = (bf16[4,832,128]{2,1,0:T(8,128)(2,1)S(1)}, bf16[4,832,128]{2,1,0:T(8,128)(2,1)S(1)}, u32[]{:S(2)}, u32[]{:S(2)}) collective-permute-start(bf16[4,832,128]{2,1,0:T(8,128)(2,1)S(1)} %stack_kernel.1.back0), channel_id=1, source_target_pairs={{0,1},{1,0},{2,3},{3,2},{4,5},{5,4},{6,7},{7,6},{8,9},{9,8},{10,11... | collective-permute-start | bytes 2555912 | tf_op jit(solution)/shard_map/ppermute | solution.py:55
  136.4 11.0 %collective-permute-start.46 = (bf16[784,128]{1,0:T(8,128)(2,1)S(1)}, bf16[784,128]{1,0:T(8,128)(2,1)S(1)}, u32[]{:S(2)}, u32[]{:S(2)}) collective-permute-start(bf16[784,128]{1,0:T(8,128)(2,1)S(1)} %get-tuple-element.220), channel_id=1, source_target_pairs={{0,16},{8,24},{16,0},{24,8},{1,17},{9,25},{17,1},{25,9},{2,18},{10... | collective-permute-start | bytes 602120 | tf_op jit(solution)/shard_map/ppermute | solution.py:55
  137.2 10.1 %collective-permute-start.47 = (bf16[784,128]{1,0:T(8,128)(2,1)S(1)}, bf16[784,128]{1,0:T(8,128)(2,1)S(1)}, u32[]{:S(2)}, u32[]{:S(2)}) collective-permute-start(bf16[784,128]{1,0:T(8,128)(2,1)S(1)} %get-tuple-element.221), channel_id=1, source_target_pairs={{0,24},{8,16},{16,8},{24,0},{1,25},{9,17},{17,9},{25,1},{2,26},{10... | collective-permute-start | bytes 602120 | tf_op jit(solution)/shard_map/ppermute | solution.py:55
  155.8 8.8 %collective-permute-start.57 = (bf16[784,128]{1,0:T(8,128)(2,1)S(1)}, bf16[784,128]{1,0:T(8,128)(2,1)S(1)}, u32[]{:S(2)}, u32[]{:S(2)}) collective-permute-start(bf16[784,128]{1,0:T(8,128)(2,1)S(1)} %norm_back_kernel.1.d0), channel_id=1, source_target_pairs={{0,24},{8,16},{16,8},{24,0},{1,25},{9,17},{17,9},{25,1},{2,26},{10... | collective-permute-start | bytes 602120 | tf_op jit(solution)/shard_map/ppermute | solution.py:55
  157.0 9.7 %collective-permute-start.56 = (bf16[784,128]{1,0:T(8,128)(2,1)S(1)}, bf16[784,128]{1,0:T(8,128)(2,1)S(1)}, u32[]{:S(2)}, u32[]{:S(2)}) collective-permute-start(bf16[784,128]{1,0:T(8,128)(2,1)S(1)} %norm_back_kernel.1.d0), channel_id=1, source_target_pairs={{0,16},{8,24},{16,0},{24,8},{1,17},{9,25},{17,1},{25,9},{2,18},{10... | collective-permute-start | bytes 602120 | tf_op jit(solution)/shard_map/ppermute | solution.py:55
  158.0 8.7 %collective-permute-start.55 = (bf16[784,128]{1,0:T(8,128)(2,1)S(1)}, bf16[784,128]{1,0:T(8,128)(2,1)S(1)}, u32[]{:S(2)}, u32[]{:S(2)}) collective-permute-start(bf16[784,128]{1,0:T(8,128)(2,1)S(1)} %norm_back_kernel.1.d0), channel_id=1, source_target_pairs={{0,8},{8,0},{16,24},{24,16},{1,9},{9,1},{17,25},{25,17},{2,10},{10... | collective-permute-start | bytes 602120 | tf_op jit(solution)/shard_map/ppermute | solution.py:55
  171.4 12.7 %collective-permute-start.67 = (bf16[4,64,1152]{2,1,0:T(8,128)(2,1)S(1)}, bf16[4,64,1152]{2,1,0:T(8,128)(2,1)S(1)}, u32[]{:S(2)}, u32[]{:S(2)}) collective-permute-start(bf16[4,64,1152]{2,1,0:T(8,128)(2,1)S(1)} %get-tuple-element.263), channel_id=1, source_target_pairs={{0,1},{1,0},{2,3},{3,2},{4,5},{5,4},{6,7},{7,6},{8,9},{9,8},{10,11... | collective-permute-start | bytes 1769480 | tf_op jit(solution)/shard_map/ppermute | solution.py:55
  180.5 9.2 %collective-permute-start.66 = (bf16[832,128]{1,0:T(8,128)(2,1)S(1)}, bf16[832,128]{1,0:T(8,128)(2,1)S(1)}, u32[]{:S(2)}, u32[]{:S(2)}) collective-permute-start(bf16[832,128]{1,0:T(8,128)(2,1)S(1)} %last_norm_back_kernel.1.n0.d0), channel_id=1, source_target_pairs={{0,24},{8,16},{16,8},{24,0},{1,25},{9,17},{17,9},{25,1},{2,26},{10... | collective-permute-start | bytes 638984 | tf_op jit(solution)/shard_map/ppermute | solution.py:55
  181.8 10.4 %collective-permute-start.65 = (bf16[832,128]{1,0:T(8,128)(2,1)S(1)}, bf16[832,128]{1,0:T(8,128)(2,1)S(1)}, u32[]{:S(2)}, u32[]{:S(2)}) collective-permute-start(bf16[832,128]{1,0:T(8,128)(2,1)S(1)} %last_norm_back_kernel.1.n0.d0), channel_id=1, source_target_pairs={{0,16},{8,24},{16,0},{24,8},{1,17},{9,25},{17,1},{25,9},{2,18},{10... | collective-permute-start | bytes 638984 | tf_op jit(solution)/shard_map/ppermute | solution.py:55
  182.7 9.6 %collective-permute-start.64 = (bf16[832,128]{1,0:T(8,128)(2,1)S(1)}, bf16[832,128]{1,0:T(8,128)(2,1)S(1)}, u32[]{:S(2)}, u32[]{:S(2)}) collective-permute-start(bf16[832,128]{1,0:T(8,128)(2,1)S(1)} %last_norm_back_kernel.1.n0.d0), channel_id=1, source_target_pairs={{0,8},{8,0},{16,24},{24,16},{1,9},{9,1},{17,25},{25,17},{2,10},{10... | collective-permute-start | bytes 638984 | tf_op jit(solution)/shard_map/ppermute | solution.py:55
  184.8 9.1 %collective-permute-start.72 = (bf16[2,64,1152]{2,1,0:T(8,128)(2,1)S(1)}, bf16[2,64,1152]{2,1,0:T(8,128)(2,1)S(1)}, u32[]{:S(2)}, u32[]{:S(2)}) collective-permute-start(bf16[2,64,1152]{2,1,0:T(8,128)(2,1)S(1)} %get-tuple-element.279), channel_id=1, source_target_pairs={{0,2},{1,3},{2,0},{3,1},{4,6},{5,7},{6,4},{7,5},{8,10},{9,11},{10,... | collective-permute-start | bytes 884744 | tf_op jit(solution)/shard_map/ppermute | solution.py:55
  193.9 13.6 %collective-permute-start.73 = (bf16[64,1152]{1,0:T(8,128)(2,1)S(1)}, bf16[64,1152]{1,0:T(8,128)(2,1)S(1)}, u32[]{:S(2)}, u32[]{:S(2)}) collective-permute-start(bf16[64,1152]{1,0:T(8,128)(2,1)S(1)} %get-tuple-element.281), channel_id=1, source_target_pairs={{0,4},{1,5},{2,6},{3,7},{4,0},{5,1},{6,2},{7,3},{8,12},{9,13},{10,... | collective-permute-start | bytes 442376 | tf_op jit(solution)/shard_map/ppermute | solution.py:55
  196.3 11.3 %collective-permute-start.69 = (bf16[64,512]{1,0:T(8,128)(2,1)S(1)}, bf16[64,512]{1,0:T(8,128)(2,1)S(1)}, u32[]{:S(2)}, u32[]{:S(2)}) collective-permute-start(bf16[64,512]{1,0:T(8,128)(2,1)S(1)} %get-tuple-element.273), channel_id=1, source_target_pairs={{0,2},{1,3},{2,0},{3,1},{4,6},{5,7},{6,4},{7,5},{8,10},{9,11},{10,... | collective-permute-start | bytes 196616 | tf_op jit(solution)/shard_map/ppermute | solution.py:55
  197.4 11.6 %collective-permute-start.70 = (bf16[64,512]{1,0:T(8,128)(2,1)S(1)}, bf16[64,512]{1,0:T(8,128)(2,1)S(1)}, u32[]{:S(2)}, u32[]{:S(2)}) collective-permute-start(bf16[64,512]{1,0:T(8,128)(2,1)S(1)} %get-tuple-element.274), channel_id=1, source_target_pairs={{0,4},{1,5},{2,6},{3,7},{4,0},{5,1},{6,2},{7,3},{8,12},{9,13},{10,... | collective-permute-start | bytes 196616 | tf_op jit(solution)/shard_map/ppermute | solution.py:55
  198.9 10.0 %collective-permute-start.71 = (bf16[64,512]{1,0:T(8,128)(2,1)S(1)}, bf16[64,512]{1,0:T(8,128)(2,1)S(1)}, u32[]{:S(2)}, u32[]{:S(2)}) collective-permute-start(bf16[64,512]{1,0:T(8,128)(2,1)S(1)} %get-tuple-element.275), channel_id=1, source_target_pairs={{0,6},{1,7},{2,4},{3,5},{4,2},{5,3},{6,0},{7,1},{8,14},{9,15},{10,... | collective-permute-start | bytes 196616 | tf_op jit(solution)/shard_map/ppermute | solution.py:55
  209.6 9.8 %collective-permute-start.74 = (bf16[64,1152]{1,0:T(8,128)(2,1)S(1)}, bf16[64,1152]{1,0:T(8,128)(2,1)S(1)}, u32[]{:S(2)}, u32[]{:S(2)}) collective-permute-start(bf16[64,1152]{1,0:T(8,128)(2,1)S(1)} %get-tuple-element.292), channel_id=1, source_target_pairs={{8,0},{0,8},{24,16},{9,1},{1,9},{25,17},{10,2},{2,10},{26,18},{11,... | collective-permute-start | bytes 442376 | tf_op jit(solution)/shard_map/ppermute | solution.py:1544
  212.1 10.2 %collective-permute-start.75 = (bf16[64,1152]{1,0:T(8,128)(2,1)S(1)}, bf16[64,1152]{1,0:T(8,128)(2,1)S(1)}, u32[]{:S(2)}, u32[]{:S(2)}) collective-permute-start(bf16[64,1152]{1,0:T(8,128)(2,1)S(1)} %get-tuple-element.293), channel_id=1, source_target_pairs={{16,0},{24,8},{0,16},{17,1},{25,9},{1,17},{18,2},{26,10},{2,18},{1... | collective-permute-start | bytes 442376 | tf_op jit(solution)/shard_map/ppermute | solution.py:1544
  213.4 8.9 %collective-permute-start.76 = (bf16[64,1152]{1,0:T(8,128)(2,1)S(1)}, bf16[64,1152]{1,0:T(8,128)(2,1)S(1)}, u32[]{:S(2)}, u32[]{:S(2)}) collective-permute-start(bf16[64,1152]{1,0:T(8,128)(2,1)S(1)} %get-tuple-element.294), channel_id=1, source_target_pairs={{24,0},{16,8},{8,16},{25,1},{17,9},{9,17},{26,2},{18,10},{10,18},{... | collective-permute-start | bytes 442376 | tf_op jit(solution)/shard_map/ppermute | solution.py:1544
  (53 other events, 313.7 us)

commit v3 on v2

--- a/solution.py
+++ b/solution.py
@@ -156,17 +156,17 @@
     flat[...] = image[...].reshape(flat.shape)
 
 
-def note_kernel(pairing, queue, out):
+def note_kernel(place, pairing, queue, keep, send):
     size = queue.shape[1]
-    for c in range(CROPS):
-        out[c * size : (c + 1) * size, :] = queue[c]
     row = lax.broadcasted_iota(jnp.int32, (16, PROJ), 0)
     lane = lax.broadcasted_iota(jnp.int32, (16, PROJ), 1)
     value = jnp.zeros((16, PROJ), F32)
     for m in range(pairing.shape[0]):
         for i in range(pairing.shape[1]):
             value = jnp.where((row == m) & (lane == i), pairing[m, i].astype(F32), value)
-    out[CROPS * size :, :] = value.astype(BF16)
+    for core, out in ((place[4], keep), (place[5], send)):
+        out[:size, :] = queue[core]
+        out[size:, :] = value.astype(BF16)
 
 
 def rows_kernel(*refs):
@@ -676,10 +676,9 @@
     row = lax.broadcasted_iota(jnp.int32, (PROJ, half), 0)
     lane = lax.broadcasted_iota(jnp.int32, (PROJ, half), 1)
     for ref in refs[:-5]:
-        rows = CROPS * size + 16
+        rows = size + 16
         for j in range(ref.shape[0] // rows):
-            mine = pl.ds(pl.multiple_of(j * rows + place[4] * size, 16), size)
-            rows_s[lanes_at(place[7] ^ told_offsets[at], size), :] = ref[mine, :]
+            rows_s[lanes_at(place[7] ^ told_offsets[at], size), :] = ref[j * rows : j * rows + size, :]
             pairs = ref[(j + 1) * rows - 16 : (j + 1) * rows, :]
             spot_at = (place[7] ^ told_offsets[at]) * images
             spot = ((row < images) & (lane == row + spot_at)).astype(F32).astype(BF16)
@@ -701,7 +700,7 @@
 
     sums = lax.fori_loop(0, steps, scored, jnp.zeros((1, 4 * QUARTER_PAD), F32))
     column[...] = jnp.broadcast_to(sums, column.shape)
-    factor = jnp.where(valid, 1.0 / sums, 0.0)
+    factor = jnp.where(valid & (sums > 1.18e-38), 1.0 / sums, 0.0)
 
     def divide(i, carry):
         mass[lanes_at(i, step), :] = (exps[lanes_at(i, step), :] * factor).astype(BF16)
@@ -1161,20 +1160,21 @@
     return value if isinstance(value, int) else pl.multiple_of(value, step)
 
 
-def pair_kernel(place, a, b, keep, out, full):
-    full[...] = dot_tn(a[...], b[...])
+def pair_kernel(place, a, b, keep, out):
+    full = dot_tn(a[...], b[...])
     own = keep.shape[1]
+    first = place[4] == 0
     for z in range(keep.shape[0]):
-        mine = (2 * z + place[4]) * own
-        other = (2 * z + place[5]) * own
-        keep[z] = full[pl.ds(pl.multiple_of(mine, own), own), :]
-        out[z] = full[pl.ds(pl.multiple_of(other, own), own), :].astype(BF16)
-
-
-def image_pair_kernel(place, d0, d1, d2, d3, image, keep, out, d_full, full):
+        one = full[2 * z * own : (2 * z + 1) * own]
+        two = full[(2 * z + 1) * own : (2 * z + 2) * own]
+        keep[z] = jnp.where(first, one, two)
+        out[z] = jnp.where(first, two, one).astype(BF16)
+
+
+def image_pair_kernel(place, d0, d1, d2, d3, image, keep, out, d_full):
     fill(place, (d0, d1, d2, d3), d_full)
     lanes = pl.ds(pl.multiple_of(place[0] * WIDE, WIDE), WIDE)
-    pair_kernel(place, d_full, image.at[:, lanes], keep, out, full)
+    pair_kernel(place, d_full, image.at[:, lanes], keep, out)
 
 
 def cross_kernel(place, keep, came, own, o1, o2, o3):
@@ -1183,14 +1183,14 @@
         o[...] = (keep[z] + came[z].astype(F32)).astype(o.dtype)
 
 
-def near_kernel(place, keep, came, kept, out):
+def far_kernel(place, keep, came, kept, out):
     for j in range(2):
-        mine, other = place[6] ^ (2 * j), place[6] ^ (2 * j + 1)
+        mine, other = place[6] ^ j, place[6] ^ (2 + j)
         kept[j] = keep[mine] + came[mine].astype(F32)
         out[j] = (keep[other] + came[other].astype(F32)).astype(BF16)
 
 
-def far_kernel(keep, came, kept, out):
+def near_kernel(keep, came, kept, out):
     kept[...] = keep[0] + came[0].astype(F32)
     out[...] = (keep[1] + came[1].astype(F32)).astype(BF16)
 
@@ -1235,12 +1235,17 @@
         image.transpose(0, 1, 3, 4, 2, 5).reshape(rows // images, images, D),
         us=2,
     )
-    queue_size = CROPS * queue.shape[1]
-    note = call(note_kernel, shape((queue_size + 16, PROJ), BF16), pairing, queue, us=0.5)
-    steps = [1 << bit for bit in range(ndp.bit_length() - 1)]
-    told, told_offsets = gather_dp(note, [(step,) for step in steps[:-1]])
-    *came, flat, told[0] = lax.optimization_barrier((*came, flat, *told))[:6]
-    told, told_offsets = [rows_of(told)], [sum(told_offsets, [])]
+    head_rows = rows // PLACES * ndp
+    small = ndp == 8 and head_rows <= 128 and images == 4 and queue.shape[1] * ndp <= 512
+    told, told_offsets = [flat], []
+    if small:
+        note = [shape((queue.shape[1] + 16, PROJ), BF16)] * 2
+        keep, out = call(note_kernel, note, place, pairing, queue, us=0.5)
+        told, told_offsets = [rows_of([keep, flip(out, "dp", 1)])], [0, 1]
+        told = [rows_of([told[0], flip(told[0], "dp", 2)])]
+        told_offsets = told_offsets + [offset ^ 2 for offset in told_offsets]
+    natural = unpack(packed, FIRST)
+    *came, flat, told[0], natural = lax.optimization_barrier((*came, flat, told[0], natural))
     conv_part, pair_part = call(
         pick_kernel,
         (shape((QUARTER_CONV, PART), BF16), shape((HALF_REDUCE + 4 * HALF_EXPAND, PART), BF16)),
@@ -1258,8 +1263,9 @@
 
     conv_part = rows_of([conv_part, after(conv_near, active0)])
     w_conv = (conv_part, flip(conv_part, "dp", 1))
-    told.append(flip(after(told[0], active0), "dp", steps[-1]))
-    told_offsets.append([offset ^ steps[-1] for offset in told_offsets[0]])
+    if small:
+        told.append(flip(after(told[0], active0), "dp", 4))
+        told_offsets = told_offsets + [offset ^ 4 for offset in told_offsets]
     w_proj, table = pl.pallas_call(
         tables_kernel,
         name="tables",
@@ -1277,8 +1283,8 @@
     back_own = call(
         back_parts_kernel, [shape((back_rows, PART), BF16)] * 4, place, *w_conv, *pair_parts, us=1
     )
-    joined = lax.optimization_barrier((*actives0, table, taps, told[1], *back_own))
-    actives0, (table, taps, told[1]), back_own = joined[:4], joined[4:7], joined[7:]
+    joined = lax.optimization_barrier((*actives0, table, taps, told[-1], *back_own))
+    actives0, (table, taps, told[-1]), back_own = joined[:4], joined[4:7], joined[7:]
     pre1, part = call(
         k(conv_kernel, micro, images),
         (pieces_of(PART, F32), sums_of),
@@ -1289,19 +1295,16 @@
     sums1 = sum_dp(part)
     active1_own = call(k(active_kernel, micro, count), pieces_of(PART, BF16), pre1, sums1, conv_part, us=1)
     actives1 = gather_xor(active1_own, "section")
-    natural = unpack(after(packed, active1_own), FIRST)
-    head_rows = rows // PLACES * ndp
     lanes = 4 * QUARTER_PAD
     stages = dp_stages()
     head_stages = stages[1:] + stages[:1]
     offsets = [0]
     for steps in head_stages:
         offsets = offsets + [o ^ step for step in steps for o in offsets]
-    small = head_rows <= 128 and images * ndp == 32 and queue.shape[1] * ndp <= 512
     if small:
         queued = ndp * queue.shape[1]
         mass, column, match = call(
-            k(mass_kernel, micro, images, sum(told_offsets, [])),
+            k(mass_kernel, micro, images, told_offsets),
             (
                 shape((queued, lanes), BF16), shape((8, lanes), F32),
                 shape((micro, images * ndp, images * ndp), BF16),
@@ -1310,9 +1313,8 @@
             scratch=[pltpu.VMEM((queued, PROJ), BF16), pltpu.VMEM((queued, lanes), F32)],
             vmem=16, us=5,
         )
-    joined = lax.optimization_barrier((*actives1, natural, *([mass] if small else [])))
-    actives1, natural = joined[:4], joined[4]
-    mass = joined[5] if small else None
+    if small:
+        *actives1, mass = lax.optimization_barrier((*actives1, mass))
     active1, pre2, part, w_expand = call(
         k(expand_kernel, micro),
         (pieces_of(WIDTH, BF16), pieces_of(WIDE, F32), shape((8, WIDE), F32), shape((WIDTH, WIDE), BF16)),
@@ -1365,18 +1367,13 @@
         group, single = inner // images, inner % images
         position = (group * ndp + (offset[block] ^ dp)) * images + single
         order = (position[None, :] == head_order[:, None]).astype(BF16)
-        told = jnp.concatenate(told).reshape(ndp, queue_size + 16, PROJ)
-        pairs = told[:, queue_size : queue_size + micro, :images].astype(jnp.int32)
-        told_offset = jnp.array(sum(told_offsets, []), jnp.int32)
-        pairs_dp = (told_offset ^ dp)[None, :] == jnp.arange(ndp, dtype=jnp.int32)[:, None]
-        pairs = jnp.sum(jnp.where(pairs_dp[:, :, None, None], pairs[None], 0), axis=1)
+        pairs = lax.all_gather(pairing.astype(F32), "dp").astype(jnp.int32)
         left = jnp.arange(images * ndp, dtype=jnp.int32)
         pairs = pairs.transpose(1, 0, 2).reshape(micro, ndp * images)
         match = ((left // images * images + pairs)[:, :, None] == left[None, None, :]).astype(F32)
         all_pooled = dot(order, all_pooled).astype(BF16)
         protos = jnp.concatenate([table[:, a * PROJ : (a + 1) * PROJ] for a in range(4)], axis=0)
-        queue_all = told[:, :queue_size].reshape(ndp, CROPS, queue.shape[1], PROJ)
-        queue_rows = queue_all.transpose(1, 0, 2, 3).reshape(CROPS, -1, PROJ)
+        queue_rows = lax.all_gather(queue, "dp", axis=1, tiled=True)
         loss, grads3, active3, unit, d_scores, d_embed, d_pre3 = head(
             all_pooled, natural, w_proj, protos, norm3[:, 0], queue_rows, match, micro, images, dp
         )
@@ -1398,6 +1395,7 @@
         us=1.8,
     )
     back2 = sum_dp(part)
+    back2, *back_halves = lax.optimization_barrier((back2, *back_halves))
     d_pre2, *partial = call(
         k(expand_back_kernel, micro, count),
         [pieces_of(WIDE, BF16)] + [pieces_of(PART, BF16)] * 4,
@@ -1414,7 +1412,6 @@
             pair_kernel,
             (shape((4, own, width), F32), shape((4, own, width), BF16)),
             place, a, b,
-            scratch=[pltpu.VMEM((WIDTH, width), F32)],
             us=2.5,
         )
         return keep, flip(out, "dp", 1)
@@ -1431,25 +1428,25 @@
         )
         return [kept] + [flip(out[j], "dp", 2 * (j + 1)) for j in range(3)]
 
-    def scatter_near(started, *others):
+    def scatter_far(started, *others):
         if ndp != 8:
             return lax.psum_scatter(started.astype(BF16), "dp", scatter_dimension=0, tiled=True), None
         keep, came = started
         if others:
             keep = after(keep, *others)
         dims = (2, *keep.shape[1:])
-        kept, out = call(near_kernel, (shape(dims, F32), shape(dims, BF16)), place, keep, came, us=0.7)
-        return kept, flip(out, "dp", 2)
-
-    def scatter_far(started, *others):
+        kept, out = call(far_kernel, (shape(dims, F32), shape(dims, BF16)), place, keep, came, us=0.7)
+        return kept, flip(out, "dp", 4)
+
+    def scatter_near(started, *others):
         if ndp != 8:
             return started
         keep, came = started
         if others:
             keep = after(keep, *others)
         dims = keep.shape[1:]
-        kept, out = call(far_kernel, (shape(dims, F32), shape(dims, BF16)), keep, came, us=0.5)
-        return kept, flip(out, "dp", 4)
+        kept, out = call(near_kernel, (shape(dims, F32), shape(dims, BF16)), keep, came, us=0.5)
+        return kept, flip(out, "dp", 2)
 
     def scatter_last(started):
         if ndp != 8:
@@ -1461,15 +1458,15 @@
             return crossed[0].astype(BF16)
         return call(add_kernel, shape(crossed[0].shape, BF16), *crossed, us=0.6)
 
-    expand_near = scatter_near(scatter_start(d_pre2, active1, WIDTH))
+    expand_half = scatter_far(scatter_start(d_pre2, active1, WIDTH))
     tail = call(
         tail_grads_kernel,
         shape((own, WIDTH + QUARTER_PAD), F32),
         place, after(active3, d_pre2), unit, d_scores, flip(d_scores, "dp", 1), d_embed,
         us=3,
     )
-    joined = lax.optimization_barrier((*partial, tail, *expand_near[: 2 if ndp == 8 else 1]))
-    partial, tail, expand_near = joined[:SECTIONS], joined[SECTIONS], joined[SECTIONS + 1 :]
+    joined = lax.optimization_barrier((*partial, tail, *expand_half[: 2 if ndp == 8 else 1]))
+    partial, tail, expand_half = joined[:SECTIONS], joined[SECTIONS], joined[SECTIONS + 1 :]
 
     d_y1, part = call(
         k(silu_back_kernel, micro, count),
@@ -1481,7 +1478,7 @@
         k(norm_back_kernel, micro, count), pieces_of(PART, BF16), d_y1, pre1, sums1, back1, conv_part
     )
     d_pre1s = gather_xor(d_pre1_own, "section")
-    expand_far = scatter_far(expand_near, d_pre1_own)
+    expand_last = scatter_near(expand_half, d_pre1_own)
     base = call(
         head_grads_kernel,
         shape((own, param_rows), F32),
@@ -1489,8 +1486,8 @@
         scratch=[pltpu.VMEM((4 * own, D), BF16)],
         us=4,
     )
-    joined = lax.optimization_barrier((*d_pre1s, base, *expand_far))
-    d_pre1s, base, expand_far = joined[:SECTIONS], joined[SECTIONS], joined[SECTIONS + 1 :]
+    joined = lax.optimization_barrier((*d_pre1s, base, *expand_last))
+    d_pre1s, base, expand_last = joined[:SECTIONS], joined[SECTIONS], joined[SECTIONS + 1 :]
     d_pre1, d_y0, part = call(
         k(conv_back_kernel, micro, images, count),
         (pieces_of(WIDTH, BF16), pieces_of(PART, F32), sums_of),
@@ -1506,17 +1503,18 @@
         place, d_y0, pre0, sums0, back0, pair_part, back2, back1, notes3,
     )
     d_pre0s = gather_xor(d_pre0_own, "section")
-    conv_near_sum = scatter_near(conv_started, d_pre0_own)
-    joined = lax.optimization_barrier((*d_pre0s, conv_near_sum[0]))
-    d_pre0s, conv_near_sum = joined[:SECTIONS], (joined[SECTIONS], conv_near_sum[1])
-    conv_far = scatter_far(conv_near_sum)
+    conv_half = scatter_far(conv_started)
+    joined = lax.optimization_barrier((*d_pre0s, conv_half[0]))
+    d_pre0s, conv_half = joined[:SECTIONS], (joined[SECTIONS], conv_half[1])
+    conv_last = scatter_near(conv_half)
+    joined = lax.optimization_barrier((*d_pre0s, conv_last[0]))
+    d_pre0s, conv_last = joined[:SECTIONS], (joined[SECTIONS], conv_last[1])
 
     if ndp == 8:
         keep, out, d_pre0 = call(
             image_pair_kernel,
             (shape((4, own, WIDE), F32), shape((4, own, WIDE), BF16), pieces_of(WIDTH, BF16)),
             place, *d_pre0s, flat,
-            scratch=[pltpu.VMEM((WIDTH, WIDE), F32)],
             us=2.5,
         )
         reduce_started = keep, flip(out, "dp", 1)
@@ -1534,8 +1532,8 @@
     norm_grads, loss = call(
         told_kernel, (shape((3, 1, D), F32), shape((8, PROJ), F32)), place, *d_pre0s, notes3, us=0.5
     )
-    g_conv = scatter_last(conv_far)
-    g_expand = scatter_last(expand_far)
+    g_conv = scatter_last(conv_last)
+    g_expand = scatter_last(expand_last)
     joined = lax.optimization_barrier((*reduce_crossed, grad_in, norm_grads, g_conv, g_expand))
     *reduce_crossed, grad_in, norm_grads, g_conv, g_expand = joined
     g_reduce = scatter_finish(reduce_crossed)

time: 226 us -> 224 us (level)
  starting transfers between devices: 97.3 us -> 95 us
    ppermute x71, starting transfers between devices: 78.8 us -> 76.3 us  [flip(): lax.ppermute(value, axis, [(source, source ^ step) for source in range(co...]
  transfers between devices with their start and end apart: 77 -> 77, of which waited for: 45 -> 46; matrix products, arithmetic and copies ran while one was open for 0% -> 0% of each run, Pallas kernels for 19% -> 19%
where the time goes in v3:
time: 224 us; the launch traced here: 222 us
  starting transfers between devices  95 us (42%)
  waiting for transfers between devices  65.2 us (29%)
  Pallas kernels  59 us (26%)
    ppermute x71, starting transfers between devices, flip(): lax.ppermute(value, axis, [(source, source ^ step) for source in range(co...  76.3 us
    ppermute x71, waiting for transfers between devices, flip(): lax.ppermute(value, axis, [(source, source ^ step) for source in range(co...  61.9 us
    pallas_call x42, Pallas kernels, call(): pl.pallas_call(kernel, name=getattr(kernel, 'func', kernel).__name__, out...  49.7 us
    ppermute x3, starting transfers between devices, body(): lax.ppermute(messages[j - 1], 'section', [(u, u ^ j) for u in range(3)])  9.48 us
    ppermute x3, starting transfers between devices, body(): lax.ppermute(mixed[j - 1], 'section', [(u ^ j, u) for u in range(3)])  9.21 us
  transfers between devices with their start and end apart: 77, of which 46 were waited for; matrix products, arithmetic and copies ran while one was open for 0% of the time, Pallas kernels for 19%

profile of v3, /device:TPU:2, one launch (start us, length us, event | category | flops | bytes accessed | tf_op | source)
XLA Modules:
  0.0 222.0 jit_solution(5348034251521322666)
XLA Ops:
  1.5 2.3 %pack.1 = (bf16[1168,128]{1,0:T(8,128)(2,1)S(1)}, bf16[1168,128]{1,0:T(8,128)(2,1)S(1)}, bf16[1168,128]{1,0:T(8,128)(2,1)S(1)}, bf16[1168,128]{1,0:T(8,128)(2,1)S(1)}) custom-call(s32[9]{0:T(128)S(1)} %stack.39.place, bf16[9456,512]{1,0:T(8,128)(2,1)} %bitcast.22, f32[3,1,2048]{2,1,0:T(1,128)S(1)} %bitcast.26), custom_call_target="tpu_custom_call" | custom-call | bytes 6000000 | tf_op jit(solution)/shard_map/pack/pallas_call | solution.py:1141
  3.9 2.2 collective-permute-start
  7.5 5.8 %collective-permute-start.2 = (bf16[1168,128]{1,0:T(8,128)(2,1)S(1)}, bf16[1168,128]{1,0:T(8,128)(2,1)S(1)}, u32[]{:S(2)}, u32[]{:S(2)}) collective-permute-start(bf16[1168,128]{1,0:T(8,128)(2,1)S(1)} %get-tuple-element.161), channel_id=1, source_target_pairs={{0,24},{8,16},{16,8},{1,25},{9,17},{17,9},{2,26},{10,18},{18,10},{... | collective-permute-start | bytes 897032 | tf_op jit(solution)/shard_map/ppermute | solution.py:1232
  16.8 3.6 %unpack.1.w_head = bf16[2048,2048]{1,0:T(8,128)(2,1)S(1)} custom-call(bf16[9456,512]{1,0:T(8,128)(2,1)S(1)} %bitcast.24), custom_call_target="tpu_custom_call" | custom-call | bytes 12000000 | tf_op jit(solution)/shard_map/unpack/pallas_call | solution.py:1068
  26.3 3.6 %collective-permute-start.9 = (f32[8,128]{1,0:T(8,128)S(1)}, f32[8,128]{1,0:T(8,128)S(1)}, u32[]{:S(2)}, u32[]{:S(2)}) collective-permute-start(f32[8,128]{1,0:T(8,128)S(1)} %add.82), channel_id=1, source_target_pairs={{0,6},{1,7},{2,4},{3,5},{4,2},{5,3},{6,0},{7,1},{8,14},{9,15},{10,... | collective-permute-start | bytes 12296 | tf_op jit(solution)/shard_map/ppermute | solution.py:55
  30.6 2.6 %collective-permute-done.9 = f32[8,128]{1,0:T(8,128)S(1)} collective-permute-done((f32[8,128]{1,0:T(8,128)S(1)}, f32[8,128]{1,0:T(8,128)S(1)}, u32[]{:S(2)}, u32[]{:S(2)}) %collective-permute-start.9) | collective-permute-done | bytes 4128 | tf_op jit(solution)/shard_map/ppermute | solution.py:55
  34.6 4.0 %collective-permute-start.12 = (bf16[784,128]{1,0:T(8,128)(2,1)S(1)}, bf16[784,128]{1,0:T(8,128)(2,1)S(1)}, u32[]{:S(2)}, u32[]{:S(2)}) collective-permute-start(bf16[784,128]{1,0:T(8,128)(2,1)S(1)} %active_kernel.2.active.a0), channel_id=1, source_target_pairs={{0,24},{8,16},{16,8},{24,0},{1,25},{9,17},{17,9},{25,1},{2,26},{10... | collective-permute-start | bytes 602120 | tf_op jit(solution)/shard_map/ppermute | solution.py:55
  39.2 2.0 collective-permute-start.13
  45.4 3.1 %collective-permute-done.11.a2 = bf16[784,128]{1,0:T(8,128)(2,1)S(1)} collective-permute-done((bf16[784,128]{1,0:T(8,128)(2,1)S(1)}, bf16[784,128]{1,0:T(8,128)(2,1)S(1)}, u32[]{:S(2)}, u32[]{:S(2)}) %collective-permute-start.11) | collective-permute-done | bytes 200736 | tf_op jit(solution)/shard_map/ppermute | solution.py:55
  48.5 2.2 conv_kernel.1
  53.9 2.4 %collective-permute-start.17 = (f32[8,128]{1,0:T(8,128)S(1)}, f32[8,128]{1,0:T(8,128)S(1)}, u32[]{:S(2)}, u32[]{:S(2)}) collective-permute-start(f32[8,128]{1,0:T(8,128)S(1)} %add.86), channel_id=1, source_target_pairs={{0,2},{1,3},{2,0},{3,1},{4,6},{5,7},{6,4},{7,5},{8,10},{9,11},{10,... | collective-permute-start | bytes 12296 | tf_op jit(solution)/shard_map/ppermute | solution.py:55
  61.6 3.1 %mass_kernel.1 = (bf16[512,3072]{1,0:T(8,128)(2,1)S(1)}, f32[8,3072]{1,0:T(8,128)S(1)}, bf16[2,32,32]{2,1,0:T(8,128)(2,1)S(1)}) custom-call(s32[9]{0:T(128)S(1)} %stack.39.place, bf16[768,512]{1,0:T(8,128)(2,1)S(1)} %get-tuple-element.189.table, bf16[320,128]{1,0:T(8,128)(2,1)S(1)} %rows_kernel.5.refs_0_, bf16[320,128]{1,0:T(8,128)(2,1)S(1)} %collective-permute-done.13.refs_1_), custom_call_target="tpu_custom_call" | custom-call | bytes 15000000 | tf_op jit(solution)/shard_map/mass_kernel/pallas_call | solution.py:139
  64.7 2.3 %collective-permute-done.22.a3 = bf16[784,128]{1,0:T(8,128)(2,1)S(1)} collective-permute-done((bf16[784,128]{1,0:T(8,128)(2,1)S(1)}, bf16[784,128]{1,0:T(8,128)(2,1)S(1)}, u32[]{:S(2)}, u32[]{:S(2)}) %collective-permute-start.22) | collective-permute-done | bytes 200736 | tf_op jit(solution)/shard_map/ppermute | solution.py:55
  67.0 2.3 %collective-permute-done.21.a2 = bf16[784,128]{1,0:T(8,128)(2,1)S(1)} collective-permute-done((bf16[784,128]{1,0:T(8,128)(2,1)S(1)}, bf16[784,128]{1,0:T(8,128)(2,1)S(1)}, u32[]{:S(2)}, u32[]{:S(2)}) %collective-permute-start.21) | collective-permute-done | bytes 200736 | tf_op jit(solution)/shard_map/ppermute | solution.py:55
  71.9 2.0 collective-permute-start.26
  98.6 10.9 %head_kernel.1 = (bf16[128,2048]{1,0:T(8,128)(2,1)S(1)}, bf16[128,2048]{1,0:T(8,128)(2,1)S(1)}, bf16[128,128]{1,0:T(8,128)(2,1)S(1)}, bf16[64,3072]{1,0:T(8,128)...) custom-call(s32[9]{0:T(128)S(1)} %stack.39.place, ...), custom_call_target="tpu_custom_call" | custom-call | bytes 36000000 | tf_op jit(solution)/shard_map/head_kernel/pallas_call | solution.py:139
  110.8 4.5 %head_back_kernel.1 = (bf16[16,512]{1,0:T(8,128)(2,1)S(1)}, bf16[16,512]{1,0:T(8,128)(2,1)S(1)}, bf16[16,512]{1,0:T(8,128)(2,1)S(1)}, bf16[16,512]{1,0:T(8,128)(...) custom-call(s32[9]{0:T(128)S(1)} %stack.39.place, ...), custom_call_target="tpu_custom_call" | custom-call | bytes 15000000 | tf_op jit(solution)/shard_map/head_back_kernel/pallas_call | solution.py:139
  124.9 2.1 collective-permute-start.44
  138.7 2.1 collective-permute-start.51
  142.4 4.9 %collective-permute-done.47.q2 = bf16[784,128]{1,0:T(8,128)(2,1)S(1)} collective-permute-done((bf16[784,128]{1,0:T(8,128)(2,1)S(1)}, bf16[784,128]{1,0:T(8,128)(2,1)S(1)}, u32[]{:S(2)}, u32[]{:S(2)}) %collective-permute-start.47) | collective-permute-done | bytes 200736 | tf_op jit(solution)/shard_map/ppermute | solution.py:55
  160.8 2.1 head_grads_kernel.1.base
  164.3 2.2 %collective-permute-done.57.d2 = bf16[784,128]{1,0:T(8,128)(2,1)S(1)} collective-permute-done((bf16[784,128]{1,0:T(8,128)(2,1)S(1)}, bf16[784,128]{1,0:T(8,128)(2,1)S(1)}, u32[]{:S(2)}, u32[]{:S(2)}) %collective-permute-start.57) | collective-permute-done | bytes 200736 | tf_op jit(solution)/shard_map/ppermute | solution.py:55
  166.6 2.4 %conv_back_kernel.1 = (bf16[784,512]{1,0:T(8,128)(2,1)S(1)}, f32[784,128]{1,0:T(8,128)S(1)}, f32[8,128]{1,0:T(8,128)S(1)}) custom-call(s32[9]{0:T(128)S(1)} %stack.39.place, bf16[784,128]{1,0:T(8,128)(2,1)S(1)} %norm_back_kernel.1.d0, bf16[784,128]{1,0:T(8,128)(2,1)S(1)} %collective-permute-done.56.d1, bf16[784,128]{1,0:T(8,128)(2,1)S(1)} %collective-permute-done.57.d2, ...), custom_call_target="tpu_custom_call" | custom-call | bytes 10500000 | tf_op jit(solution)/shard_map/conv_back_kernel/pallas_call | solution.py:139
  169.0 2.1 pair_kernel.3
  173.2 2.0 collective-permute-start.63
  184.0 5.6 %collective-permute-done.66.n3.d3 = bf16[832,128]{1,0:T(8,128)(2,1)S(1)} collective-permute-done((bf16[832,128]{1,0:T(8,128)(2,1)S(1)}, bf16[832,128]{1,0:T(8,128)(2,1)S(1)}, u32[]{:S(2)}, u32[]{:S(2)}) %collective-permute-start.66) | collective-permute-done | bytes 213024 | tf_op jit(solution)/shard_map/ppermute | solution.py:55
  189.6 2.4 %collective-permute-done.65.n2.d2 = bf16[832,128]{1,0:T(8,128)(2,1)S(1)} collective-permute-done((bf16[832,128]{1,0:T(8,128)(2,1)S(1)}, bf16[832,128]{1,0:T(8,128)(2,1)S(1)}, u32[]{:S(2)}, u32[]{:S(2)}) %collective-permute-start.65) | collective-permute-done | bytes 213024 | tf_op jit(solution)/shard_map/ppermute | solution.py:55
  199.9 2.0 collective-permute-start.72
  203.2 2.5 %reduce_back_kernel.1 = f32[196,4,512]{2,1,0:T(4,128)} custom-call(s32[9]{0:T(128)S(1)} %stack.39.place, bf16[784,512]{1,0:T(8,128)(2,1)S(1)} %get-tuple-element.294.d_full, bf16[4,832,128]{2,1,0:T(8,128)(2,1)S(1)} %stack_kernel.1.back0, bf16[4,832,128]{2,1,0:T(8,128)(2,1)S(1)} %collective-permute-done.45.back1, f32[784,512]{1,0:T(8,128)S(1)} %get-tuple-element.224.d_z), custom_call_target="tpu_custom_call" | custom-call | bytes 6000000 | tf_op jit(solution)/shard_map/reduce_back_kernel/pallas_call | solution.py:139
  207.1 3.1 %collective-permute-start.74 = (bf16[64,1152]{1,0:T(8,128)(2,1)S(1)}, bf16[64,1152]{1,0:T(8,128)(2,1)S(1)}, u32[]{:S(2)}, u32[]{:S(2)}) collective-permute-start(bf16[64,1152]{1,0:T(8,128)(2,1)S(1)} %get-tuple-element.308), channel_id=1, source_target_pairs={{8,0},{0,8},{24,16},{9,1},{1,9},{25,17},{10,2},{2,10},{26,18},{11,... | collective-permute-start | bytes 442376 | tf_op jit(solution)/shard_map/ppermute | solution.py:1542
  211.5 4.8 %collective-permute-start.76 = (bf16[64,1152]{1,0:T(8,128)(2,1)S(1)}, bf16[64,1152]{1,0:T(8,128)(2,1)S(1)}, u32[]{:S(2)}, u32[]{:S(2)}) collective-permute-start(bf16[64,1152]{1,0:T(8,128)(2,1)S(1)} %get-tuple-element.310), channel_id=1, source_target_pairs={{24,0},{16,8},{8,16},{25,1},{17,9},{9,17},{26,2},{18,10},{10,18},{... | collective-permute-start | bytes 442376 | tf_op jit(solution)/shard_map/ppermute | solution.py:1542
  216.8 3.3 %collective-permute-done.75.m2 = bf16[64,1152]{1,0:T(8,128)(2,1)S(1)} collective-permute-done((bf16[64,1152]{1,0:T(8,128)(2,1)S(1)}, bf16[64,1152]{1,0:T(8,128)(2,1)S(1)}, u32[]{:S(2)}, u32[]{:S(2)}) %collective-permute-start.75) | collective-permute-done | bytes 147488 | tf_op jit(solution)/shard_map/ppermute | solution.py:1542
  (194 shorter events, 118.0 us)
Async XLA Ops:
  3.9 16.9 %collective-permute-start = (bf16[1168,128]{1,0:T(8,128)(2,1)S(1)}, bf16[1168,128]{1,0:T(8,128)(2,1)S(1)}, u32[]{:S(2)}, u32[]{:S(2)}) collective-permute-start(bf16[1168,128]{1,0:T(8,128)(2,1)S(1)} %get-tuple-element.159), channel_id=1, source_target_pairs={{0,8},{8,0},{16,24},{1,9},{9,1},{17,25},{2,10},{10,2},{18,26},{3,1... | collective-permute-start | bytes 897032 | tf_op jit(solution)/shard_map/ppermute | solution.py:1232
  6.0 14.7 %collective-permute-start.1 = (bf16[1168,128]{1,0:T(8,128)(2,1)S(1)}, bf16[1168,128]{1,0:T(8,128)(2,1)S(1)}, u32[]{:S(2)}, u32[]{:S(2)}) collective-permute-start(bf16[1168,128]{1,0:T(8,128)(2,1)S(1)} %get-tuple-element.160), channel_id=1, source_target_pairs={{0,16},{8,24},{16,0},{1,17},{9,25},{17,1},{2,18},{10,26},{18,2},{3... | collective-permute-start | bytes 897032 | tf_op jit(solution)/shard_map/ppermute | solution.py:1232
  7.5 13.2 %collective-permute-start.2 = (bf16[1168,128]{1,0:T(8,128)(2,1)S(1)}, bf16[1168,128]{1,0:T(8,128)(2,1)S(1)}, u32[]{:S(2)}, u32[]{:S(2)}) collective-permute-start(bf16[1168,128]{1,0:T(8,128)(2,1)S(1)} %get-tuple-element.161), channel_id=1, source_target_pairs={{0,24},{8,16},{16,8},{1,25},{9,17},{17,9},{2,26},{10,18},{18,10},{... | collective-permute-start | bytes 897032 | tf_op jit(solution)/shard_map/ppermute | solution.py:1232
  21.6 12.9 %collective-permute-start.14 = (bf16[1168,128]{1,0:T(8,128)(2,1)S(1)}, bf16[1168,128]{1,0:T(8,128)(2,1)S(1)}, u32[]{:S(2)}, u32[]{:S(2)}) collective-permute-start(bf16[1168,128]{1,0:T(8,128)(2,1)S(1)} %get-tuple-element.176.refs_0_), channel_id=1, source_target_pairs={{0,2},{1,3},{2,0},{3,1},{4,6},{5,7},{6,4},{7,5},{8,10},{9,11},{10,... | collective-permute-start | bytes 897032 | tf_op jit(solution)/shard_map/ppermute | solution.py:55
  34.6 9.0 %collective-permute-start.15 = (bf16[2336,128]{1,0:T(8,128)(2,1)S(1)}, bf16[2336,128]{1,0:T(8,128)(2,1)S(1)}, u32[]{:S(2)}, u32[]{:S(2)}) collective-permute-start(bf16[2336,128]{1,0:T(8,128)(2,1)S(1)} %rows_kernel.6.conv_a.wa.told), channel_id=1, source_target_pairs={{0,1},{1,0},{2,3},{3,2},{4,5},{5,4},{6,7},{7,6},{8,9},{9,8},{10,11... | collective-permute-start | bytes 1794056 | tf_op jit(solution)/shard_map/ppermute | solution.py:55
  34.6 10.7 %collective-permute-start.12 = (bf16[784,128]{1,0:T(8,128)(2,1)S(1)}, bf16[784,128]{1,0:T(8,128)(2,1)S(1)}, u32[]{:S(2)}, u32[]{:S(2)}) collective-permute-start(bf16[784,128]{1,0:T(8,128)(2,1)S(1)} %active_kernel.2.active.a0), channel_id=1, source_target_pairs={{0,24},{8,16},{16,8},{24,0},{1,25},{9,17},{17,9},{25,1},{2,26},{10... | collective-permute-start | bytes 602120 | tf_op jit(solution)/shard_map/ppermute | solution.py:55
  38.6 9.9 %collective-permute-start.11 = (bf16[784,128]{1,0:T(8,128)(2,1)S(1)}, bf16[784,128]{1,0:T(8,128)(2,1)S(1)}, u32[]{:S(2)}, u32[]{:S(2)}) collective-permute-start(bf16[784,128]{1,0:T(8,128)(2,1)S(1)} %active_kernel.2.active.a0), channel_id=1, source_target_pairs={{0,16},{8,24},{16,0},{24,8},{1,17},{9,25},{17,1},{25,9},{2,18},{10... | collective-permute-start | bytes 602120 | tf_op jit(solution)/shard_map/ppermute | solution.py:55
  38.6 9.9 %collective-permute-start.10 = (bf16[784,128]{1,0:T(8,128)(2,1)S(1)}, bf16[784,128]{1,0:T(8,128)(2,1)S(1)}, u32[]{:S(2)}, u32[]{:S(2)}) collective-permute-start(bf16[784,128]{1,0:T(8,128)(2,1)S(1)} %active_kernel.2.active.a0), channel_id=1, source_target_pairs={{0,8},{8,0},{16,24},{24,16},{1,9},{9,1},{17,25},{25,17},{2,10},{10... | collective-permute-start | bytes 602120 | tf_op jit(solution)/shard_map/ppermute | solution.py:55
  58.1 8.9 %collective-permute-start.22 = (bf16[784,128]{1,0:T(8,128)(2,1)S(1)}, bf16[784,128]{1,0:T(8,128)(2,1)S(1)}, u32[]{:S(2)}, u32[]{:S(2)}) collective-permute-start(bf16[784,128]{1,0:T(8,128)(2,1)S(1)} %active_kernel.3.a0), channel_id=1, source_target_pairs={{0,24},{8,16},{16,8},{24,0},{1,25},{9,17},{17,9},{25,1},{2,26},{10... | collective-permute-start | bytes 602120 | tf_op jit(solution)/shard_map/ppermute | solution.py:55
  59.9 9.4 %collective-permute-start.21 = (bf16[784,128]{1,0:T(8,128)(2,1)S(1)}, bf16[784,128]{1,0:T(8,128)(2,1)S(1)}, u32[]{:S(2)}, u32[]{:S(2)}) collective-permute-start(bf16[784,128]{1,0:T(8,128)(2,1)S(1)} %active_kernel.3.a0), channel_id=1, source_target_pairs={{0,16},{8,24},{16,0},{24,8},{1,17},{9,25},{17,1},{25,9},{2,18},{10... | collective-permute-start | bytes 602120 | tf_op jit(solution)/shard_map/ppermute | solution.py:55
  61.4 7.9 %collective-permute-start.20 = (bf16[784,128]{1,0:T(8,128)(2,1)S(1)}, bf16[784,128]{1,0:T(8,128)(2,1)S(1)}, u32[]{:S(2)}, u32[]{:S(2)}) collective-permute-start(bf16[784,128]{1,0:T(8,128)(2,1)S(1)} %active_kernel.3.a0), channel_id=1, source_target_pairs={{0,8},{8,0},{16,24},{24,16},{1,9},{9,1},{17,25},{25,17},{2,10},{10... | collective-permute-start | bytes 602120 | tf_op jit(solution)/shard_map/ppermute | solution.py:55
  95.0 20.3 %collective-permute-start.35 = (bf16[832,128]{1,0:T(8,128)(2,1)S(1)}, bf16[832,128]{1,0:T(8,128)(2,1)S(1)}, u32[]{:S(2)}, u32[]{:S(2)}) collective-permute-start(bf16[832,128]{1,0:T(8,128)(2,1)S(1)} %get-tuple-element.217), channel_id=1, source_target_pairs={{0,8},{8,0},{16,24},{24,16},{1,9},{9,1},{17,25},{25,17},{2,10},{10... | collective-permute-start | bytes 638984 | tf_op jit(solution)/shard_map/ppermute | solution.py:55
  95.8 19.5 %collective-permute-start.36 = (bf16[832,128]{1,0:T(8,128)(2,1)S(1)}, bf16[832,128]{1,0:T(8,128)(2,1)S(1)}, u32[]{:S(2)}, u32[]{:S(2)}) collective-permute-start(bf16[832,128]{1,0:T(8,128)(2,1)S(1)} %get-tuple-element.218), channel_id=1, source_target_pairs={{0,16},{8,24},{16,0},{24,8},{1,17},{9,25},{17,1},{25,9},{2,18},{10... | collective-permute-start | bytes 638984 | tf_op jit(solution)/shard_map/ppermute | solution.py:55
  96.8 18.6 %collective-permute-start.37 = (bf16[832,128]{1,0:T(8,128)(2,1)S(1)}, bf16[832,128]{1,0:T(8,128)(2,1)S(1)}, u32[]{:S(2)}, u32[]{:S(2)}) collective-permute-start(bf16[832,128]{1,0:T(8,128)(2,1)S(1)} %get-tuple-element.219), channel_id=1, source_target_pairs={{0,24},{8,16},{16,8},{24,0},{1,25},{9,17},{17,9},{25,1},{2,26},{10... | collective-permute-start | bytes 638984 | tf_op jit(solution)/shard_map/ppermute | solution.py:55
  115.4 16.3 %collective-permute-start.45 = (bf16[4,832,128]{2,1,0:T(8,128)(2,1)S(1)}, bf16[4,832,128]{2,1,0:T(8,128)(2,1)S(1)}, u32[]{:S(2)}, u32[]{:S(2)}) collective-permute-start(bf16[4,832,128]{2,1,0:T(8,128)(2,1)S(1)} %stack_kernel.1.back0), channel_id=1, source_target_pairs={{0,1},{1,0},{2,3},{3,2},{4,5},{5,4},{6,7},{7,6},{8,9},{9,8},{10,11... | collective-permute-start | bytes 2555912 | tf_op jit(solution)/shard_map/ppermute | solution.py:55
  129.3 11.4 %collective-permute-start.49 = (bf16[64,3072]{1,0:T(8,128)(2,1)S(1)}, bf16[64,3072]{1,0:T(8,128)(2,1)S(1)}, u32[]{:S(2)}, u32[]{:S(2)}) collective-permute-start(bf16[64,3072]{1,0:T(8,128)(2,1)S(1)} %get-tuple-element.240.d_here), channel_id=1, source_target_pairs={{0,1},{1,0},{2,3},{3,2},{4,5},{5,4},{6,7},{7,6},{8,9},{9,8},{10,11... | collective-permute-start | bytes 1179656 | tf_op jit(solution)/shard_map/ppermute | solution.py:55
  135.9 11.4 %collective-permute-start.47 = (bf16[784,128]{1,0:T(8,128)(2,1)S(1)}, bf16[784,128]{1,0:T(8,128)(2,1)S(1)}, u32[]{:S(2)}, u32[]{:S(2)}) collective-permute-start(bf16[784,128]{1,0:T(8,128)(2,1)S(1)} %get-tuple-element.234), channel_id=1, source_target_pairs={{0,16},{8,24},{16,0},{24,8},{1,17},{9,25},{17,1},{25,9},{2,18},{10... | collective-permute-start | bytes 602120 | tf_op jit(solution)/shard_map/ppermute | solution.py:55
  137.0 10.3 %collective-permute-start.48 = (bf16[784,128]{1,0:T(8,128)(2,1)S(1)}, bf16[784,128]{1,0:T(8,128)(2,1)S(1)}, u32[]{:S(2)}, u32[]{:S(2)}) collective-permute-start(bf16[784,128]{1,0:T(8,128)(2,1)S(1)} %get-tuple-element.235), channel_id=1, source_target_pairs={{0,24},{8,16},{16,8},{24,0},{1,25},{9,17},{17,9},{25,1},{2,26},{10... | collective-permute-start | bytes 602120 | tf_op jit(solution)/shard_map/ppermute | solution.py:55
  138.7 8.8 %collective-permute-start.51 = (bf16[2,64,512]{2,1,0:T(8,128)(2,1)S(1)}, bf16[2,64,512]{2,1,0:T(8,128)(2,1)S(1)}, u32[]{:S(2)}, u32[]{:S(2)}) collective-permute-start(bf16[2,64,512]{2,1,0:T(8,128)(2,1)S(1)} %get-tuple-element.246), channel_id=1, source_target_pairs={{0,4},{1,5},{2,6},{3,7},{4,0},{5,1},{6,2},{7,3},{8,12},{9,13},{10,... | collective-permute-start | bytes 393224 | tf_op jit(solution)/shard_map/ppermute | solution.py:55
  155.4 8.9 %collective-permute-start.58 = (bf16[784,128]{1,0:T(8,128)(2,1)S(1)}, bf16[784,128]{1,0:T(8,128)(2,1)S(1)}, u32[]{:S(2)}, u32[]{:S(2)}) collective-permute-start(bf16[784,128]{1,0:T(8,128)(2,1)S(1)} %norm_back_kernel.1.d0), channel_id=1, source_target_pairs={{0,24},{8,16},{16,8},{24,0},{1,25},{9,17},{17,9},{25,1},{2,26},{10... | collective-permute-start | bytes 602120 | tf_op jit(solution)/shard_map/ppermute | solution.py:55
  157.3 9.3 %collective-permute-start.57 = (bf16[784,128]{1,0:T(8,128)(2,1)S(1)}, bf16[784,128]{1,0:T(8,128)(2,1)S(1)}, u32[]{:S(2)}, u32[]{:S(2)}) collective-permute-start(bf16[784,128]{1,0:T(8,128)(2,1)S(1)} %norm_back_kernel.1.d0), channel_id=1, source_target_pairs={{0,16},{8,24},{16,0},{24,8},{1,17},{9,25},{17,1},{25,9},{2,18},{10... | collective-permute-start | bytes 602120 | tf_op jit(solution)/shard_map/ppermute | solution.py:55
  158.2 8.3 %collective-permute-start.56 = (bf16[784,128]{1,0:T(8,128)(2,1)S(1)}, bf16[784,128]{1,0:T(8,128)(2,1)S(1)}, u32[]{:S(2)}, u32[]{:S(2)}) collective-permute-start(bf16[784,128]{1,0:T(8,128)(2,1)S(1)} %norm_back_kernel.1.d0), channel_id=1, source_target_pairs={{0,8},{8,0},{16,24},{24,16},{1,9},{9,1},{17,25},{25,17},{2,10},{10... | collective-permute-start | bytes 602120 | tf_op jit(solution)/shard_map/ppermute | solution.py:55
  178.2 15.5 %collective-permute-start.68 = (bf16[2,64,1152]{2,1,0:T(8,128)(2,1)S(1)}, bf16[2,64,1152]{2,1,0:T(8,128)(2,1)S(1)}, u32[]{:S(2)}, u32[]{:S(2)}) collective-permute-start(bf16[2,64,1152]{2,1,0:T(8,128)(2,1)S(1)} %get-tuple-element.281), channel_id=1, source_target_pairs={{0,4},{1,5},{2,6},{3,7},{4,0},{5,1},{6,2},{7,3},{8,12},{9,13},{10,... | collective-permute-start | bytes 884744 | tf_op jit(solution)/shard_map/ppermute | solution.py:55
  180.4 9.2 %collective-permute-start.66 = (bf16[832,128]{1,0:T(8,128)(2,1)S(1)}, bf16[832,128]{1,0:T(8,128)(2,1)S(1)}, u32[]{:S(2)}, u32[]{:S(2)}) collective-permute-start(bf16[832,128]{1,0:T(8,128)(2,1)S(1)} %last_norm_back_kernel.1.n0.d0), channel_id=1, source_target_pairs={{0,24},{8,16},{16,8},{24,0},{1,25},{9,17},{17,9},{25,1},{2,26},{10... | collective-permute-start | bytes 638984 | tf_op jit(solution)/shard_map/ppermute | solution.py:55
  182.2 9.9 %collective-permute-start.65 = (bf16[832,128]{1,0:T(8,128)(2,1)S(1)}, bf16[832,128]{1,0:T(8,128)(2,1)S(1)}, u32[]{:S(2)}, u32[]{:S(2)}) collective-permute-start(bf16[832,128]{1,0:T(8,128)(2,1)S(1)} %last_norm_back_kernel.1.n0.d0), channel_id=1, source_target_pairs={{0,16},{8,24},{16,0},{24,8},{1,17},{9,25},{17,1},{25,9},{2,18},{10... | collective-permute-start | bytes 638984 | tf_op jit(solution)/shard_map/ppermute | solution.py:55
  183.2 8.8 %collective-permute-start.64 = (bf16[832,128]{1,0:T(8,128)(2,1)S(1)}, bf16[832,128]{1,0:T(8,128)(2,1)S(1)}, u32[]{:S(2)}, u32[]{:S(2)}) collective-permute-start(bf16[832,128]{1,0:T(8,128)(2,1)S(1)} %last_norm_back_kernel.1.n0.d0), channel_id=1, source_target_pairs={{0,8},{8,0},{16,24},{24,16},{1,9},{9,1},{17,25},{25,17},{2,10},{10... | collective-permute-start | bytes 638984 | tf_op jit(solution)/shard_map/ppermute | solution.py:55
  195.4 10.3 %collective-permute-start.73 = (bf16[64,1152]{1,0:T(8,128)(2,1)S(1)}, bf16[64,1152]{1,0:T(8,128)(2,1)S(1)}, u32[]{:S(2)}, u32[]{:S(2)}) collective-permute-start(bf16[64,1152]{1,0:T(8,128)(2,1)S(1)} %get-tuple-element.297), channel_id=1, source_target_pairs={{0,2},{1,3},{2,0},{3,1},{4,6},{5,7},{6,4},{7,5},{8,10},{9,11},{10,... | collective-permute-start | bytes 442376 | tf_op jit(solution)/shard_map/ppermute | solution.py:55
  197.5 8.2 %collective-permute-start.70 = (bf16[64,512]{1,0:T(8,128)(2,1)S(1)}, bf16[64,512]{1,0:T(8,128)(2,1)S(1)}, u32[]{:S(2)}, u32[]{:S(2)}) collective-permute-start(bf16[64,512]{1,0:T(8,128)(2,1)S(1)} %get-tuple-element.291), channel_id=1, source_target_pairs={{0,2},{1,3},{2,0},{3,1},{4,6},{5,7},{6,4},{7,5},{8,10},{9,11},{10,... | collective-permute-start | bytes 196616 | tf_op jit(solution)/shard_map/ppermute | solution.py:55
  198.1 8.3 %collective-permute-start.71 = (bf16[64,512]{1,0:T(8,128)(2,1)S(1)}, bf16[64,512]{1,0:T(8,128)(2,1)S(1)}, u32[]{:S(2)}, u32[]{:S(2)}) collective-permute-start(bf16[64,512]{1,0:T(8,128)(2,1)S(1)} %get-tuple-element.292), channel_id=1, source_target_pairs={{0,4},{1,5},{2,6},{3,7},{4,0},{5,1},{6,2},{7,3},{8,12},{9,13},{10,... | collective-permute-start | bytes 196616 | tf_op jit(solution)/shard_map/ppermute | solution.py:55
  207.1 9.8 %collective-permute-start.74 = (bf16[64,1152]{1,0:T(8,128)(2,1)S(1)}, bf16[64,1152]{1,0:T(8,128)(2,1)S(1)}, u32[]{:S(2)}, u32[]{:S(2)}) collective-permute-start(bf16[64,1152]{1,0:T(8,128)(2,1)S(1)} %get-tuple-element.308), channel_id=1, source_target_pairs={{8,0},{0,8},{24,16},{9,1},{1,9},{25,17},{10,2},{2,10},{26,18},{11,... | collective-permute-start | bytes 442376 | tf_op jit(solution)/shard_map/ppermute | solution.py:1542
  210.2 9.9 %collective-permute-start.75 = (bf16[64,1152]{1,0:T(8,128)(2,1)S(1)}, bf16[64,1152]{1,0:T(8,128)(2,1)S(1)}, u32[]{:S(2)}, u32[]{:S(2)}) collective-permute-start(bf16[64,1152]{1,0:T(8,128)(2,1)S(1)} %get-tuple-element.309), channel_id=1, source_target_pairs={{16,0},{24,8},{0,16},{17,1},{25,9},{1,17},{18,2},{26,10},{2,18},{1... | collective-permute-start | bytes 442376 | tf_op jit(solution)/shard_map/ppermute | solution.py:1542
  211.5 8.6 %collective-permute-start.76 = (bf16[64,1152]{1,0:T(8,128)(2,1)S(1)}, bf16[64,1152]{1,0:T(8,128)(2,1)S(1)}, u32[]{:S(2)}, u32[]{:S(2)}) collective-permute-start(bf16[64,1152]{1,0:T(8,128)(2,1)S(1)} %get-tuple-element.310), channel_id=1, source_target_pairs={{24,0},{16,8},{8,16},{25,1},{17,9},{9,17},{26,2},{18,10},{10,18},{... | collective-permute-start | bytes 442376 | tf_op jit(solution)/shard_map/ppermute | solution.py:1542
  (51 other events, 251.4 us)

commit v4 on v3

--- a/solution.py
+++ b/solution.py
@@ -66,7 +66,7 @@
     while step < count:
         if 2 * step < count:
             near = value + flip(value, "dp", step)
-            far = flip(value, "dp", 2 * step) + flip(value, "dp", 3 * step)
+            far = flip(value, "dp", 3 * step) + flip(value, "dp", 2 * step)
             value = near + far
             step *= 4
         else:
@@ -513,7 +513,9 @@
             out[j * rows : (j + 1) * rows, :] = ref[...]
 
 
-def mixed_kernel(place, reduce, conv, expand, *outs):
+def mixed_kernel(place, own, r1, r2, r3, conv, expand, reduce, *outs):
+    value = (own[...] + r1[...].astype(F32)) + (r2[...].astype(F32) + r3[...].astype(F32))
+    reduce[...] = value.astype(BF16)
     for k, out in enumerate(outs):
         target = place[k + 1]
 
@@ -1021,17 +1023,21 @@
     mixed = (None, m1, m2, m3)
     t = place[0]
 
-    def write(lanes):
-        copy = pltpu.make_async_copy(buffer.at[:, pl.ds(0, lanes)], out.at[:, pl.ds(0, lanes)], sem)
+    def write(first, lanes):
+        part = pl.ds(first, lanes)
+        copy = pltpu.make_async_copy(buffer.at[:, part], out.at[:, part], sem.at[first // WIDE])
         copy.start()
-        copy.wait()
+        return copy
 
     @pl.when(t == 0)
     def _():
+        copies = []
         for u in range(SECTIONS):
             piece = reduce if u == 0 else mixed[u]
             buffer[:, u * WIDE : (u + 1) * WIDE] = piece[:, :WIDE].astype(F32)
-        write(D)
+            copies.append(write(u * WIDE, WIDE))
+        for copy in copies:
+            copy.wait()
 
     @pl.when(t == 1)
     def _():
@@ -1040,7 +1046,7 @@
             for tap in range(9):
                 at = tap * WIDTH + u * PART
                 buffer[:, at : at + PART] = piece[:, tap * PART : (tap + 1) * PART].astype(F32)
-        write(9 * WIDTH)
+        write(0, 9 * WIDTH).wait()
 
     @pl.when(t == 2)
     def _():
@@ -1050,7 +1056,7 @@
             lanes = slice(b * PART, (b + 1) * PART)
             row = jnp.concatenate([f[:, lanes] for f in four], axis=1)
             buffer[:, 4 * b * PART : 4 * (b + 1) * PART] = dot(row, weave)
-        write(D)
+        write(0, D).wait()
 
 
 def unpack_kernel(packed, out, buffer):
@@ -1536,8 +1542,15 @@
     g_expand = scatter_last(expand_last)
     joined = lax.optimization_barrier((*reduce_crossed, grad_in, norm_grads, g_conv, g_expand))
     *reduce_crossed, grad_in, norm_grads, g_conv, g_expand = joined
-    g_reduce = scatter_finish(reduce_crossed)
-    mixed = call(mixed_kernel, [shape(g_conv.shape, BF16)] * 3, place, g_reduce, g_conv, g_expand, us=0.3)
+    if ndp != 8:
+        nothing = jnp.zeros(reduce_crossed[0].shape, BF16)
+        reduce_crossed = [reduce_crossed[0].astype(F32), nothing, nothing, nothing]
+    g_reduce, *mixed = call(
+        mixed_kernel,
+        [shape(reduce_crossed[0].shape, BF16)] + [shape(g_conv.shape, BF16)] * 3,
+        place, *reduce_crossed, g_conv, g_expand,
+        us=0.5,
+    )
     mixed = [
         lax.ppermute(mixed[j - 1], "section", [(u ^ j, u) for u in range(3)]) for j in range(1, SECTIONS)
     ]
@@ -1548,7 +1561,7 @@
         in_specs=[pl.BlockSpec(memory_space=pltpu.SMEM), pl.BlockSpec(memory_space=pltpu.HBM)]
         + [pl.BlockSpec(memory_space=pltpu.VMEM)] * 6,
         out_specs=pl.BlockSpec(memory_space=pltpu.HBM),
-        scratch_shapes=[pltpu.VMEM((own, 9 * WIDTH), F32), pltpu.SemaphoreType.DMA],
+        scratch_shapes=[pltpu.VMEM((own, 9 * WIDTH), F32), pltpu.SemaphoreType.DMA((SECTIONS,))],
         input_output_aliases={1: 0},
         compiler_params=pltpu.CompilerParams(vmem_limit_bytes=12 * 2**20),
         cost_estimate=cost(2),

time: 224 us -> 223 us (level)
  starting transfers between devices: 95 us -> 88.7 us
  waiting for transfers between devices: 65.2 us -> 70.1 us
    ppermute x71, starting transfers between devices: 76.3 us -> 70 us  [flip(): lax.ppermute(value, axis, [(source, source ^ step) for source in range(co...]
    ppermute x71, waiting for transfers between devices: 61.9 us -> 66.9 us  [flip(): lax.ppermute(value, axis, [(source, source ^ step) for source in range(co...]
    pallas_call x42 -> x41, Pallas kernels: 49.7 us -> 49.7 us  [call(): pl.pallas_call(kernel, name=getattr(kernel, 'func', kernel).__name__, out...]
  transfers between devices with their start and end apart: 77 -> 77, of which waited for: 46 -> 47; matrix products, arithmetic and copies ran while one was open for 0% -> 0% of each run, Pallas kernels for 19% -> 19%
where the time goes in v4:
time: 223 us; the launch traced here: 221 us
  starting transfers between devices  88.7 us (40%)
  waiting for transfers between devices  70.1 us (31%)
  Pallas kernels  59 us (26%)
    ppermute x71, starting transfers between devices, flip(): lax.ppermute(value, axis, [(source, source ^ step) for source in range(co...  70 us
    ppermute x71, waiting for transfers between devices, flip(): lax.ppermute(value, axis, [(source, source ^ step) for source in range(co...  66.9 us
    pallas_call x41, Pallas kernels, call(): pl.pallas_call(kernel, name=getattr(kernel, 'func', kernel).__name__, out...  49.7 us
    ppermute x3, starting transfers between devices, body(): lax.ppermute(messages[j - 1], 'section', [(u, u ^ j) for u in range(3)])  9.48 us
    ppermute x3, starting transfers between devices, body(): lax.ppermute(mixed[j - 1], 'section', [(u ^ j, u) for u in range(3)])  9.21 us
  transfers between devices with their start and end apart: 77, of which 47 were waited for; matrix products, arithmetic and copies ran while one was open for 0% of the time, Pallas kernels for 19%

profile of v4, /device:TPU:2, one launch (start us, length us, event | category | flops | bytes accessed | tf_op | source)
XLA Modules:
  0.0 220.7 jit_solution(17710317158781713173)
XLA Ops:
  1.5 2.3 %pack.1 = (bf16[1168,128]{1,0:T(8,128)(2,1)S(1)}, bf16[1168,128]{1,0:T(8,128)(2,1)S(1)}, bf16[1168,128]{1,0:T(8,128)(2,1)S(1)}, bf16[1168,128]{1,0:T(8,128)(2,1)S(1)}) custom-call(s32[9]{0:T(128)S(1)} %stack.39.place, bf16[9456,512]{1,0:T(8,128)(2,1)} %bitcast.22, f32[3,1,2048]{2,1,0:T(1,128)S(1)} %bitcast.26), custom_call_target="tpu_custom_call" | custom-call | bytes 6000000 | tf_op jit(solution)/shard_map/pack/pallas_call | solution.py:1147
  3.9 2.2 collective-permute-start
  7.5 5.8 %collective-permute-start.2 = (bf16[1168,128]{1,0:T(8,128)(2,1)S(1)}, bf16[1168,128]{1,0:T(8,128)(2,1)S(1)}, u32[]{:S(2)}, u32[]{:S(2)}) collective-permute-start(bf16[1168,128]{1,0:T(8,128)(2,1)S(1)} %get-tuple-element.162), channel_id=1, source_target_pairs={{0,24},{8,16},{16,8},{1,25},{9,17},{17,9},{2,26},{10,18},{18,10},{... | collective-permute-start | bytes 897032 | tf_op jit(solution)/shard_map/ppermute | solution.py:1238
  16.8 3.6 %unpack.1.w_head = bf16[2048,2048]{1,0:T(8,128)(2,1)S(1)} custom-call(bf16[9456,512]{1,0:T(8,128)(2,1)S(1)} %bitcast.24), custom_call_target="tpu_custom_call" | custom-call | bytes 12000000 | tf_op jit(solution)/shard_map/unpack/pallas_call | solution.py:1074
  26.3 2.6 %collective-permute-start.9 = (f32[8,128]{1,0:T(8,128)S(1)}, f32[8,128]{1,0:T(8,128)S(1)}, u32[]{:S(2)}, u32[]{:S(2)}) collective-permute-start(f32[8,128]{1,0:T(8,128)S(1)} %add.82), channel_id=1, source_target_pairs={{0,4},{1,5},{2,6},{3,7},{4,0},{5,1},{6,2},{7,3},{8,12},{9,13},{10,... | collective-permute-start | bytes 12296 | tf_op jit(solution)/shard_map/ppermute | solution.py:55
  30.9 3.4 %collective-permute-done.8 = f32[8,128]{1,0:T(8,128)S(1)} collective-permute-done((f32[8,128]{1,0:T(8,128)S(1)}, f32[8,128]{1,0:T(8,128)S(1)}, u32[]{:S(2)}, u32[]{:S(2)}) %collective-permute-start.8) | collective-permute-done | bytes 4128 | tf_op jit(solution)/shard_map/ppermute | solution.py:55
  34.6 3.9 %collective-permute-start.12 = (bf16[784,128]{1,0:T(8,128)(2,1)S(1)}, bf16[784,128]{1,0:T(8,128)(2,1)S(1)}, u32[]{:S(2)}, u32[]{:S(2)}) collective-permute-start(bf16[784,128]{1,0:T(8,128)(2,1)S(1)} %active_kernel.2.active.a0), channel_id=1, source_target_pairs={{0,24},{8,16},{16,8},{24,0},{1,25},{9,17},{17,9},{25,1},{2,26},{10... | collective-permute-start | bytes 602120 | tf_op jit(solution)/shard_map/ppermute | solution.py:55
  45.3 3.1 %collective-permute-done.11.a2 = bf16[784,128]{1,0:T(8,128)(2,1)S(1)} collective-permute-done((bf16[784,128]{1,0:T(8,128)(2,1)S(1)}, bf16[784,128]{1,0:T(8,128)(2,1)S(1)}, u32[]{:S(2)}, u32[]{:S(2)}) %collective-permute-start.11) | collective-permute-done | bytes 200736 | tf_op jit(solution)/shard_map/ppermute | solution.py:55
  48.4 2.2 conv_kernel.1
  56.3 2.1 collective-permute-done.18
  62.1 3.1 %mass_kernel.1 = (bf16[512,3072]{1,0:T(8,128)(2,1)S(1)}, f32[8,3072]{1,0:T(8,128)S(1)}, bf16[2,32,32]{2,1,0:T(8,128)(2,1)S(1)}) custom-call(s32[9]{0:T(128)S(1)} %stack.39.place, bf16[768,512]{1,0:T(8,128)(2,1)S(1)} %get-tuple-element.190.table, bf16[320,128]{1,0:T(8,128)(2,1)S(1)} %rows_kernel.5.refs_0_, bf16[320,128]{1,0:T(8,128)(2,1)S(1)} %collective-permute-done.13.refs_1_), custom_call_target="tpu_custom_call" | custom-call | bytes 15000000 | tf_op jit(solution)/shard_map/mass_kernel/pallas_call | solution.py:139
  65.2 2.1 collective-permute-done.22.a3
  67.4 2.1 collective-permute-done.21.a2
  89.4 2.1 collective-permute-start.30
  98.3 10.9 %head_kernel.1 = (bf16[128,2048]{1,0:T(8,128)(2,1)S(1)}, bf16[128,2048]{1,0:T(8,128)(2,1)S(1)}, bf16[128,128]{1,0:T(8,128)(2,1)S(1)}, bf16[64,3072]{1,0:T(8,128)...) custom-call(s32[9]{0:T(128)S(1)} %stack.39.place, ...), custom_call_target="tpu_custom_call" | custom-call | bytes 36000000 | tf_op jit(solution)/shard_map/head_kernel/pallas_call | solution.py:139
  110.4 4.5 %head_back_kernel.1 = (bf16[16,512]{1,0:T(8,128)(2,1)S(1)}, bf16[16,512]{1,0:T(8,128)(2,1)S(1)}, bf16[16,512]{1,0:T(8,128)(2,1)S(1)}, bf16[16,512]{1,0:T(8,128)(...) custom-call(s32[9]{0:T(128)S(1)} %stack.39.place, ...), custom_call_target="tpu_custom_call" | custom-call | bytes 15000000 | tf_op jit(solution)/shard_map/head_back_kernel/pallas_call | solution.py:139
  126.1 2.0 collective-permute-start.43
  129.4 2.3 %collective-permute-done.43 = f32[8,512]{1,0:T(8,128)S(1)} collective-permute-done((f32[8,512]{1,0:T(8,128)S(1)}, f32[8,512]{1,0:T(8,128)S(1)}, u32[]{:S(2)}, u32[]{:S(2)}) %collective-permute-start.43) | collective-permute-done | bytes 16416 | tf_op jit(solution)/shard_map/ppermute | solution.py:55
  140.2 2.3 %collective-permute-done.46.q1 = bf16[784,128]{1,0:T(8,128)(2,1)S(1)} collective-permute-done((bf16[784,128]{1,0:T(8,128)(2,1)S(1)}, bf16[784,128]{1,0:T(8,128)(2,1)S(1)}, u32[]{:S(2)}, u32[]{:S(2)}) %collective-permute-start.46) | collective-permute-done | bytes 200736 | tf_op jit(solution)/shard_map/ppermute | solution.py:55
  142.5 4.9 %collective-permute-done.47.q2 = bf16[784,128]{1,0:T(8,128)(2,1)S(1)} collective-permute-done((bf16[784,128]{1,0:T(8,128)(2,1)S(1)}, bf16[784,128]{1,0:T(8,128)(2,1)S(1)}, u32[]{:S(2)}, u32[]{:S(2)}) %collective-permute-start.47) | collective-permute-done | bytes 200736 | tf_op jit(solution)/shard_map/ppermute | solution.py:55
  149.6 2.0 collective-permute-start.54
  159.9 2.1 head_grads_kernel.1.base
  164.0 2.1 collective-permute-done.57.d2
  166.1 2.4 %conv_back_kernel.1 = (bf16[784,512]{1,0:T(8,128)(2,1)S(1)}, f32[784,128]{1,0:T(8,128)S(1)}, f32[8,128]{1,0:T(8,128)S(1)}) custom-call(s32[9]{0:T(128)S(1)} %stack.39.place, bf16[784,128]{1,0:T(8,128)(2,1)S(1)} %norm_back_kernel.1.d0, bf16[784,128]{1,0:T(8,128)(2,1)S(1)} %collective-permute-done.56.d1, bf16[784,128]{1,0:T(8,128)(2,1)S(1)} %collective-permute-done.57.d2, ...), custom_call_target="tpu_custom_call" | custom-call | bytes 10500000 | tf_op jit(solution)/shard_map/conv_back_kernel/pallas_call | solution.py:139
  168.5 2.1 pair_kernel.3
  176.8 2.3 %collective-permute-start.68 = (bf16[2,64,1152]{2,1,0:T(8,128)(2,1)S(1)}, bf16[2,64,1152]{2,1,0:T(8,128)(2,1)S(1)}, u32[]{:S(2)}, u32[]{:S(2)}) collective-permute-start(bf16[2,64,1152]{2,1,0:T(8,128)(2,1)S(1)} %get-tuple-element.282), channel_id=1, source_target_pairs={{0,4},{1,5},{2,6},{3,7},{4,0},{5,1},{6,2},{7,3},{8,12},{9,13},{10,... | collective-permute-start | bytes 884744 | tf_op jit(solution)/shard_map/ppermute | solution.py:55
  183.7 5.6 %collective-permute-done.66.n3.d3 = bf16[832,128]{1,0:T(8,128)(2,1)S(1)} collective-permute-done((bf16[832,128]{1,0:T(8,128)(2,1)S(1)}, bf16[832,128]{1,0:T(8,128)(2,1)S(1)}, u32[]{:S(2)}, u32[]{:S(2)}) %collective-permute-start.66) | collective-permute-done | bytes 213024 | tf_op jit(solution)/shard_map/ppermute | solution.py:55
  189.3 2.2 %collective-permute-done.65.n2.d2 = bf16[832,128]{1,0:T(8,128)(2,1)S(1)} collective-permute-done((bf16[832,128]{1,0:T(8,128)(2,1)S(1)}, bf16[832,128]{1,0:T(8,128)(2,1)S(1)}, u32[]{:S(2)}, u32[]{:S(2)}) %collective-permute-start.65) | collective-permute-done | bytes 213024 | tf_op jit(solution)/shard_map/ppermute | solution.py:55
  201.8 2.5 %reduce_back_kernel.1 = f32[196,4,512]{2,1,0:T(4,128)} custom-call(s32[9]{0:T(128)S(1)} %stack.39.place, bf16[784,512]{1,0:T(8,128)(2,1)S(1)} %get-tuple-element.295.d_full, bf16[4,832,128]{2,1,0:T(8,128)(2,1)S(1)} %stack_kernel.1.back0, bf16[4,832,128]{2,1,0:T(8,128)(2,1)S(1)} %collective-permute-done.45.back1, f32[784,512]{1,0:T(8,128)S(1)} %get-tuple-element.225.d_z), custom_call_target="tpu_custom_call" | custom-call | bytes 6000000 | tf_op jit(solution)/shard_map/reduce_back_kernel/pallas_call | solution.py:139
  205.7 2.9 %collective-permute-start.74 = (bf16[64,1152]{1,0:T(8,128)(2,1)S(1)}, bf16[64,1152]{1,0:T(8,128)(2,1)S(1)}, u32[]{:S(2)}, u32[]{:S(2)}) collective-permute-start(bf16[64,1152]{1,0:T(8,128)(2,1)S(1)} %get-tuple-element.310), channel_id=1, source_target_pairs={{8,0},{0,8},{24,16},{9,1},{1,9},{25,17},{10,2},{2,10},{26,18},{11,... | collective-permute-start | bytes 442376 | tf_op jit(solution)/shard_map/ppermute | solution.py:1555
  210.0 5.0 %collective-permute-start.76 = (bf16[64,1152]{1,0:T(8,128)(2,1)S(1)}, bf16[64,1152]{1,0:T(8,128)(2,1)S(1)}, u32[]{:S(2)}, u32[]{:S(2)}) collective-permute-start(bf16[64,1152]{1,0:T(8,128)(2,1)S(1)} %get-tuple-element.312), channel_id=1, source_target_pairs={{24,0},{16,8},{8,16},{25,1},{17,9},{9,17},{26,2},{18,10},{10,18},{... | collective-permute-start | bytes 442376 | tf_op jit(solution)/shard_map/ppermute | solution.py:1555
  215.5 3.3 %collective-permute-done.75.m2 = bf16[64,1152]{1,0:T(8,128)(2,1)S(1)} collective-permute-done((bf16[64,1152]{1,0:T(8,128)(2,1)S(1)}, bf16[64,1152]{1,0:T(8,128)(2,1)S(1)}, u32[]{:S(2)}, u32[]{:S(2)}) %collective-permute-start.75) | collective-permute-done | bytes 147488 | tf_op jit(solution)/shard_map/ppermute | solution.py:1555
  (193 shorter events, 117.2 us)
Async XLA Ops:
  3.9 16.9 %collective-permute-start = (bf16[1168,128]{1,0:T(8,128)(2,1)S(1)}, bf16[1168,128]{1,0:T(8,128)(2,1)S(1)}, u32[]{:S(2)}, u32[]{:S(2)}) collective-permute-start(bf16[1168,128]{1,0:T(8,128)(2,1)S(1)} %get-tuple-element.160), channel_id=1, source_target_pairs={{0,8},{8,0},{16,24},{1,9},{9,1},{17,25},{2,10},{10,2},{18,26},{3,1... | collective-permute-start | bytes 897032 | tf_op jit(solution)/shard_map/ppermute | solution.py:1238
  6.0 14.7 %collective-permute-start.1 = (bf16[1168,128]{1,0:T(8,128)(2,1)S(1)}, bf16[1168,128]{1,0:T(8,128)(2,1)S(1)}, u32[]{:S(2)}, u32[]{:S(2)}) collective-permute-start(bf16[1168,128]{1,0:T(8,128)(2,1)S(1)} %get-tuple-element.161), channel_id=1, source_target_pairs={{0,16},{8,24},{16,0},{1,17},{9,25},{17,1},{2,18},{10,26},{18,2},{3... | collective-permute-start | bytes 897032 | tf_op jit(solution)/shard_map/ppermute | solution.py:1238
  7.5 13.2 %collective-permute-start.2 = (bf16[1168,128]{1,0:T(8,128)(2,1)S(1)}, bf16[1168,128]{1,0:T(8,128)(2,1)S(1)}, u32[]{:S(2)}, u32[]{:S(2)}) collective-permute-start(bf16[1168,128]{1,0:T(8,128)(2,1)S(1)} %get-tuple-element.162), channel_id=1, source_target_pairs={{0,24},{8,16},{16,8},{1,25},{9,17},{17,9},{2,26},{10,18},{18,10},{... | collective-permute-start | bytes 897032 | tf_op jit(solution)/shard_map/ppermute | solution.py:1238
  21.6 12.9 %collective-permute-start.14 = (bf16[1168,128]{1,0:T(8,128)(2,1)S(1)}, bf16[1168,128]{1,0:T(8,128)(2,1)S(1)}, u32[]{:S(2)}, u32[]{:S(2)}) collective-permute-start(bf16[1168,128]{1,0:T(8,128)(2,1)S(1)} %get-tuple-element.177.refs_0_), channel_id=1, source_target_pairs={{0,2},{1,3},{2,0},{3,1},{4,6},{5,7},{6,4},{7,5},{8,10},{9,11},{10,... | collective-permute-start | bytes 897032 | tf_op jit(solution)/shard_map/ppermute | solution.py:55
  34.5 8.2 %collective-permute-start.15 = (bf16[2336,128]{1,0:T(8,128)(2,1)S(1)}, bf16[2336,128]{1,0:T(8,128)(2,1)S(1)}, u32[]{:S(2)}, u32[]{:S(2)}) collective-permute-start(bf16[2336,128]{1,0:T(8,128)(2,1)S(1)} %rows_kernel.6.conv_a.wa.told), channel_id=1, source_target_pairs={{0,1},{1,0},{2,3},{3,2},{4,5},{5,4},{6,7},{7,6},{8,9},{9,8},{10,11... | collective-permute-start | bytes 1794056 | tf_op jit(solution)/shard_map/ppermute | solution.py:55
  34.6 10.7 %collective-permute-start.12 = (bf16[784,128]{1,0:T(8,128)(2,1)S(1)}, bf16[784,128]{1,0:T(8,128)(2,1)S(1)}, u32[]{:S(2)}, u32[]{:S(2)}) collective-permute-start(bf16[784,128]{1,0:T(8,128)(2,1)S(1)} %active_kernel.2.active.a0), channel_id=1, source_target_pairs={{0,24},{8,16},{16,8},{24,0},{1,25},{9,17},{17,9},{25,1},{2,26},{10... | collective-permute-start | bytes 602120 | tf_op jit(solution)/shard_map/ppermute | solution.py:55
  38.5 9.9 %collective-permute-start.11 = (bf16[784,128]{1,0:T(8,128)(2,1)S(1)}, bf16[784,128]{1,0:T(8,128)(2,1)S(1)}, u32[]{:S(2)}, u32[]{:S(2)}) collective-permute-start(bf16[784,128]{1,0:T(8,128)(2,1)S(1)} %active_kernel.2.active.a0), channel_id=1, source_target_pairs={{0,16},{8,24},{16,0},{24,8},{1,17},{9,25},{17,1},{25,9},{2,18},{10... | collective-permute-start | bytes 602120 | tf_op jit(solution)/shard_map/ppermute | solution.py:55
  38.5 9.9 %collective-permute-start.10 = (bf16[784,128]{1,0:T(8,128)(2,1)S(1)}, bf16[784,128]{1,0:T(8,128)(2,1)S(1)}, u32[]{:S(2)}, u32[]{:S(2)}) collective-permute-start(bf16[784,128]{1,0:T(8,128)(2,1)S(1)} %active_kernel.2.active.a0), channel_id=1, source_target_pairs={{0,8},{8,0},{16,24},{24,16},{1,9},{9,1},{17,25},{25,17},{2,10},{10... | collective-permute-start | bytes 602120 | tf_op jit(solution)/shard_map/ppermute | solution.py:55
  58.6 8.8 %collective-permute-start.22 = (bf16[784,128]{1,0:T(8,128)(2,1)S(1)}, bf16[784,128]{1,0:T(8,128)(2,1)S(1)}, u32[]{:S(2)}, u32[]{:S(2)}) collective-permute-start(bf16[784,128]{1,0:T(8,128)(2,1)S(1)} %active_kernel.3.a0), channel_id=1, source_target_pairs={{0,24},{8,16},{16,8},{24,0},{1,25},{9,17},{17,9},{25,1},{2,26},{10... | collective-permute-start | bytes 602120 | tf_op jit(solution)/shard_map/ppermute | solution.py:55
  60.4 9.1 %collective-permute-start.21 = (bf16[784,128]{1,0:T(8,128)(2,1)S(1)}, bf16[784,128]{1,0:T(8,128)(2,1)S(1)}, u32[]{:S(2)}, u32[]{:S(2)}) collective-permute-start(bf16[784,128]{1,0:T(8,128)(2,1)S(1)} %active_kernel.3.a0), channel_id=1, source_target_pairs={{0,16},{8,24},{16,0},{24,8},{1,17},{9,25},{17,1},{25,9},{2,18},{10... | collective-permute-start | bytes 602120 | tf_op jit(solution)/shard_map/ppermute | solution.py:55
  94.7 20.3 %collective-permute-start.35 = (bf16[832,128]{1,0:T(8,128)(2,1)S(1)}, bf16[832,128]{1,0:T(8,128)(2,1)S(1)}, u32[]{:S(2)}, u32[]{:S(2)}) collective-permute-start(bf16[832,128]{1,0:T(8,128)(2,1)S(1)} %get-tuple-element.218), channel_id=1, source_target_pairs={{0,8},{8,0},{16,24},{24,16},{1,9},{9,1},{17,25},{25,17},{2,10},{10... | collective-permute-start | bytes 638984 | tf_op jit(solution)/shard_map/ppermute | solution.py:55
  95.5 19.5 %collective-permute-start.36 = (bf16[832,128]{1,0:T(8,128)(2,1)S(1)}, bf16[832,128]{1,0:T(8,128)(2,1)S(1)}, u32[]{:S(2)}, u32[]{:S(2)}) collective-permute-start(bf16[832,128]{1,0:T(8,128)(2,1)S(1)} %get-tuple-element.219), channel_id=1, source_target_pairs={{0,16},{8,24},{16,0},{24,8},{1,17},{9,25},{17,1},{25,9},{2,18},{10... | collective-permute-start | bytes 638984 | tf_op jit(solution)/shard_map/ppermute | solution.py:55
  96.4 18.6 %collective-permute-start.37 = (bf16[832,128]{1,0:T(8,128)(2,1)S(1)}, bf16[832,128]{1,0:T(8,128)(2,1)S(1)}, u32[]{:S(2)}, u32[]{:S(2)}) collective-permute-start(bf16[832,128]{1,0:T(8,128)(2,1)S(1)} %get-tuple-element.220), channel_id=1, source_target_pairs={{0,24},{8,16},{16,8},{24,0},{1,25},{9,17},{17,9},{25,1},{2,26},{10... | collective-permute-start | bytes 638984 | tf_op jit(solution)/shard_map/ppermute | solution.py:55
  115.1 16.8 %collective-permute-start.45 = (bf16[4,832,128]{2,1,0:T(8,128)(2,1)S(1)}, bf16[4,832,128]{2,1,0:T(8,128)(2,1)S(1)}, u32[]{:S(2)}, u32[]{:S(2)}) collective-permute-start(bf16[4,832,128]{2,1,0:T(8,128)(2,1)S(1)} %stack_kernel.1.back0), channel_id=1, source_target_pairs={{0,1},{1,0},{2,3},{3,2},{4,5},{5,4},{6,7},{7,6},{8,9},{9,8},{10,11... | collective-permute-start | bytes 2555912 | tf_op jit(solution)/shard_map/ppermute | solution.py:55
  128.1 11.3 %collective-permute-start.49 = (bf16[64,3072]{1,0:T(8,128)(2,1)S(1)}, bf16[64,3072]{1,0:T(8,128)(2,1)S(1)}, u32[]{:S(2)}, u32[]{:S(2)}) collective-permute-start(bf16[64,3072]{1,0:T(8,128)(2,1)S(1)} %get-tuple-element.241.d_here), channel_id=1, source_target_pairs={{0,1},{1,0},{2,3},{3,2},{4,5},{5,4},{6,7},{7,6},{8,9},{9,8},{10,11... | collective-permute-start | bytes 1179656 | tf_op jit(solution)/shard_map/ppermute | solution.py:55
  134.7 7.9 %collective-permute-start.46 = (bf16[784,128]{1,0:T(8,128)(2,1)S(1)}, bf16[784,128]{1,0:T(8,128)(2,1)S(1)}, u32[]{:S(2)}, u32[]{:S(2)}) collective-permute-start(bf16[784,128]{1,0:T(8,128)(2,1)S(1)} %get-tuple-element.234), channel_id=1, source_target_pairs={{0,8},{8,0},{16,24},{24,16},{1,9},{9,1},{17,25},{25,17},{2,10},{10... | collective-permute-start | bytes 602120 | tf_op jit(solution)/shard_map/ppermute | solution.py:55
  136.1 11.4 %collective-permute-start.47 = (bf16[784,128]{1,0:T(8,128)(2,1)S(1)}, bf16[784,128]{1,0:T(8,128)(2,1)S(1)}, u32[]{:S(2)}, u32[]{:S(2)}) collective-permute-start(bf16[784,128]{1,0:T(8,128)(2,1)S(1)} %get-tuple-element.235), channel_id=1, source_target_pairs={{0,16},{8,24},{16,0},{24,8},{1,17},{9,25},{17,1},{25,9},{2,18},{10... | collective-permute-start | bytes 602120 | tf_op jit(solution)/shard_map/ppermute | solution.py:55
  137.2 10.3 %collective-permute-start.48 = (bf16[784,128]{1,0:T(8,128)(2,1)S(1)}, bf16[784,128]{1,0:T(8,128)(2,1)S(1)}, u32[]{:S(2)}, u32[]{:S(2)}) collective-permute-start(bf16[784,128]{1,0:T(8,128)(2,1)S(1)} %get-tuple-element.236), channel_id=1, source_target_pairs={{0,24},{8,16},{16,8},{24,0},{1,25},{9,17},{17,9},{25,1},{2,26},{10... | collective-permute-start | bytes 602120 | tf_op jit(solution)/shard_map/ppermute | solution.py:55
  138.8 8.6 %collective-permute-start.51 = (bf16[2,64,512]{2,1,0:T(8,128)(2,1)S(1)}, bf16[2,64,512]{2,1,0:T(8,128)(2,1)S(1)}, u32[]{:S(2)}, u32[]{:S(2)}) collective-permute-start(bf16[2,64,512]{2,1,0:T(8,128)(2,1)S(1)} %get-tuple-element.247), channel_id=1, source_target_pairs={{0,4},{1,5},{2,6},{3,7},{4,0},{5,1},{6,2},{7,3},{8,12},{9,13},{10,... | collective-permute-start | bytes 393224 | tf_op jit(solution)/shard_map/ppermute | solution.py:55
  155.3 8.7 %collective-permute-start.58 = (bf16[784,128]{1,0:T(8,128)(2,1)S(1)}, bf16[784,128]{1,0:T(8,128)(2,1)S(1)}, u32[]{:S(2)}, u32[]{:S(2)}) collective-permute-start(bf16[784,128]{1,0:T(8,128)(2,1)S(1)} %norm_back_kernel.1.d0), channel_id=1, source_target_pairs={{0,24},{8,16},{16,8},{24,0},{1,25},{9,17},{17,9},{25,1},{2,26},{10... | collective-permute-start | bytes 602120 | tf_op jit(solution)/shard_map/ppermute | solution.py:55
  156.6 9.5 %collective-permute-start.57 = (bf16[784,128]{1,0:T(8,128)(2,1)S(1)}, bf16[784,128]{1,0:T(8,128)(2,1)S(1)}, u32[]{:S(2)}, u32[]{:S(2)}) collective-permute-start(bf16[784,128]{1,0:T(8,128)(2,1)S(1)} %norm_back_kernel.1.d0), channel_id=1, source_target_pairs={{0,16},{8,24},{16,0},{24,8},{1,17},{9,25},{17,1},{25,9},{2,18},{10... | collective-permute-start | bytes 602120 | tf_op jit(solution)/shard_map/ppermute | solution.py:55
  157.6 8.5 %collective-permute-start.56 = (bf16[784,128]{1,0:T(8,128)(2,1)S(1)}, bf16[784,128]{1,0:T(8,128)(2,1)S(1)}, u32[]{:S(2)}, u32[]{:S(2)}) collective-permute-start(bf16[784,128]{1,0:T(8,128)(2,1)S(1)} %norm_back_kernel.1.d0), channel_id=1, source_target_pairs={{0,8},{8,0},{16,24},{24,16},{1,9},{9,1},{17,25},{25,17},{2,10},{10... | collective-permute-start | bytes 602120 | tf_op jit(solution)/shard_map/ppermute | solution.py:55
  176.8 15.5 %collective-permute-start.68 = (bf16[2,64,1152]{2,1,0:T(8,128)(2,1)S(1)}, bf16[2,64,1152]{2,1,0:T(8,128)(2,1)S(1)}, u32[]{:S(2)}, u32[]{:S(2)}) collective-permute-start(bf16[2,64,1152]{2,1,0:T(8,128)(2,1)S(1)} %get-tuple-element.282), channel_id=1, source_target_pairs={{0,4},{1,5},{2,6},{3,7},{4,0},{5,1},{6,2},{7,3},{8,12},{9,13},{10,... | collective-permute-start | bytes 884744 | tf_op jit(solution)/shard_map/ppermute | solution.py:55
  180.2 9.2 %collective-permute-start.66 = (bf16[832,128]{1,0:T(8,128)(2,1)S(1)}, bf16[832,128]{1,0:T(8,128)(2,1)S(1)}, u32[]{:S(2)}, u32[]{:S(2)}) collective-permute-start(bf16[832,128]{1,0:T(8,128)(2,1)S(1)} %last_norm_back_kernel.1.n0.d0), channel_id=1, source_target_pairs={{0,24},{8,16},{16,8},{24,0},{1,25},{9,17},{17,9},{25,1},{2,26},{10... | collective-permute-start | bytes 638984 | tf_op jit(solution)/shard_map/ppermute | solution.py:55
  181.8 9.7 %collective-permute-start.65 = (bf16[832,128]{1,0:T(8,128)(2,1)S(1)}, bf16[832,128]{1,0:T(8,128)(2,1)S(1)}, u32[]{:S(2)}, u32[]{:S(2)}) collective-permute-start(bf16[832,128]{1,0:T(8,128)(2,1)S(1)} %last_norm_back_kernel.1.n0.d0), channel_id=1, source_target_pairs={{0,16},{8,24},{16,0},{24,8},{1,17},{9,25},{17,1},{25,9},{2,18},{10... | collective-permute-start | bytes 638984 | tf_op jit(solution)/shard_map/ppermute | solution.py:55
  182.8 8.8 %collective-permute-start.64 = (bf16[832,128]{1,0:T(8,128)(2,1)S(1)}, bf16[832,128]{1,0:T(8,128)(2,1)S(1)}, u32[]{:S(2)}, u32[]{:S(2)}) collective-permute-start(bf16[832,128]{1,0:T(8,128)(2,1)S(1)} %last_norm_back_kernel.1.n0.d0), channel_id=1, source_target_pairs={{0,8},{8,0},{16,24},{24,16},{1,9},{9,1},{17,25},{25,17},{2,10},{10... | collective-permute-start | bytes 638984 | tf_op jit(solution)/shard_map/ppermute | solution.py:55
  194.0 10.3 %collective-permute-start.73 = (bf16[64,1152]{1,0:T(8,128)(2,1)S(1)}, bf16[64,1152]{1,0:T(8,128)(2,1)S(1)}, u32[]{:S(2)}, u32[]{:S(2)}) collective-permute-start(bf16[64,1152]{1,0:T(8,128)(2,1)S(1)} %get-tuple-element.298), channel_id=1, source_target_pairs={{0,2},{1,3},{2,0},{3,1},{4,6},{5,7},{6,4},{7,5},{8,10},{9,11},{10,... | collective-permute-start | bytes 442376 | tf_op jit(solution)/shard_map/ppermute | solution.py:55
  196.1 8.2 %collective-permute-start.70 = (bf16[64,512]{1,0:T(8,128)(2,1)S(1)}, bf16[64,512]{1,0:T(8,128)(2,1)S(1)}, u32[]{:S(2)}, u32[]{:S(2)}) collective-permute-start(bf16[64,512]{1,0:T(8,128)(2,1)S(1)} %get-tuple-element.292), channel_id=1, source_target_pairs={{0,2},{1,3},{2,0},{3,1},{4,6},{5,7},{6,4},{7,5},{8,10},{9,11},{10,... | collective-permute-start | bytes 196616 | tf_op jit(solution)/shard_map/ppermute | solution.py:55
  196.7 8.4 %collective-permute-start.71 = (bf16[64,512]{1,0:T(8,128)(2,1)S(1)}, bf16[64,512]{1,0:T(8,128)(2,1)S(1)}, u32[]{:S(2)}, u32[]{:S(2)}) collective-permute-start(bf16[64,512]{1,0:T(8,128)(2,1)S(1)} %get-tuple-element.293), channel_id=1, source_target_pairs={{0,4},{1,5},{2,6},{3,7},{4,0},{5,1},{6,2},{7,3},{8,12},{9,13},{10,... | collective-permute-start | bytes 196616 | tf_op jit(solution)/shard_map/ppermute | solution.py:55
  205.7 9.8 %collective-permute-start.74 = (bf16[64,1152]{1,0:T(8,128)(2,1)S(1)}, bf16[64,1152]{1,0:T(8,128)(2,1)S(1)}, u32[]{:S(2)}, u32[]{:S(2)}) collective-permute-start(bf16[64,1152]{1,0:T(8,128)(2,1)S(1)} %get-tuple-element.310), channel_id=1, source_target_pairs={{8,0},{0,8},{24,16},{9,1},{1,9},{25,17},{10,2},{2,10},{26,18},{11,... | collective-permute-start | bytes 442376 | tf_op jit(solution)/shard_map/ppermute | solution.py:1555
  208.7 10.1 %collective-permute-start.75 = (bf16[64,1152]{1,0:T(8,128)(2,1)S(1)}, bf16[64,1152]{1,0:T(8,128)(2,1)S(1)}, u32[]{:S(2)}, u32[]{:S(2)}) collective-permute-start(bf16[64,1152]{1,0:T(8,128)(2,1)S(1)} %get-tuple-element.311), channel_id=1, source_target_pairs={{16,0},{24,8},{0,16},{17,1},{25,9},{1,17},{18,2},{26,10},{2,18},{1... | collective-permute-start | bytes 442376 | tf_op jit(solution)/shard_map/ppermute | solution.py:1555
  210.0 8.8 %collective-permute-start.76 = (bf16[64,1152]{1,0:T(8,128)(2,1)S(1)}, bf16[64,1152]{1,0:T(8,128)(2,1)S(1)}, u32[]{:S(2)}, u32[]{:S(2)}) collective-permute-start(bf16[64,1152]{1,0:T(8,128)(2,1)S(1)} %get-tuple-element.312), channel_id=1, source_target_pairs={{24,0},{16,8},{8,16},{25,1},{17,9},{9,17},{26,2},{18,10},{10,18},{... | collective-permute-start | bytes 442376 | tf_op jit(solution)/shard_map/ppermute | solution.py:1555
  (51 other events, 249.8 us)

commit v5 on v4

--- a/solution.py
+++ b/solution.py
@@ -296,7 +296,7 @@
     return place[8] ^ (0, 2, 1, 3)[j]
 
 
-def conv_kernel(micro, images, place, a0, a1, a2, a3, wa, wb, pre, sums, full, weight):
+def conv_kernel(micro, images, place, a0, a2, a3, a1, wa, wb, pre, sums, full, weight):
     fill(place, (a0, a1, a2, a3), full)
     quarter = WIDTH // 4
     for j in range(4):
@@ -319,7 +319,7 @@
     sums[...] = split_sums(parts, [v * v for v in parts], micro)
 
 
-def expand_kernel(micro, place, a0, a1, a2, a3, w0, w1, active, pre, sums, weight):
+def expand_kernel(micro, place, a0, a2, a3, a1, w0, w1, active, pre, sums, weight):
     fill(place, (a0, a1, a2, a3), active)
     half = WIDTH // 2
     for j, w in enumerate((w0, w1)):
@@ -442,7 +442,7 @@
 
 
 def conv_back_kernel(
-    micro, images, count, place, d0, d1, d2, d3, back0, back1, pre, sums, told, d_full, d_y, sums_out, weight
+    micro, images, count, place, d0, d2, d3, d1, back0, back1, pre, sums, told, d_full, d_y, sums_out, weight
 ):
     fill(place, (d0, d1, d2, d3), d_full)
     d_low = d_full[...]
@@ -1177,7 +1177,7 @@
         out[z] = jnp.where(first, two, one).astype(BF16)
 
 
-def image_pair_kernel(place, d0, d1, d2, d3, image, keep, out, d_full):
+def image_pair_kernel(place, d0, d2, d3, d1, image, keep, out, d_full):
     fill(place, (d0, d1, d2, d3), d_full)
     lanes = pl.ds(pl.multiple_of(place[0] * WIDE, WIDE), WIDE)
     pair_kernel(place, d_full, image.at[:, lanes], keep, out)
@@ -1207,6 +1207,10 @@
 
 def add_kernel(own, r1, r2, r3, out):
     out[...] = ((own[...] + r1[...].astype(F32)) + (r2[...].astype(F32) + r3[...].astype(F32))).astype(BF16)
+
+
+def ordered(pieces):
+    return [pieces[j] for j in (0, 2, 3, 1)]
 
 
 def after(value, *others):
@@ -1294,7 +1298,7 @@
     pre1, part = call(
         k(conv_kernel, micro, images),
         (pieces_of(PART, F32), sums_of),
-        place, *actives0, *w_conv,
+        place, *ordered(actives0), *w_conv,
         scratch=[pltpu.VMEM((rows, WIDTH), BF16), pltpu.VMEM((WIDTH, 9 * PART), BF16)],
         us=3,
     )
@@ -1324,7 +1328,7 @@
     active1, pre2, part, w_expand = call(
         k(expand_kernel, micro),
         (pieces_of(WIDTH, BF16), pieces_of(WIDE, F32), shape((8, WIDE), F32), shape((WIDTH, WIDE), BF16)),
-        place, *actives1, *pair_parts,
+        place, *ordered(actives1), *pair_parts,
         us=2,
     )
     back_own = lax.optimization_barrier((*back_own, part))[:4]
@@ -1497,7 +1501,7 @@
     d_pre1, d_y0, part = call(
         k(conv_back_kernel, micro, images, count),
         (pieces_of(WIDTH, BF16), pieces_of(PART, F32), sums_of),
-        place, *d_pre1s, *back_halves, pre0, sums0, pair_part,
+        place, *ordered(d_pre1s), *back_halves, pre0, sums0, pair_part,
         scratch=[pltpu.VMEM((9 * PART, WIDTH), BF16)],
         us=3.5,
     )
@@ -1520,7 +1524,7 @@
         keep, out, d_pre0 = call(
             image_pair_kernel,
             (shape((4, own, WIDE), F32), shape((4, own, WIDE), BF16), pieces_of(WIDTH, BF16)),
-            place, *d_pre0s, flat,
+            place, *ordered(d_pre0s), flat,
             us=2.5,
         )
         reduce_started = keep, flip(out, "dp", 1)

time: 223 us -> 223 us (level)
  no operation moved by 1% of the time
where the time goes in v5:
time: 223 us; the launch traced here: 221 us
  starting transfers between devices  88.7 us (40%)
  waiting for transfers between devices  70.1 us (31%)
  Pallas kernels  59 us (26%)
    ppermute x71, starting transfers between devices, flip(): lax.ppermute(value, axis, [(source, source ^ step) for source in range(co...  70 us
    ppermute x71, waiting for transfers between devices, flip(): lax.ppermute(value, axis, [(source, source ^ step) for source in range(co...  66.9 us
    pallas_call x41, Pallas kernels, call(): pl.pallas_call(kernel, name=getattr(kernel, 'func', kernel).__name__, out...  49.7 us
    ppermute x3, starting transfers between devices, body(): lax.ppermute(messages[j - 1], 'section', [(u, u ^ j) for u in range(3)])  9.48 us
    ppermute x3, starting transfers between devices, body(): lax.ppermute(mixed[j - 1], 'section', [(u ^ j, u) for u in range(3)])  9.21 us
  transfers between devices with their start and end apart: 77, of which 47 were waited for; matrix products, arithmetic and copies ran while one was open for 0% of the time, Pallas kernels for 19%

profile of v5, /device:TPU:2, one launch (start us, length us, event | category | flops | bytes accessed | tf_op | source)
XLA Modules:
  0.0 220.7 jit_solution(16077007925392182682)
XLA Ops:
  1.5 2.3 %pack.1 = (bf16[1168,128]{1,0:T(8,128)(2,1)S(1)}, bf16[1168,128]{1,0:T(8,128)(2,1)S(1)}, bf16[1168,128]{1,0:T(8,128)(2,1)S(1)}, bf16[1168,128]{1,0:T(8,128)(2,1)S(1)}) custom-call(s32[9]{0:T(128)S(1)} %stack.39.place, bf16[9456,512]{1,0:T(8,128)(2,1)} %bitcast.22, f32[3,1,2048]{2,1,0:T(1,128)S(1)} %bitcast.26), custom_call_target="tpu_custom_call" | custom-call | bytes 6000000 | tf_op jit(solution)/shard_map/pack/pallas_call | solution.py:1147
  3.9 2.2 collective-permute-start
  7.5 5.8 %collective-permute-start.2 = (bf16[1168,128]{1,0:T(8,128)(2,1)S(1)}, bf16[1168,128]{1,0:T(8,128)(2,1)S(1)}, u32[]{:S(2)}, u32[]{:S(2)}) collective-permute-start(bf16[1168,128]{1,0:T(8,128)(2,1)S(1)} %get-tuple-element.162), channel_id=1, source_target_pairs={{0,24},{8,16},{16,8},{1,25},{9,17},{17,9},{2,26},{10,18},{18,10},{... | collective-permute-start | bytes 897032 | tf_op jit(solution)/shard_map/ppermute | solution.py:1242
  16.8 3.6 %unpack.1.w_head = bf16[2048,2048]{1,0:T(8,128)(2,1)S(1)} custom-call(bf16[9456,512]{1,0:T(8,128)(2,1)S(1)} %bitcast.24), custom_call_target="tpu_custom_call" | custom-call | bytes 12000000 | tf_op jit(solution)/shard_map/unpack/pallas_call | solution.py:1074
  26.3 2.6 %collective-permute-start.9 = (f32[8,128]{1,0:T(8,128)S(1)}, f32[8,128]{1,0:T(8,128)S(1)}, u32[]{:S(2)}, u32[]{:S(2)}) collective-permute-start(f32[8,128]{1,0:T(8,128)S(1)} %add.82), channel_id=1, source_target_pairs={{0,4},{1,5},{2,6},{3,7},{4,0},{5,1},{6,2},{7,3},{8,12},{9,13},{10,... | collective-permute-start | bytes 12296 | tf_op jit(solution)/shard_map/ppermute | solution.py:55
  30.9 3.4 %collective-permute-done.8 = f32[8,128]{1,0:T(8,128)S(1)} collective-permute-done((f32[8,128]{1,0:T(8,128)S(1)}, f32[8,128]{1,0:T(8,128)S(1)}, u32[]{:S(2)}, u32[]{:S(2)}) %collective-permute-start.8) | collective-permute-done | bytes 4128 | tf_op jit(solution)/shard_map/ppermute | solution.py:55
  34.6 3.9 %collective-permute-start.12 = (bf16[784,128]{1,0:T(8,128)(2,1)S(1)}, bf16[784,128]{1,0:T(8,128)(2,1)S(1)}, u32[]{:S(2)}, u32[]{:S(2)}) collective-permute-start(bf16[784,128]{1,0:T(8,128)(2,1)S(1)} %active_kernel.2.active.a0), channel_id=1, source_target_pairs={{0,24},{8,16},{16,8},{24,0},{1,25},{9,17},{17,9},{25,1},{2,26},{10... | collective-permute-start | bytes 602120 | tf_op jit(solution)/shard_map/ppermute | solution.py:55
  45.3 3.1 %collective-permute-done.11.a2 = bf16[784,128]{1,0:T(8,128)(2,1)S(1)} collective-permute-done((bf16[784,128]{1,0:T(8,128)(2,1)S(1)}, bf16[784,128]{1,0:T(8,128)(2,1)S(1)}, u32[]{:S(2)}, u32[]{:S(2)}) %collective-permute-start.11) | collective-permute-done | bytes 200736 | tf_op jit(solution)/shard_map/ppermute | solution.py:55
  48.4 2.2 conv_kernel.1
  56.3 2.1 collective-permute-done.18
  62.1 3.1 %mass_kernel.1 = (bf16[512,3072]{1,0:T(8,128)(2,1)S(1)}, f32[8,3072]{1,0:T(8,128)S(1)}, bf16[2,32,32]{2,1,0:T(8,128)(2,1)S(1)}) custom-call(s32[9]{0:T(128)S(1)} %stack.39.place, bf16[768,512]{1,0:T(8,128)(2,1)S(1)} %get-tuple-element.190.table, bf16[320,128]{1,0:T(8,128)(2,1)S(1)} %rows_kernel.5.refs_0_, bf16[320,128]{1,0:T(8,128)(2,1)S(1)} %collective-permute-done.13.refs_1_), custom_call_target="tpu_custom_call" | custom-call | bytes 15000000 | tf_op jit(solution)/shard_map/mass_kernel/pallas_call | solution.py:139
  65.2 2.1 collective-permute-done.22.a3
  67.4 2.1 collective-permute-done.21.a2
  89.4 2.1 collective-permute-start.30
  98.3 10.9 %head_kernel.1 = (bf16[128,2048]{1,0:T(8,128)(2,1)S(1)}, bf16[128,2048]{1,0:T(8,128)(2,1)S(1)}, bf16[128,128]{1,0:T(8,128)(2,1)S(1)}, bf16[64,3072]{1,0:T(8,128)...) custom-call(s32[9]{0:T(128)S(1)} %stack.39.place, ...), custom_call_target="tpu_custom_call" | custom-call | bytes 36000000 | tf_op jit(solution)/shard_map/head_kernel/pallas_call | solution.py:139
  110.4 4.5 %head_back_kernel.1 = (bf16[16,512]{1,0:T(8,128)(2,1)S(1)}, bf16[16,512]{1,0:T(8,128)(2,1)S(1)}, bf16[16,512]{1,0:T(8,128)(2,1)S(1)}, bf16[16,512]{1,0:T(8,128)(...) custom-call(s32[9]{0:T(128)S(1)} %stack.39.place, ...), custom_call_target="tpu_custom_call" | custom-call | bytes 15000000 | tf_op jit(solution)/shard_map/head_back_kernel/pallas_call | solution.py:139
  126.1 2.0 collective-permute-start.43
  129.4 2.3 %collective-permute-done.43 = f32[8,512]{1,0:T(8,128)S(1)} collective-permute-done((f32[8,512]{1,0:T(8,128)S(1)}, f32[8,512]{1,0:T(8,128)S(1)}, u32[]{:S(2)}, u32[]{:S(2)}) %collective-permute-start.43) | collective-permute-done | bytes 16416 | tf_op jit(solution)/shard_map/ppermute | solution.py:55
  140.2 2.3 %collective-permute-done.46.q1 = bf16[784,128]{1,0:T(8,128)(2,1)S(1)} collective-permute-done((bf16[784,128]{1,0:T(8,128)(2,1)S(1)}, bf16[784,128]{1,0:T(8,128)(2,1)S(1)}, u32[]{:S(2)}, u32[]{:S(2)}) %collective-permute-start.46) | collective-permute-done | bytes 200736 | tf_op jit(solution)/shard_map/ppermute | solution.py:55
  142.5 4.9 %collective-permute-done.47.q2 = bf16[784,128]{1,0:T(8,128)(2,1)S(1)} collective-permute-done((bf16[784,128]{1,0:T(8,128)(2,1)S(1)}, bf16[784,128]{1,0:T(8,128)(2,1)S(1)}, u32[]{:S(2)}, u32[]{:S(2)}) %collective-permute-start.47) | collective-permute-done | bytes 200736 | tf_op jit(solution)/shard_map/ppermute | solution.py:55
  149.6 2.0 collective-permute-start.54
  159.9 2.1 head_grads_kernel.1.base
  164.0 2.1 collective-permute-done.57.d2
  166.1 2.4 %conv_back_kernel.1 = (bf16[784,512]{1,0:T(8,128)(2,1)S(1)}, f32[784,128]{1,0:T(8,128)S(1)}, f32[8,128]{1,0:T(8,128)S(1)}) custom-call(s32[9]{0:T(128)S(1)} %stack.39.place, bf16[784,128]{1,0:T(8,128)(2,1)S(1)} %norm_back_kernel.1.d0, bf16[784,128]{1,0:T(8,128)(2,1)S(1)} %collective-permute-done.57.d2, bf16[784,128]{1,0:T(8,128)(2,1)S(1)} %collective-permute-done.58.d3, ...), custom_call_target="tpu_custom_call" | custom-call | bytes 10500000 | tf_op jit(solution)/shard_map/conv_back_kernel/pallas_call | solution.py:139
  168.5 2.1 pair_kernel.3
  176.8 2.3 %collective-permute-start.68 = (bf16[2,64,1152]{2,1,0:T(8,128)(2,1)S(1)}, bf16[2,64,1152]{2,1,0:T(8,128)(2,1)S(1)}, u32[]{:S(2)}, u32[]{:S(2)}) collective-permute-start(bf16[2,64,1152]{2,1,0:T(8,128)(2,1)S(1)} %get-tuple-element.282), channel_id=1, source_target_pairs={{0,4},{1,5},{2,6},{3,7},{4,0},{5,1},{6,2},{7,3},{8,12},{9,13},{10,... | collective-permute-start | bytes 884744 | tf_op jit(solution)/shard_map/ppermute | solution.py:55
  183.7 5.6 %collective-permute-done.66.n3.d3 = bf16[832,128]{1,0:T(8,128)(2,1)S(1)} collective-permute-done((bf16[832,128]{1,0:T(8,128)(2,1)S(1)}, bf16[832,128]{1,0:T(8,128)(2,1)S(1)}, u32[]{:S(2)}, u32[]{:S(2)}) %collective-permute-start.66) | collective-permute-done | bytes 213024 | tf_op jit(solution)/shard_map/ppermute | solution.py:55
  189.3 2.2 %collective-permute-done.65.n2.d2 = bf16[832,128]{1,0:T(8,128)(2,1)S(1)} collective-permute-done((bf16[832,128]{1,0:T(8,128)(2,1)S(1)}, bf16[832,128]{1,0:T(8,128)(2,1)S(1)}, u32[]{:S(2)}, u32[]{:S(2)}) %collective-permute-start.65) | collective-permute-done | bytes 213024 | tf_op jit(solution)/shard_map/ppermute | solution.py:55
  201.8 2.5 %reduce_back_kernel.1 = f32[196,4,512]{2,1,0:T(4,128)} custom-call(s32[9]{0:T(128)S(1)} %stack.39.place, bf16[784,512]{1,0:T(8,128)(2,1)S(1)} %get-tuple-element.295.d_full, bf16[4,832,128]{2,1,0:T(8,128)(2,1)S(1)} %stack_kernel.1.back0, bf16[4,832,128]{2,1,0:T(8,128)(2,1)S(1)} %collective-permute-done.45.back1, f32[784,512]{1,0:T(8,128)S(1)} %get-tuple-element.225.d_z), custom_call_target="tpu_custom_call" | custom-call | bytes 6000000 | tf_op jit(solution)/shard_map/reduce_back_kernel/pallas_call | solution.py:139
  205.7 2.9 %collective-permute-start.74 = (bf16[64,1152]{1,0:T(8,128)(2,1)S(1)}, bf16[64,1152]{1,0:T(8,128)(2,1)S(1)}, u32[]{:S(2)}, u32[]{:S(2)}) collective-permute-start(bf16[64,1152]{1,0:T(8,128)(2,1)S(1)} %get-tuple-element.310), channel_id=1, source_target_pairs={{8,0},{0,8},{24,16},{9,1},{1,9},{25,17},{10,2},{2,10},{26,18},{11,... | collective-permute-start | bytes 442376 | tf_op jit(solution)/shard_map/ppermute | solution.py:1559
  210.0 5.0 %collective-permute-start.76 = (bf16[64,1152]{1,0:T(8,128)(2,1)S(1)}, bf16[64,1152]{1,0:T(8,128)(2,1)S(1)}, u32[]{:S(2)}, u32[]{:S(2)}) collective-permute-start(bf16[64,1152]{1,0:T(8,128)(2,1)S(1)} %get-tuple-element.312), channel_id=1, source_target_pairs={{24,0},{16,8},{8,16},{25,1},{17,9},{9,17},{26,2},{18,10},{10,18},{... | collective-permute-start | bytes 442376 | tf_op jit(solution)/shard_map/ppermute | solution.py:1559
  215.5 3.3 %collective-permute-done.75.m2 = bf16[64,1152]{1,0:T(8,128)(2,1)S(1)} collective-permute-done((bf16[64,1152]{1,0:T(8,128)(2,1)S(1)}, bf16[64,1152]{1,0:T(8,128)(2,1)S(1)}, u32[]{:S(2)}, u32[]{:S(2)}) %collective-permute-start.75) | collective-permute-done | bytes 147488 | tf_op jit(solution)/shard_map/ppermute | solution.py:1559
  (193 shorter events, 117.2 us)
Async XLA Ops:
  3.9 16.9 %collective-permute-start = (bf16[1168,128]{1,0:T(8,128)(2,1)S(1)}, bf16[1168,128]{1,0:T(8,128)(2,1)S(1)}, u32[]{:S(2)}, u32[]{:S(2)}) collective-permute-start(bf16[1168,128]{1,0:T(8,128)(2,1)S(1)} %get-tuple-element.160), channel_id=1, source_target_pairs={{0,8},{8,0},{16,24},{1,9},{9,1},{17,25},{2,10},{10,2},{18,26},{3,1... | collective-permute-start | bytes 897032 | tf_op jit(solution)/shard_map/ppermute | solution.py:1242
  6.0 14.7 %collective-permute-start.1 = (bf16[1168,128]{1,0:T(8,128)(2,1)S(1)}, bf16[1168,128]{1,0:T(8,128)(2,1)S(1)}, u32[]{:S(2)}, u32[]{:S(2)}) collective-permute-start(bf16[1168,128]{1,0:T(8,128)(2,1)S(1)} %get-tuple-element.161), channel_id=1, source_target_pairs={{0,16},{8,24},{16,0},{1,17},{9,25},{17,1},{2,18},{10,26},{18,2},{3... | collective-permute-start | bytes 897032 | tf_op jit(solution)/shard_map/ppermute | solution.py:1242
  7.5 13.2 %collective-permute-start.2 = (bf16[1168,128]{1,0:T(8,128)(2,1)S(1)}, bf16[1168,128]{1,0:T(8,128)(2,1)S(1)}, u32[]{:S(2)}, u32[]{:S(2)}) collective-permute-start(bf16[1168,128]{1,0:T(8,128)(2,1)S(1)} %get-tuple-element.162), channel_id=1, source_target_pairs={{0,24},{8,16},{16,8},{1,25},{9,17},{17,9},{2,26},{10,18},{18,10},{... | collective-permute-start | bytes 897032 | tf_op jit(solution)/shard_map/ppermute | solution.py:1242
  21.6 12.9 %collective-permute-start.14 = (bf16[1168,128]{1,0:T(8,128)(2,1)S(1)}, bf16[1168,128]{1,0:T(8,128)(2,1)S(1)}, u32[]{:S(2)}, u32[]{:S(2)}) collective-permute-start(bf16[1168,128]{1,0:T(8,128)(2,1)S(1)} %get-tuple-element.177.refs_0_), channel_id=1, source_target_pairs={{0,2},{1,3},{2,0},{3,1},{4,6},{5,7},{6,4},{7,5},{8,10},{9,11},{10,... | collective-permute-start | bytes 897032 | tf_op jit(solution)/shard_map/ppermute | solution.py:55
  34.5 8.2 %collective-permute-start.15 = (bf16[2336,128]{1,0:T(8,128)(2,1)S(1)}, bf16[2336,128]{1,0:T(8,128)(2,1)S(1)}, u32[]{:S(2)}, u32[]{:S(2)}) collective-permute-start(bf16[2336,128]{1,0:T(8,128)(2,1)S(1)} %rows_kernel.6.conv_a.wa.told), channel_id=1, source_target_pairs={{0,1},{1,0},{2,3},{3,2},{4,5},{5,4},{6,7},{7,6},{8,9},{9,8},{10,11... | collective-permute-start | bytes 1794056 | tf_op jit(solution)/shard_map/ppermute | solution.py:55
  34.6 10.7 %collective-permute-start.12 = (bf16[784,128]{1,0:T(8,128)(2,1)S(1)}, bf16[784,128]{1,0:T(8,128)(2,1)S(1)}, u32[]{:S(2)}, u32[]{:S(2)}) collective-permute-start(bf16[784,128]{1,0:T(8,128)(2,1)S(1)} %active_kernel.2.active.a0), channel_id=1, source_target_pairs={{0,24},{8,16},{16,8},{24,0},{1,25},{9,17},{17,9},{25,1},{2,26},{10... | collective-permute-start | bytes 602120 | tf_op jit(solution)/shard_map/ppermute | solution.py:55
  38.5 9.9 %collective-permute-start.11 = (bf16[784,128]{1,0:T(8,128)(2,1)S(1)}, bf16[784,128]{1,0:T(8,128)(2,1)S(1)}, u32[]{:S(2)}, u32[]{:S(2)}) collective-permute-start(bf16[784,128]{1,0:T(8,128)(2,1)S(1)} %active_kernel.2.active.a0), channel_id=1, source_target_pairs={{0,16},{8,24},{16,0},{24,8},{1,17},{9,25},{17,1},{25,9},{2,18},{10... | collective-permute-start | bytes 602120 | tf_op jit(solution)/shard_map/ppermute | solution.py:55
  38.5 9.9 %collective-permute-start.10 = (bf16[784,128]{1,0:T(8,128)(2,1)S(1)}, bf16[784,128]{1,0:T(8,128)(2,1)S(1)}, u32[]{:S(2)}, u32[]{:S(2)}) collective-permute-start(bf16[784,128]{1,0:T(8,128)(2,1)S(1)} %active_kernel.2.active.a0), channel_id=1, source_target_pairs={{0,8},{8,0},{16,24},{24,16},{1,9},{9,1},{17,25},{25,17},{2,10},{10... | collective-permute-start | bytes 602120 | tf_op jit(solution)/shard_map/ppermute | solution.py:55
  58.6 8.8 %collective-permute-start.22 = (bf16[784,128]{1,0:T(8,128)(2,1)S(1)}, bf16[784,128]{1,0:T(8,128)(2,1)S(1)}, u32[]{:S(2)}, u32[]{:S(2)}) collective-permute-start(bf16[784,128]{1,0:T(8,128)(2,1)S(1)} %active_kernel.3.a0), channel_id=1, source_target_pairs={{0,24},{8,16},{16,8},{24,0},{1,25},{9,17},{17,9},{25,1},{2,26},{10... | collective-permute-start | bytes 602120 | tf_op jit(solution)/shard_map/ppermute | solution.py:55
  60.4 9.1 %collective-permute-start.21 = (bf16[784,128]{1,0:T(8,128)(2,1)S(1)}, bf16[784,128]{1,0:T(8,128)(2,1)S(1)}, u32[]{:S(2)}, u32[]{:S(2)}) collective-permute-start(bf16[784,128]{1,0:T(8,128)(2,1)S(1)} %active_kernel.3.a0), channel_id=1, source_target_pairs={{0,16},{8,24},{16,0},{24,8},{1,17},{9,25},{17,1},{25,9},{2,18},{10... | collective-permute-start | bytes 602120 | tf_op jit(solution)/shard_map/ppermute | solution.py:55
  94.7 20.3 %collective-permute-start.35 = (bf16[832,128]{1,0:T(8,128)(2,1)S(1)}, bf16[832,128]{1,0:T(8,128)(2,1)S(1)}, u32[]{:S(2)}, u32[]{:S(2)}) collective-permute-start(bf16[832,128]{1,0:T(8,128)(2,1)S(1)} %get-tuple-element.218), channel_id=1, source_target_pairs={{0,8},{8,0},{16,24},{24,16},{1,9},{9,1},{17,25},{25,17},{2,10},{10... | collective-permute-start | bytes 638984 | tf_op jit(solution)/shard_map/ppermute | solution.py:55
  95.5 19.5 %collective-permute-start.36 = (bf16[832,128]{1,0:T(8,128)(2,1)S(1)}, bf16[832,128]{1,0:T(8,128)(2,1)S(1)}, u32[]{:S(2)}, u32[]{:S(2)}) collective-permute-start(bf16[832,128]{1,0:T(8,128)(2,1)S(1)} %get-tuple-element.219), channel_id=1, source_target_pairs={{0,16},{8,24},{16,0},{24,8},{1,17},{9,25},{17,1},{25,9},{2,18},{10... | collective-permute-start | bytes 638984 | tf_op jit(solution)/shard_map/ppermute | solution.py:55
  96.4 18.6 %collective-permute-start.37 = (bf16[832,128]{1,0:T(8,128)(2,1)S(1)}, bf16[832,128]{1,0:T(8,128)(2,1)S(1)}, u32[]{:S(2)}, u32[]{:S(2)}) collective-permute-start(bf16[832,128]{1,0:T(8,128)(2,1)S(1)} %get-tuple-element.220), channel_id=1, source_target_pairs={{0,24},{8,16},{16,8},{24,0},{1,25},{9,17},{17,9},{25,1},{2,26},{10... | collective-permute-start | bytes 638984 | tf_op jit(solution)/shard_map/ppermute | solution.py:55
  115.1 16.8 %collective-permute-start.45 = (bf16[4,832,128]{2,1,0:T(8,128)(2,1)S(1)}, bf16[4,832,128]{2,1,0:T(8,128)(2,1)S(1)}, u32[]{:S(2)}, u32[]{:S(2)}) collective-permute-start(bf16[4,832,128]{2,1,0:T(8,128)(2,1)S(1)} %stack_kernel.1.back0), channel_id=1, source_target_pairs={{0,1},{1,0},{2,3},{3,2},{4,5},{5,4},{6,7},{7,6},{8,9},{9,8},{10,11... | collective-permute-start | bytes 2555912 | tf_op jit(solution)/shard_map/ppermute | solution.py:55
  128.1 11.3 %collective-permute-start.49 = (bf16[64,3072]{1,0:T(8,128)(2,1)S(1)}, bf16[64,3072]{1,0:T(8,128)(2,1)S(1)}, u32[]{:S(2)}, u32[]{:S(2)}) collective-permute-start(bf16[64,3072]{1,0:T(8,128)(2,1)S(1)} %get-tuple-element.241.d_here), channel_id=1, source_target_pairs={{0,1},{1,0},{2,3},{3,2},{4,5},{5,4},{6,7},{7,6},{8,9},{9,8},{10,11... | collective-permute-start | bytes 1179656 | tf_op jit(solution)/shard_map/ppermute | solution.py:55
  134.7 7.9 %collective-permute-start.46 = (bf16[784,128]{1,0:T(8,128)(2,1)S(1)}, bf16[784,128]{1,0:T(8,128)(2,1)S(1)}, u32[]{:S(2)}, u32[]{:S(2)}) collective-permute-start(bf16[784,128]{1,0:T(8,128)(2,1)S(1)} %get-tuple-element.234), channel_id=1, source_target_pairs={{0,8},{8,0},{16,24},{24,16},{1,9},{9,1},{17,25},{25,17},{2,10},{10... | collective-permute-start | bytes 602120 | tf_op jit(solution)/shard_map/ppermute | solution.py:55
  136.1 11.4 %collective-permute-start.47 = (bf16[784,128]{1,0:T(8,128)(2,1)S(1)}, bf16[784,128]{1,0:T(8,128)(2,1)S(1)}, u32[]{:S(2)}, u32[]{:S(2)}) collective-permute-start(bf16[784,128]{1,0:T(8,128)(2,1)S(1)} %get-tuple-element.235), channel_id=1, source_target_pairs={{0,16},{8,24},{16,0},{24,8},{1,17},{9,25},{17,1},{25,9},{2,18},{10... | collective-permute-start | bytes 602120 | tf_op jit(solution)/shard_map/ppermute | solution.py:55
  137.2 10.3 %collective-permute-start.48 = (bf16[784,128]{1,0:T(8,128)(2,1)S(1)}, bf16[784,128]{1,0:T(8,128)(2,1)S(1)}, u32[]{:S(2)}, u32[]{:S(2)}) collective-permute-start(bf16[784,128]{1,0:T(8,128)(2,1)S(1)} %get-tuple-element.236), channel_id=1, source_target_pairs={{0,24},{8,16},{16,8},{24,0},{1,25},{9,17},{17,9},{25,1},{2,26},{10... | collective-permute-start | bytes 602120 | tf_op jit(solution)/shard_map/ppermute | solution.py:55
  138.8 8.6 %collective-permute-start.51 = (bf16[2,64,512]{2,1,0:T(8,128)(2,1)S(1)}, bf16[2,64,512]{2,1,0:T(8,128)(2,1)S(1)}, u32[]{:S(2)}, u32[]{:S(2)}) collective-permute-start(bf16[2,64,512]{2,1,0:T(8,128)(2,1)S(1)} %get-tuple-element.247), channel_id=1, source_target_pairs={{0,4},{1,5},{2,6},{3,7},{4,0},{5,1},{6,2},{7,3},{8,12},{9,13},{10,... | collective-permute-start | bytes 393224 | tf_op jit(solution)/shard_map/ppermute | solution.py:55
  155.3 8.7 %collective-permute-start.58 = (bf16[784,128]{1,0:T(8,128)(2,1)S(1)}, bf16[784,128]{1,0:T(8,128)(2,1)S(1)}, u32[]{:S(2)}, u32[]{:S(2)}) collective-permute-start(bf16[784,128]{1,0:T(8,128)(2,1)S(1)} %norm_back_kernel.1.d0), channel_id=1, source_target_pairs={{0,24},{8,16},{16,8},{24,0},{1,25},{9,17},{17,9},{25,1},{2,26},{10... | collective-permute-start | bytes 602120 | tf_op jit(solution)/shard_map/ppermute | solution.py:55
  156.6 9.5 %collective-permute-start.57 = (bf16[784,128]{1,0:T(8,128)(2,1)S(1)}, bf16[784,128]{1,0:T(8,128)(2,1)S(1)}, u32[]{:S(2)}, u32[]{:S(2)}) collective-permute-start(bf16[784,128]{1,0:T(8,128)(2,1)S(1)} %norm_back_kernel.1.d0), channel_id=1, source_target_pairs={{0,16},{8,24},{16,0},{24,8},{1,17},{9,25},{17,1},{25,9},{2,18},{10... | collective-permute-start | bytes 602120 | tf_op jit(solution)/shard_map/ppermute | solution.py:55
  157.6 8.5 %collective-permute-start.56 = (bf16[784,128]{1,0:T(8,128)(2,1)S(1)}, bf16[784,128]{1,0:T(8,128)(2,1)S(1)}, u32[]{:S(2)}, u32[]{:S(2)}) collective-permute-start(bf16[784,128]{1,0:T(8,128)(2,1)S(1)} %norm_back_kernel.1.d0), channel_id=1, source_target_pairs={{0,8},{8,0},{16,24},{24,16},{1,9},{9,1},{17,25},{25,17},{2,10},{10... | collective-permute-start | bytes 602120 | tf_op jit(solution)/shard_map/ppermute | solution.py:55
  176.8 15.5 %collective-permute-start.68 = (bf16[2,64,1152]{2,1,0:T(8,128)(2,1)S(1)}, bf16[2,64,1152]{2,1,0:T(8,128)(2,1)S(1)}, u32[]{:S(2)}, u32[]{:S(2)}) collective-permute-start(bf16[2,64,1152]{2,1,0:T(8,128)(2,1)S(1)} %get-tuple-element.282), channel_id=1, source_target_pairs={{0,4},{1,5},{2,6},{3,7},{4,0},{5,1},{6,2},{7,3},{8,12},{9,13},{10,... | collective-permute-start | bytes 884744 | tf_op jit(solution)/shard_map/ppermute | solution.py:55
  180.2 9.2 %collective-permute-start.66 = (bf16[832,128]{1,0:T(8,128)(2,1)S(1)}, bf16[832,128]{1,0:T(8,128)(2,1)S(1)}, u32[]{:S(2)}, u32[]{:S(2)}) collective-permute-start(bf16[832,128]{1,0:T(8,128)(2,1)S(1)} %last_norm_back_kernel.1.n0.d0), channel_id=1, source_target_pairs={{0,24},{8,16},{16,8},{24,0},{1,25},{9,17},{17,9},{25,1},{2,26},{10... | collective-permute-start | bytes 638984 | tf_op jit(solution)/shard_map/ppermute | solution.py:55
  181.8 9.7 %collective-permute-start.65 = (bf16[832,128]{1,0:T(8,128)(2,1)S(1)}, bf16[832,128]{1,0:T(8,128)(2,1)S(1)}, u32[]{:S(2)}, u32[]{:S(2)}) collective-permute-start(bf16[832,128]{1,0:T(8,128)(2,1)S(1)} %last_norm_back_kernel.1.n0.d0), channel_id=1, source_target_pairs={{0,16},{8,24},{16,0},{24,8},{1,17},{9,25},{17,1},{25,9},{2,18},{10... | collective-permute-start | bytes 638984 | tf_op jit(solution)/shard_map/ppermute | solution.py:55
  182.8 8.8 %collective-permute-start.64 = (bf16[832,128]{1,0:T(8,128)(2,1)S(1)}, bf16[832,128]{1,0:T(8,128)(2,1)S(1)}, u32[]{:S(2)}, u32[]{:S(2)}) collective-permute-start(bf16[832,128]{1,0:T(8,128)(2,1)S(1)} %last_norm_back_kernel.1.n0.d0), channel_id=1, source_target_pairs={{0,8},{8,0},{16,24},{24,16},{1,9},{9,1},{17,25},{25,17},{2,10},{10... | collective-permute-start | bytes 638984 | tf_op jit(solution)/shard_map/ppermute | solution.py:55
  194.0 10.3 %collective-permute-start.73 = (bf16[64,1152]{1,0:T(8,128)(2,1)S(1)}, bf16[64,1152]{1,0:T(8,128)(2,1)S(1)}, u32[]{:S(2)}, u32[]{:S(2)}) collective-permute-start(bf16[64,1152]{1,0:T(8,128)(2,1)S(1)} %get-tuple-element.298), channel_id=1, source_target_pairs={{0,2},{1,3},{2,0},{3,1},{4,6},{5,7},{6,4},{7,5},{8,10},{9,11},{10,... | collective-permute-start | bytes 442376 | tf_op jit(solution)/shard_map/ppermute | solution.py:55
  196.1 8.2 %collective-permute-start.70 = (bf16[64,512]{1,0:T(8,128)(2,1)S(1)}, bf16[64,512]{1,0:T(8,128)(2,1)S(1)}, u32[]{:S(2)}, u32[]{:S(2)}) collective-permute-start(bf16[64,512]{1,0:T(8,128)(2,1)S(1)} %get-tuple-element.292), channel_id=1, source_target_pairs={{0,2},{1,3},{2,0},{3,1},{4,6},{5,7},{6,4},{7,5},{8,10},{9,11},{10,... | collective-permute-start | bytes 196616 | tf_op jit(solution)/shard_map/ppermute | solution.py:55
  196.7 8.4 %collective-permute-start.71 = (bf16[64,512]{1,0:T(8,128)(2,1)S(1)}, bf16[64,512]{1,0:T(8,128)(2,1)S(1)}, u32[]{:S(2)}, u32[]{:S(2)}) collective-permute-start(bf16[64,512]{1,0:T(8,128)(2,1)S(1)} %get-tuple-element.293), channel_id=1, source_target_pairs={{0,4},{1,5},{2,6},{3,7},{4,0},{5,1},{6,2},{7,3},{8,12},{9,13},{10,... | collective-permute-start | bytes 196616 | tf_op jit(solution)/shard_map/ppermute | solution.py:55
  205.7 9.8 %collective-permute-start.74 = (bf16[64,1152]{1,0:T(8,128)(2,1)S(1)}, bf16[64,1152]{1,0:T(8,128)(2,1)S(1)}, u32[]{:S(2)}, u32[]{:S(2)}) collective-permute-start(bf16[64,1152]{1,0:T(8,128)(2,1)S(1)} %get-tuple-element.310), channel_id=1, source_target_pairs={{8,0},{0,8},{24,16},{9,1},{1,9},{25,17},{10,2},{2,10},{26,18},{11,... | collective-permute-start | bytes 442376 | tf_op jit(solution)/shard_map/ppermute | solution.py:1559
  208.7 10.1 %collective-permute-start.75 = (bf16[64,1152]{1,0:T(8,128)(2,1)S(1)}, bf16[64,1152]{1,0:T(8,128)(2,1)S(1)}, u32[]{:S(2)}, u32[]{:S(2)}) collective-permute-start(bf16[64,1152]{1,0:T(8,128)(2,1)S(1)} %get-tuple-element.311), channel_id=1, source_target_pairs={{16,0},{24,8},{0,16},{17,1},{25,9},{1,17},{18,2},{26,10},{2,18},{1... | collective-permute-start | bytes 442376 | tf_op jit(solution)/shard_map/ppermute | solution.py:1559
  210.0 8.8 %collective-permute-start.76 = (bf16[64,1152]{1,0:T(8,128)(2,1)S(1)}, bf16[64,1152]{1,0:T(8,128)(2,1)S(1)}, u32[]{:S(2)}, u32[]{:S(2)}) collective-permute-start(bf16[64,1152]{1,0:T(8,128)(2,1)S(1)} %get-tuple-element.312), channel_id=1, source_target_pairs={{24,0},{16,8},{8,16},{25,1},{17,9},{9,17},{26,2},{18,10},{10,18},{... | collective-permute-start | bytes 442376 | tf_op jit(solution)/shard_map/ppermute | solution.py:1559
  (51 other events, 249.8 us)
